TPU v7x, 256 devices: a whole 4x4x8 slice. The times are simulated.
256 devices in a mesh: gx: 4 (over y), gy: 8 (over z), gz: 8 (over x, core).
Axes of the slice: x: 4, y: 4, z: 8, core: 2. Of those that a mesh axis runs over, the one named last changes fastest.
Arguments:
- residual_start: float32 [16, 65536], P(None, ('gx', 'gy', 'gz')), may hold values from -1 to 1
- near_tiles: bfloat16 [32768, 128, 128], P(('gx', 'gy', 'gz')), may hold values from -1 to 1
- near_target: int32 [32768], P(('gx', 'gy', 'gz')), may hold values from 0 to 511, as said below
- near_source: int32 [32768], P(('gx', 'gy', 'gz')), may hold values from 0 to 511, as said below
- near_count: int32 [256], P(('gx', 'gy', 'gz')), may hold values from 42 to 128, as said below
- far_left: bfloat16 [49152, 128, 64], P(('gx', 'gy', 'gz')), may hold values from -0.5 to 0.5
- far_right: bfloat16 [49152, 128, 64], P(('gx', 'gy', 'gz')), may hold values from -0.078125 to 0.078125
- far_target: int32 [49152], P(('gx', 'gy', 'gz')), may hold values from 0 to 511, as said below
- far_source: int32 [49152], P(('gx', 'gy', 'gz')), may hold values from 0 to 511, as said below
- far_count: int32 [256], P(('gx', 'gy', 'gz')), may hold values from 64 to 192, as said below
Outputs:
- next_basis: float32 [16, 65536], P(None, ('gx', 'gy', 'gz'))
- arnoldi: float32 [16, 6], replicated
Inputs may be any that keep to these rules, and one draw needn't show every extreme that they name: `near_target`: A slot on the device with gx index a and gy index c has a target cluster t with (t // 2) // 8 % 8 == c and a source cluster s with (s // 2) // 64 == a. `near_source`: as for near_target. `far_target`: as for near_target. `far_source`: as for near_target. `near_count`: some device is full and some device holds the fewest. `far_count`: some device is full and some device holds the fewest.
All inputs are finite; a program needn't handle non-finite values.
Results may differ from a plain program's by a relative error of at most 0.0039.
Values may be sent and summed in bfloat16 or wider, within the bound.
No kernel may reach another device: no remote copies, remote signals or barrier semaphores. Data moves between devices by JAX's collectives and lax.ppermute only.
A program may use at most 64 MiB of HBM per device.

v0:
```python
import jax
import jax.numpy as jnp
from jax import lax
from jax.sharding import PartitionSpec as P

OBJ = 16
LEAF = 128
CL_DEV = 2
NEAR_DEV = 128
FAR_DEV = 192


EPS = 1e-06


def target_position(cluster, count_gy, count_gz):
    group = cluster // CL_DEV
    within = cluster % CL_DEV
    return (group // (count_gy * count_gz) * count_gz + group % count_gz) * CL_DEV + within


def source_position(cluster, count_gy, count_gz):
    group = cluster // CL_DEV
    within = cluster % CL_DEV
    return (group // count_gz % count_gy * count_gz + group % count_gz) * CL_DEV + within


def apply_transposed(
    vector,
    near_tiles,
    near_rows,
    near_cols,
    near_alive,
    far_left,
    far_right,
    far_rows,
    far_cols,
    far_alive,
    source_total,
):
    rounded = vector.astype(jnp.bfloat16)
    gathered = lax.all_gather(rounded, ("gx", "gz"), axis=1, tiled=True)
    grouped = gathered.reshape(OBJ, -1, LEAF)
    picked = jnp.take(grouped, near_rows, axis=1)
    contrib = (
        jnp.einsum("obl,bls->obs", picked, near_tiles, preferred_element_type=jnp.float32)
        * near_alive[None, :, None]
    )
    partial_value = jnp.zeros((OBJ, source_total, LEAF), jnp.float32).at[:, near_cols].add(contrib)
    picked_far = jnp.take(grouped, far_rows, axis=1)
    reduced = jnp.einsum(
        "obl,blr->obr", picked_far, far_left, preferred_element_type=jnp.float32
    ).astype(jnp.bfloat16)
    contrib_far = (
        jnp.einsum("obr,bsr->obs", reduced, far_right, preferred_element_type=jnp.float32)
        * far_alive[None, :, None]
    )
    partial_value = partial_value.at[:, far_cols].add(contrib_far)
    flat = partial_value.reshape(OBJ, -1)
    summed = lax.psum_scatter(flat, ("gy", "gz"), scatter_dimension=1, tiled=True)
    return 0.5 * vector + summed


def local_inner(first, second):
    return jnp.sum(first * second, axis=1)


def on_device(
    residual_start,
    near_tiles,
    near_target,
    near_source,
    near_count,
    far_left,
    far_right,
    far_target,
    far_source,
    far_count,
):
    count_gy = lax.axis_size("gy")
    count_gz = lax.axis_size("gz")
    source_total = CL_DEV * count_gy * count_gz
    near_rows = target_position(near_target, count_gy, count_gz)
    near_cols = source_position(near_source, count_gy, count_gz)
    far_rows = target_position(far_target, count_gy, count_gz)
    far_cols = source_position(far_source, count_gy, count_gz)
    near_alive = (jnp.arange(NEAR_DEV, dtype=jnp.int32) < near_count[0]).astype(jnp.float32)
    far_alive = (jnp.arange(FAR_DEV, dtype=jnp.int32) < far_count[0]).astype(jnp.float32)
    beta = jnp.sqrt(lax.psum(local_inner(residual_start, residual_start), ("gx", "gy", "gz")) + EPS)
    basis_list = [residual_start / beta[:, None]]
    entries = [beta]
    for turn_index in range(2):
        image = apply_transposed(
            basis_list[-1],
            near_tiles,
            near_rows,
            near_cols,
            near_alive,
            far_left,
            far_right,
            far_rows,
            far_cols,
            far_alive,
            source_total,
        )
        local_dots = jnp.stack([local_inner(member, image) for member in basis_list])
        dots = lax.psum(local_dots, ("gx", "gy", "gz"))
        remainder = image
        for position, member in enumerate(basis_list):
            remainder = remainder - dots[position][:, None] * member
        total_sq = lax.psum(local_inner(remainder, remainder), ("gx", "gy", "gz"))
        length_row = jnp.sqrt(total_sq + EPS)
        basis_list.append(remainder / length_row[:, None])
        entries = (
            entries + [dots[position] for position in range(len(basis_list) - 1)] + [length_row]
        )
    return (basis_list[-1], jnp.stack(entries, axis=1))


def solution(mesh):
    placed = (
        P(None, ("gx", "gy", "gz")),
        P(("gx", "gy", "gz"), None, None),
        P(("gx", "gy", "gz")),
        P(("gx", "gy", "gz")),
        P(("gx", "gy", "gz")),
        P(("gx", "gy", "gz"), None, None),
        P(("gx", "gy", "gz"), None, None),
        P(("gx", "gy", "gz")),
        P(("gx", "gy", "gz")),
        P(("gx", "gy", "gz")),
    )
    return jax.shard_map(
        on_device,
        mesh=mesh,
        in_specs=placed,
        out_specs=(P(None, ("gx", "gy", "gz")), P()),
        check_vma=False,
    )
```

profile of v0, /device:TPU:1, one launch (start us, length us, event | category | flops | bytes accessed | tf_op | source)
XLA Modules:
  0.0 835.8 jit_solution(4533954224313394627)
XLA Ops:
  7.2 1.0 multiply_reduce_fusion.5
  8.9 81.4 %psum.35 = f32[16]{0:T(128)S(1)} all-reduce(f32[16]{0:T(128)S(1)} %multiply_reduce_fusion.5), channel_id=1, replica_groups=mesh['gx'=4,'gy'=8,'gz'=8] {'gx','gy','gz'}, use_global_device_ids=true, to_apply=%region_1.2 | all-reduce | flops 16 | bytes 128 | tf_op jit(solution)/shard_map/psum | solution.py:89
  90.3 0.8 fusion.47
  91.1 22.9 %all_gather.6 = bf16[16,8192]{1,0:T(8,128)(2,1)S(1)} all-gather(bf16[16,256]{1,0:T(8,128)(2,1)S(1)} %fusion.47), channel_id=1, replica_groups=mesh['gx'=4,'gy'=8,'gz'=8] {'gx','gz'}, dimensions={1}, use_global_device_ids=true | all-gather | bytes 270336 | tf_op jit(solution)/shard_map/all_gather | solution.py:42
  116.9 1.5 gather_fusion
  118.4 1.6 gather_fusion.1
  120.7 4.6 convolution_multiply_fusion.3
  125.3 1.0 broadcast.120.clone
  126.3 16.1 %scatter_fusion = f32[16,128,128]{2,0,1:T(8,128)} fusion(f32[16,128,128]{2,0,1:T(8,128)} %broadcast.120.clone, s32[128]{0:T(128)S(1)} %compare_select_fusion.3, f32[128,16,128]{2,1,0:T(8,128)} %convolution_multiply_fusion.3), kind=kCustom, calls=%fused_computation.4 | custom fusion | flops 262144 | bytes 3146240 | tf_op jit(solution)/shard_map/scatter-add | solution.py:49
  142.5 5.9 convolution_multiply_fusion.1
  148.4 23.9 %scatter_fusion.1 = f32[16,128,128]{2,0,1:T(8,128)} fusion(f32[16,128,128]{2,0,1:T(8,128)} %scatter_fusion, s32[192]{0:T(256)S(1)} %compare_select_fusion.1, f32[192,16,128]{2,1,0:T(8,128)} %convolution_multiply_fusion.1), kind=kCustom, calls=%fused_computation.5 | custom fusion | flops 393216 | bytes 4719360 | tf_op jit(solution)/shard_map/scatter-add | solution.py:58
  172.3 2.3 copy_bitcast_fusion.1
  174.7 130.2 %reduce-scatter.3.cloned.1.call-done = f32[16,256]{1,0:T(8,128)} async-done(((f32[16,16384]{1,0:T(8,128)}), f32[16,256]{1,0:T(8,128)}) %reduce-scatter.3.cloned.1.call-update) | async-done | bytes 16400 | tf_op jit(solution)/shard_map/reduce_scatter | solution.py:60
  304.9 0.9 multiply_reduce_fusion.4
  305.8 79.9 %psum.36 = f32[1,16]{1,0:T(1,128)S(1)} all-reduce(f32[1,16]{1,0:T(1,128)S(1)} %bitcast.76), channel_id=1, replica_groups=mesh['gx'=4,'gy'=8,'gz'=8] {'gx','gy','gz'}, use_global_device_ids=true, to_apply=%region_6.9 | all-reduce | flops 16 | bytes 128 | tf_op jit(solution)/shard_map/psum | solution.py:107
  385.7 0.9 multiply_reduce_fusion.3
  386.6 73.4 %psum.37 = f32[16]{0:T(128)S(1)} all-reduce(f32[16]{0:T(128)S(1)} %multiply_reduce_fusion.3), channel_id=1, replica_groups=mesh['gx'=4,'gy'=8,'gz'=8] {'gx','gy','gz'}, use_global_device_ids=true, to_apply=%region_8.11 | all-reduce | flops 16 | bytes 128 | tf_op jit(solution)/shard_map/psum | solution.py:111
  460.0 0.8 fusion.48
  460.8 24.2 %all_gather.7 = bf16[16,8192]{1,0:T(8,128)(2,1)S(1)} all-gather(bf16[16,256]{1,0:T(8,128)(2,1)S(1)} %get-tuple-element.8), channel_id=1, replica_groups=mesh['gx'=4,'gy'=8,'gz'=8] {'gx','gz'}, dimensions={1}, use_global_device_ids=true | all-gather | bytes 270336 | tf_op jit(solution)/shard_map/all_gather | solution.py:42
  485.1 1.5 gather_fusion.2
  486.5 1.6 gather_fusion.3
  488.2 4.6 convolution_multiply_fusion.2
  492.8 5.9 convolution_multiply_fusion
  498.7 1.1 broadcast.120
  499.8 16.1 %scatter_fusion.2 = f32[16,128,128]{2,0,1:T(8,128)} fusion(f32[16,128,128]{2,0,1:T(8,128)} %broadcast.120, s32[128]{0:T(128)S(1)} %compare_select_fusion.3, f32[128,16,128]{2,1,0:T(8,128)} %convolution_multiply_fusion.2), kind=kCustom, calls=%fused_computation.6 | custom fusion | flops 262144 | bytes 3146240 | tf_op jit(solution)/shard_map/scatter-add | solution.py:49
  515.9 23.9 %scatter_fusion.3 = f32[16,128,128]{2,0,1:T(8,128)} fusion(f32[16,128,128]{2,0,1:T(8,128)} %scatter_fusion.2, s32[192]{0:T(256)S(1)} %compare_select_fusion.1, f32[192,16,128]{2,1,0:T(8,128)} %convolution_multiply_fusion), kind=kCustom, calls=%fused_computation.7 | custom fusion | flops 393216 | bytes 4719360 | tf_op jit(solution)/shard_map/scatter-add | solution.py:58
  539.8 2.3 copy_bitcast_fusion
  542.1 130.8 %reduce-scatter.5.cloned.1.call-done = f32[16,256]{1,0:T(8,128)} async-done(((f32[16,16384]{1,0:T(8,128)}), f32[16,256]{1,0:T(8,128)}) %reduce-scatter.5.cloned.1.call-update) | async-done | bytes 16400 | tf_op jit(solution)/shard_map/reduce_scatter | solution.py:60
  672.9 0.9 multiply_reduce_fusion.2
  673.8 79.5 %psum.38 = f32[2,16]{1,0:T(2,128)S(1)} all-reduce(f32[2,16]{1,0:T(2,128)S(1)} %pad_maximum_fusion), channel_id=1, replica_groups=mesh['gx'=4,'gy'=8,'gz'=8] {'gx','gy','gz'}, use_global_device_ids=true, to_apply=%region_14.17 | all-reduce | flops 32 | bytes 256 | tf_op jit(solution)/shard_map/psum | solution.py:107
  753.3 0.9 multiply_reduce_fusion
  754.2 73.5 %psum.39 = f32[16]{0:T(128)S(1)} all-reduce(f32[16]{0:T(128)S(1)} %get-tuple-element.6), channel_id=1, replica_groups=mesh['gx'=4,'gy'=8,'gz'=8] {'gx','gy','gz'}, use_global_device_ids=true, to_apply=%region_16.19 | all-reduce | flops 16 | bytes 128 | tf_op jit(solution)/shard_map/psum | solution.py:111
  (25 shorter events, 4.4 us)
Async XLA Ops:
  7.2 135.3 %copy-start = (bf16[192,128,64]{1,2,0:T(8,128)(2,1)S(1)}, bf16[192,128,64]{1,2,0:T(8,128)(2,1)}, u32[]{:S(2)}) copy-start(bf16[192,128,64]{1,2,0:T(8,128)(2,1)} %param.20) | copy-start | bytes 9437188
  7.2 297.7 %reduce-scatter.3.cloned.1.call-start = ((), (), s32[]{:S(2)}) async-start(), calls=%async_computation.2 | async-start | bytes 1064960 | tf_op jit(solution)/shard_map/reduce_scatter | solution.py:60
  148.4 156.5 %copy-start.1 = (f32[16,256]{1,0:T(8,128)S(1)}, f32[16,256]{1,0:T(8,128)}, u32[]{:S(2)}) copy-start(f32[16,256]{1,0:T(8,128)} %param.14) | copy-start | bytes 49156
  174.6 498.3 %reduce-scatter.5.cloned.1.call-start = ((), (), s32[]{:S(2)}) async-start(), calls=%async_computation.3 | async-start | bytes 1064960 | tf_op jit(solution)/shard_map/reduce_scatter | solution.py:60
Sparse Core Ops, SparseCore 0:
  174.8 130.1 reduce-scatter.2
  542.2 130.6 reduce-scatter.4
where the time goes:
time: 838 us; the launch traced here: 836 us
  blocking collectives  435 us (52%)
  waiting for transfers between devices  261 us (31%)
  other arithmetic  89.8 us (11%)
  matrix products  21 us (3%)
  between operations  15.4 us (2%)
  local copies, waits for them, and re-layouts  13.6 us (2%)
    reduce_scatter x2, waiting for transfers between devices, apply_transposed(): lax.psum_scatter(flat, ('gy', 'gz'), scatter_dimension=1, tiled=True)  261 us
    psum x2, blocking collectives, on_device(): dots = lax.psum(local_dots, ('gx', 'gy', 'gz'))  159 us
    psum x2, blocking collectives, on_device(): total_sq = lax.psum(local_inner(remainder, remainder), ('gx', 'gy', 'gz'))  147 us
    psum x1, blocking collectives, on_device(): lax.psum(local_inner(residual_start, residual_start), ('gx', 'gy', 'gz'))  81.4 us
    scatter-add x2, other arithmetic, apply_transposed(): partial_value = partial_value.at[:, far_cols].add(contrib_far)  47.9 us
    all_gather x2, blocking collectives, apply_transposed(): gathered = lax.all_gather(rounded, ('gx', 'gz'), axis=1, tiled=True)  47.1 us
    scatter-add x2, other arithmetic, apply_transposed(): jnp.zeros((OBJ, source_total, LEAF), jnp.float32).at[:, near_cols]  32.3 us
  transfers between devices with their start and end apart: 2, of which 2 were waited for; matrix products, arithmetic and copies ran while one was open for 0% of the time, Pallas kernels for 0%

commit v1 on v0

v1 whole, which is shorter than its diff:
```python
import functools

import jax
import jax.numpy as jnp
from jax import lax
from jax.experimental import pallas as pl
from jax.experimental.pallas import tpu as pltpu
from jax.sharding import PartitionSpec as P

OBJ = 16
LEAF = 128
RANK = 64
CL_DEV = 2
NEAR_DEV = 128
FAR_DEV = 192
EPS = 1e-06

ALL = ("gx", "gy", "gz")
TARGETS = 64
SOURCES = 128
NEAR_CHUNK = 32
FAR_CHUNK = 48
UNROLL = 8

SMEM = pl.BlockSpec(memory_space=pltpu.SMEM)
VMEM = pl.BlockSpec(memory_space=pltpu.VMEM)
ANY = pl.BlockSpec(memory_space=pl.ANY)


def target_row(cluster):
    return (cluster >> 7) * 16 + (cluster & 15)


def source_row(cluster):
    return cluster & (SOURCES - 1)


def start_blocks(near, left, right, near_v, left_v, right_v, sems):
    copies = []
    for i in range(NEAR_DEV // NEAR_CHUNK):
        part = pl.ds(i * NEAR_CHUNK, NEAR_CHUNK)
        copies.append(pltpu.make_async_copy(near.at[part], near_v.at[part], sems.at[len(copies)]))
    for i in range(FAR_DEV // FAR_CHUNK):
        part = pl.ds(i * FAR_CHUNK, FAR_CHUNK)
        copies.append(pltpu.make_async_copy(left.at[part], left_v.at[part], sems.at[len(copies)]))
        copies.append(pltpu.make_async_copy(right.at[part], right_v.at[part], sems.at[len(copies)]))
    for copy in copies:
        copy.start()
    return copies


def multiply(copies, x, near_v, left_v, right_v, nt, ns, nc, ft, fs, fc, out):
    near_live = nc[0]
    far_live = fc[0]
    out[...] = jnp.zeros_like(out)

    def near_slot(slot):
        row = jnp.where(slot < near_live, target_row(nt[slot]), TARGETS)
        source = source_row(ns[slot])
        part = jnp.dot(x[row], near_v[slot], preferred_element_type=jnp.float32)
        return source, part

    def far_slot(slot):
        row = jnp.where(slot < far_live, target_row(ft[slot]), TARGETS)
        source = source_row(fs[slot])
        reduced = lax.dot_general(
            x[row], left_v[slot], (((1,), (1,)), ((), ())), preferred_element_type=jnp.float32
        ).astype(jnp.bfloat16)
        part = jnp.dot(reduced, right_v[slot], preferred_element_type=jnp.float32)
        return source, part

    def run(one_slot, first, live, chunk):
        groups = (jnp.clip(live - first, 0, chunk) + UNROLL - 1) // UNROLL

        def body(group, carry):
            parts = [one_slot(first + group * UNROLL + i) for i in range(UNROLL)]
            for source, part in parts:
                out[source] += part
            return carry

        lax.fori_loop(0, groups, body, 0)

    done = 0
    for i in range(NEAR_DEV // NEAR_CHUNK):
        copies[done].wait()
        done += 1
        run(near_slot, i * NEAR_CHUNK, near_live, NEAR_CHUNK)
    for i in range(FAR_DEV // FAR_CHUNK):
        copies[done].wait()
        copies[done + 1].wait()
        done += 2
        run(far_slot, i * FAR_CHUNK, far_live, FAR_CHUNK)


def first_kernel(nt, ns, nc, ft, fs, fc, beta, r, near, left, right, out, x, near_v, left_v, right_v, sems):
    copies = start_blocks(near, left, right, near_v, left_v, right_v, sems)
    x[TARGETS] = jnp.zeros((OBJ, LEAF), jnp.bfloat16)
    x[:TARGETS] = (r[...] / beta[...][None]).astype(jnp.bfloat16)
    multiply(copies, x, near_v, left_v, right_v, nt, ns, nc, ft, fs, fc, out)


def second_kernel(nt, ns, nc, ft, fs, fc, beta, h11, h21, r, image, near, left, right, out, x, near_v, left_v, right_v, sems):
    copies = start_blocks(near, left, right, near_v, left_v, right_v, sems)
    x[TARGETS] = jnp.zeros((OBJ, LEAF), jnp.bfloat16)
    basis_1 = r[...] / beta[...][None]
    basis_2 = (image[...] - h11[...][None] * basis_1) / h21[...][None]
    x[:TARGETS] = basis_2.astype(jnp.bfloat16)
    multiply(copies, x, near_v, left_v, right_v, nt, ns, nc, ft, fs, fc, out)


def product(kernel, indices, columns, fields, blocks):
    return pl.pallas_call(
        kernel,
        out_shape=jax.ShapeDtypeStruct((SOURCES, OBJ, LEAF), jnp.float32),
        in_specs=[SMEM] * 6 + [VMEM] * (len(columns) + len(fields)) + [ANY] * 3,
        out_specs=VMEM,
        scratch_shapes=[
            pltpu.VMEM((TARGETS + 1, OBJ, LEAF), jnp.bfloat16),
            pltpu.VMEM((NEAR_DEV, LEAF, LEAF), jnp.bfloat16),
            pltpu.VMEM((FAR_DEV, RANK, LEAF), jnp.bfloat16),
            pltpu.VMEM((FAR_DEV, RANK, LEAF), jnp.bfloat16),
            pltpu.SemaphoreType.DMA((NEAR_DEV // NEAR_CHUNK + 2 * (FAR_DEV // FAR_CHUNK),)),
        ],
        compiler_params=pltpu.CompilerParams(vmem_limit_bytes=56 * 1024 * 1024),
        cost_estimate=pl.CostEstimate(flops=170_000_000, bytes_accessed=12_000_000, transcendentals=0),
    )(*indices, *columns, *fields, *blocks)


def dot(first, second):
    return jnp.sum(first * second, axis=(0, 2))


def sum_gathered(value):
    for axes in (("gx", "gz"), "gy"):
        value = lax.all_gather(value, axes, axis=0, tiled=True).reshape((-1,) + value.shape).sum(0)
    return value.sum(1)


def exchange(value, axis):
    size = lax.axis_size(axis)
    total = value
    for step in range(1, size):
        total = total + lax.ppermute(value, axis, [(i, (i + step) % size) for i in range(size)])
    return total


def sum_exchanged(value):
    for axis in ("gz", "gx", "gy"):
        value = exchange(value, axis)
    return value


def sum_all_to_all(value):
    for axes in (("gx", "gz"), ("gy",)):
        size = lax.axis_size(axes)
        copies = jnp.broadcast_to(value[None], (size,) + value.shape)
        value = lax.all_to_all(copies, axes, split_axis=0, concat_axis=0).sum(0)
    return value


def scatter_sum(part, axes):
    size = lax.axis_size(axes)
    pieces = part.reshape((size, -1) + part.shape[1:])
    return lax.all_to_all(pieces, axes, split_axis=0, concat_axis=0).sum(0)


def scatter_sum_once(part):
    return scatter_sum(part, ("gy", "gz"))


def scatter_sum_twice(part):
    by_gz = jnp.swapaxes(part.reshape(8, 8, CL_DEV, OBJ, LEAF), 0, 1)
    half = scatter_sum(by_gz.reshape(8 * 8, CL_DEV, OBJ, LEAF), ("gz",))
    return scatter_sum(half, ("gy",))[0]


def guarded_square(square, whole, remainder):
    low = jnp.any(square < whole * (1.0 / 256.0))
    return lax.cond(low, lambda: lax.psum(dot(remainder, remainder), ALL), lambda: square)


def on_device(r0, near_tiles, nt, ns, nc, far_left, far_right, ft, fs, fc):
    indices = (nt, ns, nc, ft, fs, fc)
    blocks = (near_tiles, jnp.swapaxes(far_left, 1, 2), jnp.swapaxes(far_right, 1, 2))
    r = jnp.swapaxes(r0.reshape(OBJ, CL_DEV, LEAF), 0, 1)

    def spread(column):
        return jnp.broadcast_to(column[:, None], (OBJ, LEAF))

    r_targets = lax.all_gather(r, ("gx", "gz"), axis=0, tiled=True)
    square_r = sum_gathered((r * r).sum(0))
    beta = jnp.sqrt(square_r + EPS)
    basis_1 = r / beta[None, :, None]
    g11 = square_r / (square_r + EPS)

    part = product(first_kernel, indices, (spread(beta),), (r_targets,), blocks)
    image = 0.5 * basis_1 + scatter_sum_once(part)
    image_targets = lax.all_gather(image, ("gx", "gz"), axis=0, tiled=True)
    sums = sum_exchanged(jnp.stack([dot(basis_1, image), dot(image, image)]))
    h11 = sums[0]
    remainder = image - h11[None, :, None] * basis_1
    square = sums[1] - h11 * h11 * (2.0 - g11)
    square = guarded_square(square, sums[1], remainder)
    h21 = jnp.sqrt(square + EPS)
    basis_2 = remainder / h21[None, :, None]
    g12 = h11 * (1.0 - g11) / h21
    g22 = square / (square + EPS)

    part = product(
        second_kernel, indices, (spread(beta), spread(h11), spread(h21)), (r_targets, image_targets), blocks
    )
    image = 0.5 * basis_2 + scatter_sum_twice(part)
    sums = sum_all_to_all(jnp.stack([dot(basis_1, image), dot(basis_2, image), dot(image, image)]))
    h12, h22 = sums[0], sums[1]
    remainder = image - h12[None, :, None] * basis_1 - h22[None, :, None] * basis_2
    square = sums[2] - h12 * h12 * (2.0 - g11) - h22 * h22 * (2.0 - g22) + 2.0 * h12 * h22 * g12
    square = guarded_square(square, sums[2], remainder)
    h32 = jnp.sqrt(square + EPS)
    basis_3 = remainder / h32[None, :, None]
    arnoldi = jnp.stack([beta, h11, h21, h12, h22, h32], axis=1)
    return jnp.swapaxes(basis_3, 0, 1).reshape(OBJ, CL_DEV * LEAF), arnoldi


def solution(mesh):
    spread = P(ALL)
    return jax.shard_map(
        on_device,
        mesh=mesh,
        in_specs=(P(None, ALL),) + (spread,) * 9,
        out_specs=(P(None, ALL), P()),
        check_vma=False,
    )
```

time: 838 us -> 307 us (0.37)
  waiting for transfers between devices: 261 us -> 8.22 us
  blocking collectives: 435 us -> 208 us
  other arithmetic: 89.8 us -> 2.97 us
  Pallas kernels: 0 us -> 56.7 us
  starting transfers between devices: 0.08 us -> 21.8 us
  matrix products: 21 us -> 0 us
  between operations: 15.4 us -> 3.37 us
  local copies, waits for them, and re-layouts: 13.6 us -> 4.74 us
    psum x5 -> x0, blocking collectives: 388 us -> none  [the longest x2 159 us: on_device(): dots = lax.psum(local_dots, ('gx', 'gy', 'gz'))]
    reduce_scatter x2 -> x0, waiting for transfers between devices: 261 us -> none  [apply_transposed(): lax.psum_scatter(flat, ('gy', 'gz'), scatter_dimension=1, tiled=True)]
    all_to_all x0 -> x5, blocking collectives: none -> 101 us  [the longest x3 78.6 us: scatter_sum(): return lax.all_to_all(pieces, axes, split_axis=0, concat_axis=0).sum(0)]
    scatter-add x4 -> x0, other arithmetic: 80.1 us -> none  [the longest x2 47.9 us: apply_transposed(): partial_value = partial_value.at[:, far_cols].add(contrib_far)]
    all_gather x2 -> x4, blocking collectives: 47.1 us -> 107 us  [the longest x2 48.4 us: sum_gathered(): lax.all_gather(value, axes, axis=0, tiled=True).reshape((-1,) + value.shape)]
    pallas_call x0 -> x2, Pallas kernels: none -> 56.7 us  [product(): pl.pallas_call(kernel, out_shape=jax.ShapeDtypeStruct((SOURCES, OBJ, LEAF...]
    ppermute x0 -> x17, starting transfers between devices: none -> 21.8 us  [exchange(): lax.ppermute(value, axis, [(i, (i + step) % size) for i in range(size)])]
    dot_general x4 -> x0, matrix products: 21 us -> none  [the longest x2 11.8 us: apply_transposed(): jnp.einsum('obr,bsr->obs', reduced, far_right, preferred_element_type=jnp...]
  transfers between devices with their start and end apart: 2 -> 17, of which waited for: 2 -> 7; matrix products, arithmetic and copies ran while one was open for 0% -> 0% of each run, Pallas kernels for 0% -> 0%
where the time goes in v1:
time: 307 us; the launch traced here: 306 us
  blocking collectives  208 us (68%)
  Pallas kernels  56.7 us (18%)
  starting transfers between devices  21.8 us (7%)
  waiting for transfers between devices  8.22 us (3%)
  local copies, waits for them, and re-layouts  4.74 us (2%)
  between operations  3.37 us (1%)
    all_to_all x3, blocking collectives, scatter_sum(): return lax.all_to_all(pieces, axes, split_axis=0, concat_axis=0).sum(0)  78.6 us
    pallas_call x2, Pallas kernels, product(): pl.pallas_call(kernel, out_shape=jax.ShapeDtypeStruct((SOURCES, OBJ, LEAF...  56.7 us
    all_gather x2, blocking collectives, sum_gathered(): lax.all_gather(value, axes, axis=0, tiled=True).reshape((-1,) + value.shape)  48.4 us
    all_gather x1, blocking collectives, on_device(): r_targets = lax.all_gather(r, ('gx', 'gz'), axis=0, tiled=True)  32.6 us
    all_gather x1, blocking collectives, on_device(): image_targets = lax.all_gather(image, ('gx', 'gz'), axis=0, tiled=True)  26.2 us
    all_to_all x2, blocking collectives, sum_all_to_all(): value = lax.all_to_all(copies, axes, split_axis=0, concat_axis=0).sum(0)  22.4 us
    ppermute x17, starting transfers between devices, exchange(): lax.ppermute(value, axis, [(i, (i + step) % size) for i in range(size)])  21.8 us
    ppermute x17, waiting for transfers between devices, exchange(): lax.ppermute(value, axis, [(i, (i + step) % size) for i in range(size)])  8.22 us
  transfers between devices with their start and end apart: 17, of which 7 were waited for; matrix products, arithmetic and copies ran while one was open for 0% of the time, Pallas kernels for 0%

profile of v1, /device:TPU:1, one launch (start us, length us, event | category | flops | bytes accessed | tf_op | source)
XLA Modules:
  0.0 306.0 jit_solution(6622723959344744475)
XLA Ops:
  0.6 0.7 copy-done
  2.7 26.4 %all_gather.12 = f32[512,128]{1,0:T(8,128)S(1)} all-gather(f32[16,128]{1,0:T(8,128)S(1)} %multiply_reduce_fusion.7), channel_id=1, replica_groups=mesh['gx'=4,'gy'=8,'gz'=8] {'gx','gz'}, dimensions={0}, use_global_device_ids=true | all-gather | bytes 270336 | tf_op jit(solution)/shard_map/all_gather | solution.py:135
  29.1 22.0 %all_gather.13 = f32[128,128]{1,0:T(8,128)S(1)} all-gather(f32[16,128]{1,0:T(8,128)S(1)} %reduce_sum.151), channel_id=1, replica_groups=mesh['gx'=4,'gy'=8,'gz'=8] {'gy'}, dimensions={0}, use_global_device_ids=true | all-gather | bytes 73728 | tf_op jit(solution)/shard_map/all_gather | solution.py:135
  51.4 32.6 %all_gather.14.r = f32[64,16,128]{2,1,0:T(8,128)} all-gather(f32[2,16,128]{2,1,0:T(8,128)S(1)} %bitcast_bitcast_fusion), channel_id=1, replica_groups=mesh['gx'=4,'gy'=8,'gz'=8] {'gx','gz'}, dimensions={0}, use_global_device_ids=true | all-gather | bytes 540672 | tf_op jit(solution)/shard_map/all_gather | solution.py:190
  83.9 0.7 broadcast_in_dim.12.beta
  84.6 28.3 %shard_map.113 = f32[128,16,128]{2,1,0:T(8,128)} custom-call(s32[128]{0:T(128)} %nt.3, s32[128]{0:T(128)} %ns.3, s32[1]{0:T(128)S(6)} %copy.58.nc, s32[192]{0:T(256)} %ft.3, s32[192]{0:T(256)} %fs.3, s32[1]{0:T(128)S(6)} %copy.59.fc, f32[16,128]{1,0:T(8,128)} %broadcast_in_dim.12.beta, f32[64,16,128]{2,1,0:T(8,128)} %all_gather.14.r, ...), custom_call_target="tpu_custom_call" | custom-call | flops 170000000 | bytes 12000000 | tf_op jit(solution)/shard_map/pallas_call | solution.py:112
  112.9 40.1 %all_to_all.25 = f32[64,2,16,128]{3,2,1,0:T(8,128)S(1)} all-to-all(f32[64,2,16,128]{3,2,1,0:T(8,128)} %bitcast.118), channel_id=1, replica_groups=mesh['gx'=4,'gy'=8,'gz'=8] {'gy','gz'}, dimensions={0} | all-to-all | bytes 2097152 | tf_op jit(solution)/shard_map/all_to_all | solution.py:164
  153.2 1.7 collective-permute-start.5
  154.9 2.9 collective-permute-start.4
  158.1 2.4 collective-permute-start.2
  160.5 26.2 %all_gather.15.image = f32[64,16,128]{2,1,0:T(8,128)} all-gather(f32[2,16,128]{2,1,0:T(8,128)S(1)} %get-tuple-element.48), channel_id=1, replica_groups=mesh['gx'=4,'gy'=8,'gz'=8] {'gx','gz'}, dimensions={0}, use_global_device_ids=true | all-gather | bytes 540672 | tf_op jit(solution)/shard_map/all_gather | solution.py:198
  186.9 1.6 collective-permute-start
  188.5 1.2 collective-permute-done.6
  189.8 1.2 collective-permute-start.9
  192.2 2.7 collective-permute-done.8
  195.2 1.3 collective-permute-start.15
  196.6 3.1 collective-permute-start.14
  199.6 2.0 collective-permute-start.13
  201.6 1.7 collective-permute-start.12
  203.3 2.6 collective-permute-start.11
  205.9 1.1 collective-permute-done.12
  207.0 0.8 collective-permute-done.11
  207.8 1.7 collective-permute-done.10
  210.9 0.7 broadcast_in_dim.13.h11
  211.6 0.7 broadcast_in_dim.14.h21
  212.3 28.5 %shard_map.114 = f32[128,16,128]{2,1,0:T(8,128)} custom-call(s32[128]{0:T(128)} %nt.3, s32[128]{0:T(128)} %ns.3, s32[1]{0:T(128)S(6)} %copy.58.nc, s32[192]{0:T(256)} %ft.3, s32[192]{0:T(256)} %fs.3, s32[1]{0:T(128)S(6)} %copy.59.fc, f32[16,128]{1,0:T(8,128)} %broadcast_in_dim.12.beta, f32[16,128]{1,0:T(8,128)} %broadcast_in_dim.13.h11, ...), custom_call_target="tpu_custom_call" | custom-call | flops 170000000 | bytes 12000000 | tf_op jit(solution)/shard_map/pallas_call | solution.py:112
  240.8 1.3 copy.53
  242.1 27.5 %all_to_all.26 = f32[8,8,2,16,128]{4,3,2,1,0:T(8,128)S(1)} all-to-all(f32[8,8,2,16,128]{4,3,2,1,0:T(8,128)S(1)} %bitcast.119), channel_id=1, replica_groups=mesh['gx'=4,'gy'=8,'gz'=8] {'gz'}, dimensions={0} | all-to-all | bytes 2097152 | tf_op jit(solution)/shard_map/all_to_all | solution.py:164
  269.7 11.0 %all_to_all.27 = f32[8,1,2,16,128]{4,3,2,1,0:T(8,128)S(1)} all-to-all(f32[8,1,2,16,128]{4,3,2,1,0:T(8,128)S(1)} %bitcast.121), channel_id=1, replica_groups=mesh['gx'=4,'gy'=8,'gz'=8] {'gy'}, dimensions={0} | all-to-all | bytes 262144 | tf_op jit(solution)/shard_map/all_to_all | solution.py:164
  281.0 13.4 %all_to_all.28 = f32[32,3,16]{2,1,0:T(4,128)S(1)} all-to-all(f32[32,3,16]{2,1,0:T(4,128)S(1)} %broadcast_in_dim.15), channel_id=1, replica_groups=mesh['gx'=4,'gy'=8,'gz'=8] {'gx','gz'}, dimensions={0} | all-to-all | bytes 12288 | tf_op jit(solution)/shard_map/all_to_all | solution.py:157
  294.4 9.0 %all_to_all.29 = f32[8,3,16]{2,1,0:T(4,128)S(1)} all-to-all(f32[8,3,16]{2,1,0:T(4,128)S(1)} %broadcast_in_dim.16), channel_id=1, replica_groups=mesh['gx'=4,'gy'=8,'gz'=8] {'gy'}, dimensions={0} | all-to-all | bytes 3072 | tf_op jit(solution)/shard_map/all_to_all | solution.py:157
  304.7 0.7 copy_bitcast_fusion.1
  (51 shorter events, 5.0 us)
Async XLA Ops:
  0.6 0.7 copy-start
  153.2 33.5 %collective-permute-start.5 = (f32[2,16]{1,0:T(2,128)S(1)}, f32[2,16]{1,0:T(2,128)S(1)}, u32[]{:S(2)}, u32[]{:S(2)}) collective-permute-start(f32[2,16]{1,0:T(2,128)S(1)} %pad_maximum_fusion.1), channel_id=1, source_target_pairs={{0,6},{1,7},{2,0},{3,1},{4,2},{5,3},{6,4},{7,5},{8,14},{9,15},{10,... | collective-permute-start | bytes 392 | tf_op jit(solution)/shard_map/ppermute | solution.py:143
  154.9 32.0 %collective-permute-start.4 = (f32[2,16]{1,0:T(2,128)S(1)}, f32[2,16]{1,0:T(2,128)S(1)}, u32[]{:S(2)}, u32[]{:S(2)}) collective-permute-start(f32[2,16]{1,0:T(2,128)S(1)} %pad_maximum_fusion.1), channel_id=1, source_target_pairs={{0,5},{1,6},{2,7},{3,0},{4,1},{5,2},{6,3},{7,4},{8,13},{9,14},{10,... | collective-permute-start | bytes 392 | tf_op jit(solution)/shard_map/ppermute | solution.py:143
  157.8 30.6 %collective-permute-start.3 = (f32[2,16]{1,0:T(2,128)S(1)}, f32[2,16]{1,0:T(2,128)S(1)}, u32[]{:S(2)}, u32[]{:S(2)}) collective-permute-start(f32[2,16]{1,0:T(2,128)S(1)} %pad_maximum_fusion.1), channel_id=1, source_target_pairs={{0,4},{1,5},{2,6},{3,7},{4,0},{5,1},{6,2},{7,3},{8,12},{9,13},{10,... | collective-permute-start | bytes 392 | tf_op jit(solution)/shard_map/ppermute | solution.py:143
  158.1 30.4 %collective-permute-start.2 = (f32[2,16]{1,0:T(2,128)S(1)}, f32[2,16]{1,0:T(2,128)S(1)}, u32[]{:S(2)}, u32[]{:S(2)}) collective-permute-start(f32[2,16]{1,0:T(2,128)S(1)} %pad_maximum_fusion.1), channel_id=1, source_target_pairs={{0,3},{1,4},{2,5},{3,6},{4,7},{5,0},{6,1},{7,2},{8,11},{9,12},{10,... | collective-permute-start | bytes 392 | tf_op jit(solution)/shard_map/ppermute | solution.py:143
  160.5 28.0 %collective-permute-start.1 = (f32[2,16]{1,0:T(2,128)S(1)}, f32[2,16]{1,0:T(2,128)S(1)}, u32[]{:S(2)}, u32[]{:S(2)}) collective-permute-start(f32[2,16]{1,0:T(2,128)S(1)} %pad_maximum_fusion.1), channel_id=1, source_target_pairs={{0,2},{1,3},{2,4},{3,5},{4,6},{5,7},{6,0},{7,1},{8,10},{9,11},{10,... | collective-permute-start | bytes 392 | tf_op jit(solution)/shard_map/ppermute | solution.py:143
  186.7 3.0 collective-permute-start.6
  186.9 2.8 collective-permute-start
  189.8 2.5 collective-permute-start.9
  191.0 3.9 %collective-permute-start.8 = (f32[2,16]{1,0:T(2,128)S(1)}, f32[2,16]{1,0:T(2,128)S(1)}, u32[]{:S(2)}, u32[]{:S(2)}) collective-permute-start(f32[2,16]{1,0:T(2,128)S(1)} %add_add_fusion.2), channel_id=1, source_target_pairs={{0,128},{64,192},{128,0},{192,64},{1,129},{65,193},{129,1},{193,65... | collective-permute-start | bytes 392 | tf_op jit(solution)/shard_map/ppermute | solution.py:143
  191.6 3.6 %collective-permute-start.7 = (f32[2,16]{1,0:T(2,128)S(1)}, f32[2,16]{1,0:T(2,128)S(1)}, u32[]{:S(2)}, u32[]{:S(2)}) collective-permute-start(f32[2,16]{1,0:T(2,128)S(1)} %add_add_fusion.2), channel_id=1, source_target_pairs={{0,64},{64,128},{128,192},{192,0},{1,65},{65,129},{129,193},{193,1... | collective-permute-start | bytes 392 | tf_op jit(solution)/shard_map/ppermute | solution.py:143
  195.2 8.1 %collective-permute-start.16 = (f32[2,16]{1,0:T(2,128)S(1)}, f32[2,16]{1,0:T(2,128)S(1)}, u32[]{:S(2)}, u32[]{:S(2)}) collective-permute-start(f32[2,16]{1,0:T(2,128)S(1)} %add_add_fusion.1), channel_id=1, source_target_pairs={{0,56},{8,0},{16,8},{24,16},{32,24},{40,32},{48,40},{56,48},{1,57}... | collective-permute-start | bytes 392 | tf_op jit(solution)/shard_map/ppermute | solution.py:143
  195.2 10.7 %collective-permute-start.15 = (f32[2,16]{1,0:T(2,128)S(1)}, f32[2,16]{1,0:T(2,128)S(1)}, u32[]{:S(2)}, u32[]{:S(2)}) collective-permute-start(f32[2,16]{1,0:T(2,128)S(1)} %add_add_fusion.1), channel_id=1, source_target_pairs={{0,48},{8,56},{16,0},{24,8},{32,16},{40,24},{48,32},{56,40},{1,49}... | collective-permute-start | bytes 392 | tf_op jit(solution)/shard_map/ppermute | solution.py:143
  196.6 9.4 %collective-permute-start.14 = (f32[2,16]{1,0:T(2,128)S(1)}, f32[2,16]{1,0:T(2,128)S(1)}, u32[]{:S(2)}, u32[]{:S(2)}) collective-permute-start(f32[2,16]{1,0:T(2,128)S(1)} %add_add_fusion.1), channel_id=1, source_target_pairs={{0,40},{8,48},{16,56},{24,0},{32,8},{40,16},{48,24},{56,32},{1,41}... | collective-permute-start | bytes 392 | tf_op jit(solution)/shard_map/ppermute | solution.py:143
  199.6 6.3 %collective-permute-start.13 = (f32[2,16]{1,0:T(2,128)S(1)}, f32[2,16]{1,0:T(2,128)S(1)}, u32[]{:S(2)}, u32[]{:S(2)}) collective-permute-start(f32[2,16]{1,0:T(2,128)S(1)} %add_add_fusion.1), channel_id=1, source_target_pairs={{0,32},{8,40},{16,48},{24,56},{32,0},{40,8},{48,16},{56,24},{1,33}... | collective-permute-start | bytes 392 | tf_op jit(solution)/shard_map/ppermute | solution.py:143
  201.6 5.4 %collective-permute-start.12 = (f32[2,16]{1,0:T(2,128)S(1)}, f32[2,16]{1,0:T(2,128)S(1)}, u32[]{:S(2)}, u32[]{:S(2)}) collective-permute-start(f32[2,16]{1,0:T(2,128)S(1)} %add_add_fusion.1), channel_id=1, source_target_pairs={{0,24},{8,32},{16,40},{24,48},{32,56},{40,0},{48,8},{56,16},{1,25}... | collective-permute-start | bytes 392 | tf_op jit(solution)/shard_map/ppermute | solution.py:143
  203.3 4.5 %collective-permute-start.11 = (f32[2,16]{1,0:T(2,128)S(1)}, f32[2,16]{1,0:T(2,128)S(1)}, u32[]{:S(2)}, u32[]{:S(2)}) collective-permute-start(f32[2,16]{1,0:T(2,128)S(1)} %add_add_fusion.1), channel_id=1, source_target_pairs={{0,16},{8,24},{16,32},{24,40},{32,48},{40,56},{48,0},{56,8},{1,17}... | collective-permute-start | bytes 392 | tf_op jit(solution)/shard_map/ppermute | solution.py:143
  205.9 3.6 %collective-permute-start.10 = (f32[2,16]{1,0:T(2,128)S(1)}, f32[2,16]{1,0:T(2,128)S(1)}, u32[]{:S(2)}, u32[]{:S(2)}) collective-permute-start(f32[2,16]{1,0:T(2,128)S(1)} %add_add_fusion.1), channel_id=1, source_target_pairs={{0,8},{8,16},{16,24},{24,32},{32,40},{40,48},{48,56},{56,0},{1,9},... | collective-permute-start | bytes 392 | tf_op jit(solution)/shard_map/ppermute | solution.py:143

commit v2 on v1

v2 whole, which is shorter than its diff:
```python
import functools

import jax
import jax.numpy as jnp
from jax import lax
from jax.experimental import pallas as pl
from jax.experimental.pallas import tpu as pltpu
from jax.sharding import Mesh
from jax.sharding import PartitionSpec as P

OBJ = 16
LEAF = 128
RANK = 64
CL_DEV = 2
NEAR_DEV = 128
FAR_DEV = 192
EPS = 1e-06

ALL = ("gx", "gy", "gq", "core")
PLANE = ("gx", "gq", "core")
TARGETS = 64
SOURCES = 128
NEAR_CHUNK = 32
FAR_CHUNK = 48
NEAR_STEP = 16
FAR_STEP = 16

SMEM = pl.BlockSpec(memory_space=pltpu.SMEM)
VMEM = pl.BlockSpec(memory_space=pltpu.VMEM)
HBM = pl.BlockSpec(memory_space=pltpu.HBM)


def target_row(cluster):
    return (cluster >> 7) * 16 + (cluster & 15)


def source_row(cluster, core):
    local = cluster & (SOURCES - 1)
    other = ((local >> 1) & 1) ^ core
    return other * (SOURCES // 2) + ((local >> 2) << 1) + (local & 1)


def start_blocks(near, left, right, near_v, left_v, right_v, sems):
    copies = []
    for i in range(NEAR_DEV // NEAR_CHUNK):
        part = pl.ds(i * NEAR_CHUNK, NEAR_CHUNK)
        copies.append(pltpu.make_async_copy(near.at[part], near_v.at[part], sems.at[len(copies)]))
    for i in range(FAR_DEV // FAR_CHUNK):
        part = pl.ds(i * FAR_CHUNK, FAR_CHUNK)
        copies.append(pltpu.make_async_copy(left.at[part], left_v.at[part], sems.at[len(copies)]))
        copies.append(pltpu.make_async_copy(right.at[part], right_v.at[part], sems.at[len(copies)]))
    for copy in copies:
        copy.start()
    return copies


def two_terms(value):
    high = value.astype(jnp.bfloat16)
    return high, (value - high.astype(jnp.float32)).astype(jnp.bfloat16)


def multiply(copies, field, x, near_v, left_v, right_v, nt, ns, nc, ft, fs, fc, keep, send, acc):
    core = lax.axis_index("core")
    near_live = nc[0]
    far_live = fc[0]
    high, low = two_terms(field[...])
    x[:TARGETS, :OBJ] = high
    x[:TARGETS, OBJ:] = low
    x[TARGETS] = jnp.zeros((2 * OBJ, LEAF), jnp.bfloat16)
    acc[...] = jnp.zeros_like(acc)
    own_half = lax.broadcasted_iota(jnp.int32, (2 * OBJ, LEAF), 0) // OBJ == (
        lax.broadcasted_iota(jnp.int32, (2 * OBJ, LEAF), 1) // RANK
    )

    def rows(slot, count, live, targets):
        picked = [
            x[jnp.where(slot + i < live, target_row(targets[slot + i]), TARGETS)] for i in range(count)
        ]
        return jnp.concatenate(picked, axis=0)

    def near_step(first):
        parts = []
        for i in range(0, NEAR_STEP, 2):
            slot = first + i
            pair = jnp.concatenate([near_v[slot], near_v[slot + 1]], axis=1)
            both = jnp.dot(rows(slot, 2, near_live, nt), pair, preferred_element_type=jnp.float32)
            parts.append(both[:OBJ, :LEAF] + both[OBJ : 2 * OBJ, :LEAF])
            parts.append(both[2 * OBJ : 3 * OBJ, LEAF:] + both[3 * OBJ :, LEAF:])
        for i, part in enumerate(parts):
            acc[source_row(ns[first + i], core)] += part

    def far_step(first):
        reduced = []
        for i in range(0, FAR_STEP, 4):
            slot = first + i
            lefts = left_v[pl.ds(slot, 4)].reshape(4 * RANK, LEAF)
            both = lax.dot_general(
                rows(slot, 4, far_live, ft), lefts, (((1,), (1,)), ((), ())), preferred_element_type=jnp.float32
            )
            for half in (both[: 4 * OBJ, :LEAF], both[4 * OBJ :, LEAF:]):
                pair = [half[j : j + OBJ] + half[j + OBJ : j + 2 * OBJ] for j in (0, 2 * OBJ)]
                reduced += two_terms(jnp.where(own_half, jnp.concatenate(pair, axis=0), 0.0))
        parts = []
        for i in range(0, FAR_STEP, 4):
            slot = first + i
            rights = jnp.concatenate(
                [
                    right_v[pl.ds(slot, 2)].reshape(2 * RANK, LEAF),
                    right_v[pl.ds(slot + 2, 2)].reshape(2 * RANK, LEAF),
                ],
                axis=1,
            )
            both = jnp.dot(
                jnp.concatenate(reduced[i : i + 4], axis=0), rights, preferred_element_type=jnp.float32
            )
            for half in (both[: 4 * OBJ, :LEAF], both[4 * OBJ :, LEAF:]):
                parts += [half[j : j + OBJ] + half[j + 2 * OBJ : j + 3 * OBJ] for j in (0, OBJ)]
        for i, part in enumerate(parts):
            acc[source_row(fs[first + i], core)] += part

    def run(step, size, first, live, chunk):
        groups = (jnp.clip(live - first, 0, chunk) + size - 1) // size

        def body(group, carry):
            step(first + group * size)
            return carry

        lax.fori_loop(0, groups, body, 0)

    if copies is None:
        run(near_step, NEAR_STEP, 0, near_live, NEAR_DEV)
        run(far_step, FAR_STEP, 0, far_live, FAR_DEV)
    else:
        done = 0
        for i in range(NEAR_DEV // NEAR_CHUNK):
            copies[done].wait()
            done += 1
            run(near_step, NEAR_STEP, i * NEAR_CHUNK, near_live, NEAR_CHUNK)
        for i in range(FAR_DEV // FAR_CHUNK):
            copies[done].wait()
            copies[done + 1].wait()
            done += 2
            run(far_step, FAR_STEP, i * FAR_CHUNK, far_live, FAR_CHUNK)
    keep[...] = acc[: SOURCES // 2]
    send[...] = acc[SOURCES // 2 :]


def first_kernel(nt, ns, nc, ft, fs, fc, field, near, left, right, keep, send, near_v, left_v, right_v, x, acc, sems):
    copies = start_blocks(near, left, right, near_v, left_v, right_v, sems)
    multiply(copies, field, x, near_v, left_v, right_v, nt, ns, nc, ft, fs, fc, keep, send, acc)


def second_kernel(nt, ns, nc, ft, fs, fc, field, near_v, left_v, right_v, keep, send, x, acc):
    multiply(None, field, x, near_v, left_v, right_v, nt, ns, nc, ft, fs, fc, keep, send, acc)


def product(indices, field, blocks, first):
    half = jax.ShapeDtypeStruct((SOURCES // 2, OBJ, LEAF), jnp.float32)
    scratch = [
        pltpu.VMEM((TARGETS + 1, 2 * OBJ, LEAF), jnp.bfloat16),
        pltpu.VMEM((SOURCES, OBJ, LEAF), jnp.float32),
    ]
    outs = (half, half)
    if first:
        outs += tuple(pltpu.VMEM(block.shape, block.dtype) for block in blocks)
        scratch.append(pltpu.SemaphoreType.DMA((NEAR_DEV // NEAR_CHUNK + 2 * (FAR_DEV // FAR_CHUNK),)))
    return pl.pallas_call(
        first_kernel if first else second_kernel,
        out_shape=outs,
        in_specs=[SMEM] * 6 + [VMEM] + [HBM if first else VMEM] * 3,
        out_specs=(VMEM,) * len(outs),
        scratch_shapes=scratch,
        compiler_params=pltpu.CompilerParams(vmem_limit_bytes=24 * 1024 * 1024),
        cost_estimate=pl.CostEstimate(flops=170_000_000, bytes_accessed=12_000_000, transcendentals=0),
    )(*indices, field, *blocks)


def to_all(value, axes):
    size = lax.axis_size(axes)
    return lax.all_to_all(jnp.broadcast_to(value[None], (size,) + value.shape), axes, split_axis=0, concat_axis=0)


def scatter_sum(keep, send):
    chip = keep + lax.ppermute(send, "core", [(0, 1), (1, 0)])
    pieces = chip.reshape(-1, CL_DEV, OBJ, LEAF)
    return jnp.sum(lax.all_to_all(pieces, ("gy", "gq"), split_axis=0, concat_axis=0), axis=0)


def dot(first, second):
    return jnp.sum(first * second, axis=(0, 2))


def column(value):
    return value[None, :, None]


def plainly(r, indices, blocks):
    nt, ns, nc, ft, fs, fc = indices
    near, left, right = blocks
    near_alive = (jnp.arange(NEAR_DEV, dtype=jnp.int32) < nc[0]).astype(jnp.float32)
    far_alive = (jnp.arange(FAR_DEV, dtype=jnp.int32) < fc[0]).astype(jnp.float32)

    def total(first, second):
        return lax.psum(dot(first, second), ALL)

    def apply(vector):
        gathered = lax.all_gather(vector.astype(jnp.bfloat16), PLANE, axis=0, tiled=True)
        partial = jnp.zeros((SOURCES, OBJ, LEAF), jnp.float32)
        picked = gathered[target_row(nt)]
        parts = jnp.einsum("bol,bls->bos", picked, near, preferred_element_type=jnp.float32)
        partial = partial.at[ns & (SOURCES - 1)].add(parts * near_alive[:, None, None])
        picked = gathered[target_row(ft)]
        reduced = jnp.einsum("bol,brl->bor", picked, left, preferred_element_type=jnp.float32).astype(jnp.bfloat16)
        parts = jnp.einsum("bor,brs->bos", reduced, right, preferred_element_type=jnp.float32)
        partial = partial.at[fs & (SOURCES - 1)].add(parts * far_alive[:, None, None])
        summed = lax.psum_scatter(partial, ("gy", "gq", "core"), scatter_dimension=0, tiled=True)
        return 0.5 * vector + summed

    length = jnp.sqrt(total(r, r) + EPS)
    basis = [r / column(length)]
    entries = [length]
    for _ in range(2):
        image = apply(basis[-1])
        coeffs = [total(member, image) for member in basis]
        remainder = image
        for member, coeff in zip(basis, coeffs):
            remainder = remainder - column(coeff) * member
        length = jnp.sqrt(total(remainder, remainder) + EPS)
        basis.append(remainder / column(length))
        entries += coeffs + [length]
    return basis[-1], jnp.stack(entries)


def on_device(r0, near_tiles, nt, ns, nc, far_left, far_right, ft, fs, fc):
    indices = (nt, ns, nc, ft, fs, fc)
    blocks = (near_tiles, jnp.swapaxes(far_left, 1, 2), jnp.swapaxes(far_right, 1, 2))
    r = jnp.swapaxes(r0.reshape(OBJ, CL_DEV, LEAF), 0, 1)

    r_targets = to_all(r, PLANE).reshape(TARGETS, OBJ, LEAF)
    keep, send, *held = product(indices, r_targets, blocks, True)
    u = 0.5 * r + scatter_sum(keep, send)
    u_targets = to_all(u, PLANE).reshape(TARGETS, OBJ, LEAF)
    keep, send = product(indices, u_targets, held, False)
    w = 0.5 * u + scatter_sum(keep, send)

    local = jnp.stack([dot(r, r), dot(r, u), dot(u, u), dot(r, w), dot(u, w), dot(w, w)])
    sums = jnp.sum(to_all(jnp.sum(to_all(local, PLANE), axis=0), "gy"), axis=0)
    rr, ru, uu, rw, uw, ww = (sums[i] for i in range(6))
    beta_sq = rr + EPS
    beta = jnp.sqrt(beta_sq)
    h11 = ru / beta_sq
    left_1 = (uu - 2.0 * h11 * ru + h11 * h11 * rr) / beta_sq
    h21 = jnp.sqrt(left_1 + EPS)
    scale = 1.0 / (beta * h21)
    g11 = rr / beta_sq
    g12 = (ru - h11 * rr) / beta_sq / h21
    g22 = left_1 / (left_1 + EPS)
    h12 = (rw - h11 * ru) / beta_sq / h21
    h22 = (uw - h11 * uu - h11 * (rw - h11 * ru)) * scale * scale
    image_sq = (ww - 2.0 * h11 * uw + h11 * h11 * uu) * scale * scale
    left_2 = image_sq - h12 * h12 * (2.0 - g11) - h22 * h22 * (2.0 - g22) + 2.0 * h12 * h22 * g12
    h32 = jnp.sqrt(left_2 + EPS)
    entries = jnp.stack([beta, h11, h21, h12, h22, h32])
    in_w = scale / h32
    in_u = -(h11 + h22) * in_w
    in_r = (h11 * h22 * scale - h12 / beta) / h32
    basis_3 = column(in_w) * w + column(in_u) * u + column(in_r) * r
    small = 1.0 / 1024.0
    dependent = jnp.any((left_1 * beta_sq < small * uu) | (left_2 < small * ww * scale * scale))
    basis_3, entries = lax.cond(
        dependent, lambda: plainly(r, indices, blocks), lambda: (basis_3, entries)
    )
    return jnp.swapaxes(basis_3, 0, 1).reshape(OBJ, CL_DEV * LEAF), entries.T


def solution(mesh):
    fine = Mesh(mesh.devices.reshape(4, 8, 4, 2), ALL)
    spread = P(ALL)
    return jax.shard_map(
        on_device,
        mesh=fine,
        in_specs=(P(None, ALL),) + (spread,) * 9,
        out_specs=(P(None, ALL), P()),
        check_vma=False,
    )
```

time: 307 us -> 159 us (0.52)
  blocking collectives: 208 us -> 77.5 us
  Pallas kernels: 56.7 us -> 14.9 us
  between operations: 3.37 us -> 16.1 us
  waiting for transfers between devices: 8.22 us -> 20.8 us
  starting transfers between devices: 21.8 us -> 12.2 us
  local copies, waits for them, and re-layouts: 4.74 us -> 12.4 us
    all_gather x4 -> x0, blocking collectives: 107 us -> none  [the longest x2 48.4 us: sum_gathered(): lax.all_gather(value, axes, axis=0, tiled=True).reshape((-1,) + value.shape)]
    pallas_call x2, Pallas kernels: 56.7 us -> 14.9 us  [product(): pl.pallas_call(first_kernel if first else second_kernel, out_shape=outs,...]
    all_to_all x5 -> x4, blocking collectives: 101 us -> 77.5 us  [the longest x2 46.4 us: scatter_sum(): lax.all_to_all(pieces, ('gy', 'gq'), split_axis=0, concat_axis=0)]
    ppermute x17 -> x2, starting transfers between devices: 21.8 us -> 0.25 us  [scatter_sum(): chip = keep + lax.ppermute(send, 'core', [(0, 1), (1, 0)])]
    all_to_all x0 -> x2, waiting for transfers between devices: none -> 17.1 us  [to_all(): lax.all_to_all(jnp.broadcast_to(value[None], (size,) + value.shape), axes...]
    all_to_all x0 -> x2, starting transfers between devices: none -> 11.9 us  [to_all(): lax.all_to_all(jnp.broadcast_to(value[None], (size,) + value.shape), axes...]
    unnamed x2 -> x26, local copies, waits for them, and re-layouts: 0.72 us -> 10.2 us
    ppermute x17 -> x2, waiting for transfers between devices: 8.22 us -> 3.73 us  [scatter_sum(): chip = keep + lax.ppermute(send, 'core', [(0, 1), (1, 0)])]
  transfers between devices with their start and end apart: 17 -> 4, of which waited for: 7 -> 4; matrix products, arithmetic and copies ran while one was open for 0% -> 0% of each run, Pallas kernels for 0% -> 0%
where the time goes in v2:
time: 159 us; the launch traced here: 157 us
  blocking collectives  77.5 us (49%)
  waiting for transfers between devices  20.8 us (13%)
  between operations  16.1 us (10%)
  Pallas kernels  14.9 us (9%)
  local copies, waits for them, and re-layouts  12.4 us (8%)
  starting transfers between devices  12.2 us (8%)
  other arithmetic  3.43 us (2%)
    all_to_all x2, blocking collectives, scatter_sum(): lax.all_to_all(pieces, ('gy', 'gq'), split_axis=0, concat_axis=0)  46.4 us
    all_to_all x2, blocking collectives, to_all(): lax.all_to_all(jnp.broadcast_to(value[None], (size,) + value.shape), axes...  31.1 us
    all_to_all x2, waiting for transfers between devices, to_all(): lax.all_to_all(jnp.broadcast_to(value[None], (size,) + value.shape), axes...  17.1 us
    pallas_call x2, Pallas kernels, product(): pl.pallas_call(first_kernel if first else second_kernel, out_shape=outs,...  14.9 us
    all_to_all x2, starting transfers between devices, to_all(): lax.all_to_all(jnp.broadcast_to(value[None], (size,) + value.shape), axes...  11.9 us
    unnamed x26, local copies, waits for them, and re-layouts  10.2 us
    ppermute x2, waiting for transfers between devices, scatter_sum(): chip = keep + lax.ppermute(send, 'core', [(0, 1), (1, 0)])  3.73 us
  transfers between devices with their start and end apart: 4, of which 4 were waited for; matrix products, arithmetic and copies ran while one was open for 0% of the time, Pallas kernels for 0%

profile of v2, /device:TPU:1, one launch (start us, length us, event | category | flops | bytes accessed | tf_op | source)
XLA Modules:
  0.0 157.5 jit_solution(6057040132599526927)
XLA Ops:
  7.2 0.7 copy-done
  7.9 0.9 broadcast_in_dim.16
  8.7 8.6 %all-to-all-start = ((f32[32,2,16,128]{3,2,1,0:T(8,128)}), f32[32,2,16,128]{3,2,1,0:T(8,128)S(1)}, u32[]{:S(2)}, u32[]{:S(2)}) async-start(f32[32,2,16,128]{3,2,1,0:T(8,128)} %broadcast_in_dim.16), calls=%async_computation.2 | async-start | bytes 1048576 | tf_op jit(solution)/shard_map/all_to_all | solution.py:180
  18.6 10.3 %all-to-all-done = f32[32,2,16,128]{3,2,1,0:T(8,128)S(1)} async-done(((f32[32,2,16,128]{3,2,1,0:T(8,128)}), f32[32,2,16,128]{3,2,1,0:T(8,128)S(1)}, u32[]{:S(2)}, u32[]{:S(2)}) %all-to-all-start) | async-done | bytes 524320 | tf_op jit(solution)/shard_map/all_to_all | solution.py:180
  28.9 0.8 copy-done.5
  29.7 1.0 copy-done.6
  30.7 8.2 %shard_map.113 = (f32[64,16,128]{2,1,0:T(8,128)S(1)}, f32[64,16,128]{2,1,0:T(8,128)S(1)}, bf16[128,128,128]{2,1,0:T(8,128)(2,1)S(1)}, bf16[192,64,128]{2,1,0:T(8,128)(2,1)S(1)}, bf16[192,64,128]{2,1,0:T(8,128)(2,1)S(1)}) custom-call(s32[128]{0:T(128)} %nt.3, s32[128]{0:T(128)} %ns.3, s32[1]{0:T(128)S(6)} %copy.56.nc, s32[192]{0:T(256)} %ft.3, s32[192]{0:T(256)} %fs.3, ...), custom_call_target="tpu_custom_call" | custom-call | flops 170000000 | bytes 12000000 | tf_op jit(solution)/shard_map/pallas_call | solution.py:167
  39.0 1.9 %copy-done.1 = bf16[128,128,128]{2,1,0:T(8,128)(2,1)} copy-done((bf16[128,128,128]{2,1,0:T(8,128)(2,1)}, bf16[128,128,128]{2,1,0:T(8,128)(2,1)S(1)}, u32[]{:S(2)}) %copy-start.1) | copy-done | bytes 4194328
  40.9 1.7 %copy-done.3 = bf16[192,64,128]{2,1,0:T(8,128)(2,1)} copy-done((bf16[192,64,128]{2,1,0:T(8,128)(2,1)}, bf16[192,64,128]{2,1,0:T(8,128)(2,1)S(1)}, u32[]{:S(2)}) %copy-start.3) | copy-done | bytes 3145752
  42.6 0.2 collective-permute-start
  42.7 1.8 %collective-permute-done = f32[64,16,128]{2,1,0:T(8,128)S(1)} collective-permute-done((f32[64,16,128]{2,1,0:T(8,128)S(1)}, f32[64,16,128]{2,1,0:T(8,128)S(1)}, u32[]{:S(2)}, u32[]{:S(2)}) %collective-permute-start) | collective-permute-done | bytes 524320 | tf_op jit(solution)/shard_map/ppermute | solution.py:184
  44.6 0.1 add.253
  44.6 26.1 %all_to_all.30 = f32[32,2,16,128]{3,2,1,0:T(8,128)} all-to-all(f32[32,2,16,128]{3,2,1,0:T(8,128)S(1)} %bitcast.214), channel_id=1, replica_groups=mesh['gx'=4,'gy'=8,'gq'=4,'core'=2] {'gy','gq'}, dimensions={0} | all-to-all | bytes 1048576 | tf_op jit(solution)/shard_map/all_to_all | solution.py:186
  70.8 1.1 reduce_sum.145
  71.9 17.4 %all_to_all.31 = f32[32,2,16,128]{3,2,1,0:T(8,128)S(1)} all-to-all(f32[32,2,16,128]{3,2,1,0:T(8,128)S(1)} %broadcast_in_dim.17), channel_id=1, replica_groups=mesh['gx'=4,'gy'=8,'gq'=4,'core'=2] {'gx','gq','core'}, dimensions={0} | all-to-all | bytes 1048576 | tf_op jit(solution)/shard_map/all_to_all | solution.py:180
  89.3 2.2 %copy-done.2 = bf16[128,128,128]{2,1,0:T(8,128)(2,1)S(1)} copy-done((bf16[128,128,128]{2,1,0:T(8,128)(2,1)S(1)}, bf16[128,128,128]{2,1,0:T(8,128)(2,1)}, u32[]{:S(2)}) %copy-start.2) | copy-done | bytes 4194328
  91.5 1.9 %copy-done.4 = bf16[192,64,128]{2,1,0:T(8,128)(2,1)S(1)} copy-done((bf16[192,64,128]{2,1,0:T(8,128)(2,1)S(1)}, bf16[192,64,128]{2,1,0:T(8,128)(2,1)}, u32[]{:S(2)}) %copy-start.4) | copy-done | bytes 3145752
  93.4 6.6 %shard_map.114 = (f32[64,16,128]{2,1,0:T(8,128)S(1)}, f32[64,16,128]{2,1,0:T(8,128)S(1)}) custom-call(s32[128]{0:T(128)S(1)} %copy-done.12, s32[128]{0:T(128)S(1)} %copy-done.13, s32[1]{0:T(128)S(6)} %copy.56.nc, s32[192]{0:T(256)S(1)} %copy-done.10, s32[192]{0:T(256)S(1)} %copy-done.11, s32[1]{0:T(128)S(6)} %copy.57.fc, f32[64,16,128]{2,1,0:T(8,128)S(1)} %bitcast.209, ...), custom_call_target="tpu_custom_call" | custom-call | flops 170000000 | bytes 12000000 | tf_op jit(solution)/shard_map/pallas_call | solution.py:167
  100.0 0.1 collective-permute-start.1
  100.1 1.9 %collective-permute-done.1 = f32[64,16,128]{2,1,0:T(8,128)S(1)} collective-permute-done((f32[64,16,128]{2,1,0:T(8,128)S(1)}, f32[64,16,128]{2,1,0:T(8,128)S(1)}, u32[]{:S(2)}, u32[]{:S(2)}) %collective-permute-start.1) | collective-permute-done | bytes 524320 | tf_op jit(solution)/shard_map/ppermute | solution.py:184
  102.0 0.1 add.255
  102.1 20.2 %all_to_all.32 = f32[32,2,16,128]{3,2,1,0:T(8,128)} all-to-all(f32[32,2,16,128]{3,2,1,0:T(8,128)S(1)} %bitcast.215), channel_id=1, replica_groups=mesh['gx'=4,'gy'=8,'gq'=4,'core'=2] {'gy','gq'}, dimensions={0} | all-to-all | bytes 1048576 | tf_op jit(solution)/shard_map/all_to_all | solution.py:186
  122.4 1.1 reduce_sum.148
  123.5 0.2 multiply_reduce_fusion.6
  123.7 13.8 %all_to_all.33 = f32[32,6,16]{2,1,0:T(8,128)S(1)} all-to-all(f32[32,6,16]{2,1,0:T(8,128)S(1)} %broadcast_in_dim.18), channel_id=1, replica_groups=mesh['gx'=4,'gy'=8,'gq'=4,'core'=2] {'gx','gq','core'}, dimensions={0} | all-to-all | bytes 24576 | tf_op jit(solution)/shard_map/all_to_all | solution.py:180
  137.5 0.6 broadcast_in_dim.19
  138.1 3.3 %all-to-all-start.5 = ((f32[8,6,16]{2,1,0:T(8,128)}), f32[8,6,16]{2,1,0:T(8,128)S(1)}, u32[]{:S(2)}, u32[]{:S(2)}) async-start(f32[8,6,16]{2,1,0:T(8,128)} %broadcast_in_dim.19), calls=%async_computation.7 | async-start | bytes 65536 | tf_op jit(solution)/shard_map/all_to_all | solution.py:180
  141.4 6.8 %all-to-all-done.5 = f32[8,6,16]{2,1,0:T(8,128)S(1)} async-done(((f32[8,6,16]{2,1,0:T(8,128)}), f32[8,6,16]{2,1,0:T(8,128)S(1)}, u32[]{:S(2)}, u32[]{:S(2)}) %all-to-all-start.5) | async-done | bytes 3104 | tf_op jit(solution)/shard_map/all_to_all | solution.py:180
  148.3 0.7 or_reduce_fusion
  149.7 0.3 conditional.1
  149.8 0.1 multiply_add_fusion
  150.0 0.6 copy_bitcast_fusion
  (34 shorter events, 0.3 us)
Async XLA Ops:
  7.2 0.7 copy-start
  8.7 20.1 %all-to-all-start = ((f32[32,2,16,128]{3,2,1,0:T(8,128)}), f32[32,2,16,128]{3,2,1,0:T(8,128)S(1)}, u32[]{:S(2)}, u32[]{:S(2)}) async-start(f32[32,2,16,128]{3,2,1,0:T(8,128)} %broadcast_in_dim.16), calls=%async_computation.2 | async-start | bytes 1048576 | tf_op jit(solution)/shard_map/all_to_all | solution.py:180
  28.9 0.8 copy-start.5
  29.7 1.0 copy-start.6
  39.0 1.9 %copy-start.1 = (bf16[128,128,128]{2,1,0:T(8,128)(2,1)}, bf16[128,128,128]{2,1,0:T(8,128)(2,1)S(1)}, u32[]{:S(2)}) copy-start(bf16[128,128,128]{2,1,0:T(8,128)(2,1)S(1)} %get-tuple-element.193.near_v) | copy-start | bytes 12582916
  40.9 1.7 %copy-start.3 = (bf16[192,64,128]{2,1,0:T(8,128)(2,1)}, bf16[192,64,128]{2,1,0:T(8,128)(2,1)S(1)}, u32[]{:S(2)}) copy-start(bf16[192,64,128]{2,1,0:T(8,128)(2,1)S(1)} %get-tuple-element.195.right_v) | copy-start | bytes 9437188
  42.6 46.7 %copy-start.10 = (s32[192]{0:T(256)S(1)}, s32[192]{0:T(256)}, u32[]{:S(2)}) copy-start(s32[192]{0:T(256)} %ft.3) | copy-start | bytes 2308
  42.6 46.7 %copy-start.11 = (s32[192]{0:T(256)S(1)}, s32[192]{0:T(256)}, u32[]{:S(2)}) copy-start(s32[192]{0:T(256)} %fs.3) | copy-start | bytes 2308
  42.6 46.7 %copy-start.12 = (s32[128]{0:T(128)S(1)}, s32[128]{0:T(128)}, u32[]{:S(2)}) copy-start(s32[128]{0:T(128)} %nt.3) | copy-start | bytes 1540
  42.6 46.7 %copy-start.13 = (s32[128]{0:T(128)S(1)}, s32[128]{0:T(128)}, u32[]{:S(2)}) copy-start(s32[128]{0:T(128)} %ns.3) | copy-start | bytes 1540
  42.6 2.0 %collective-permute-start = (f32[64,16,128]{2,1,0:T(8,128)S(1)}, f32[64,16,128]{2,1,0:T(8,128)S(1)}, u32[]{:S(2)}, u32[]{:S(2)}) collective-permute-start(f32[64,16,128]{2,1,0:T(8,128)S(1)} %get-tuple-element.192), channel_id=1, source_target_pairs={{0,1},{1,0},{2,3},{3,2},{4,5},{5,4},{6,7},{7,6},{8,9},{9,8},{10,11... | collective-permute-start | bytes 1572872 | tf_op jit(solution)/shard_map/ppermute | solution.py:184
  89.3 2.2 %copy-start.2 = (bf16[128,128,128]{2,1,0:T(8,128)(2,1)S(1)}, bf16[128,128,128]{2,1,0:T(8,128)(2,1)}, u32[]{:S(2)}) copy-start(bf16[128,128,128]{2,1,0:T(8,128)(2,1)} %copy-done.1) | copy-start | bytes 12582916
  91.5 1.9 %copy-start.4 = (bf16[192,64,128]{2,1,0:T(8,128)(2,1)S(1)}, bf16[192,64,128]{2,1,0:T(8,128)(2,1)}, u32[]{:S(2)}) copy-start(bf16[192,64,128]{2,1,0:T(8,128)(2,1)} %copy-done.3) | copy-start | bytes 9437188
  100.0 49.7 %copy-start.7 = (bf16[192,128,64]{1,2,0:T(8,128)(2,1)S(1)}, bf16[192,128,64]{1,2,0:T(8,128)(2,1)}, u32[]{:S(2)}) copy-start(bf16[192,128,64]{1,2,0:T(8,128)(2,1)} %param.17) | copy-start | bytes 9437188
  100.0 2.0 %collective-permute-start.1 = (f32[64,16,128]{2,1,0:T(8,128)S(1)}, f32[64,16,128]{2,1,0:T(8,128)S(1)}, u32[]{:S(2)}, u32[]{:S(2)}) collective-permute-start(f32[64,16,128]{2,1,0:T(8,128)S(1)} %get-tuple-element.197), channel_id=1, source_target_pairs={{0,1},{1,0},{2,3},{3,2},{4,5},{5,4},{6,7},{7,6},{8,9},{9,8},{10,11... | collective-permute-start | bytes 1572872 | tf_op jit(solution)/shard_map/ppermute | solution.py:184
  138.1 10.1 %all-to-all-start.5 = ((f32[8,6,16]{2,1,0:T(8,128)}), f32[8,6,16]{2,1,0:T(8,128)S(1)}, u32[]{:S(2)}, u32[]{:S(2)}) async-start(f32[8,6,16]{2,1,0:T(8,128)} %broadcast_in_dim.19), calls=%async_computation.7 | async-start | bytes 65536 | tf_op jit(solution)/shard_map/all_to_all | solution.py:180
  150.0 0.6 copy-start.14

commit v3 on v2

v3 whole, which is shorter than its diff:
```python
import jax
import jax.numpy as jnp
from jax import lax
from jax.experimental import pallas as pl
from jax.experimental.pallas import tpu as pltpu
from jax.sharding import Mesh
from jax.sharding import PartitionSpec as P

OBJ = 16
LEAF = 128
RANK = 64
CL_DEV = 2
NEAR_DEV = 128
FAR_DEV = 192
EPS = 1e-06

ALL = ("gx", "gy", "gq", "core")
PLANE = ("gx", "gq", "core")
TARGETS = 64
SOURCES = 128
NEAR_CHUNK = 32
FAR_CHUNK = 48
NEAR_STEP = 32
FAR_STEP = 48

SCALE_R = 2.0**15
SCALE = 2.0**4
RATIO = 1.0 / 1024.0
FLOOR = 1e-5

NEAR_TARGETS = 0
NEAR_SOURCES = NEAR_TARGETS + NEAR_DEV
FAR_TARGETS = NEAR_SOURCES + NEAR_DEV
FAR_SOURCES = FAR_TARGETS + FAR_DEV

SMEM = pl.BlockSpec(memory_space=pltpu.SMEM)
VMEM = pl.BlockSpec(memory_space=pltpu.VMEM)
HBM = pl.BlockSpec(memory_space=pltpu.HBM)


def target_row(cluster):
    return (cluster >> 7) * 16 + (cluster & 15)


def source_row(cluster, core):
    local = cluster & (SOURCES - 1)
    other = ((local >> 1) & 1) ^ core
    return other * (SOURCES // 2) + ((local >> 2) << 1) + (local & 1)


def start_blocks(near, left, right, near_v, left_v, right_v, sems):
    copies = []
    for i in range(NEAR_DEV // NEAR_CHUNK):
        near_part = pl.ds(i * NEAR_CHUNK, NEAR_CHUNK)
        far_part = pl.ds(i * FAR_CHUNK, FAR_CHUNK)
        for source, held, part in ((left, left_v, far_part), (near, near_v, near_part), (right, right_v, far_part)):
            copies.append(pltpu.make_async_copy(source.at[part], held.at[part], sems.at[len(copies)]))
    for copy in copies:
        copy.start()
    return copies


def two_terms(value):
    high = value.astype(jnp.bfloat16)
    return high, (value - high.astype(jnp.float32)).astype(jnp.bfloat16)


def multiply(rows_of, live, field, near, left, right, keep, send, x, acc, near_v, left_v, right_v, sems):
    copies = start_blocks(near, left, right, near_v, left_v, right_v, sems)
    high, low = two_terms(field[...])
    x[:, :OBJ] = high
    x[:, OBJ:] = low
    acc[...] = jnp.zeros_like(acc)
    own_half = lax.broadcasted_iota(jnp.int32, (2 * OBJ, LEAF), 0) // OBJ == (
        lax.broadcasted_iota(jnp.int32, (2 * OBJ, LEAF), 1) // RANK
    )

    def rows(base, slot, count):
        return jnp.concatenate([x[rows_of[base + slot + i]] for i in range(count)], axis=0)

    def add(parts, base, slot):
        for i, part in enumerate(parts):
            acc[rows_of[base + slot + i]] += part

    def step(index):
        near_first = index * NEAR_STEP
        far_first = index * FAR_STEP
        reduced = []
        for i in range(0, FAR_STEP, 4):
            slot = far_first + i
            lefts = left_v[pl.ds(slot, 4)].reshape(4 * RANK, LEAF)
            both = lax.dot_general(
                rows(FAR_TARGETS, slot, 4), lefts, (((1,), (1,)), ((), ())), preferred_element_type=jnp.float32
            )
            for half in (both[: 4 * OBJ, :LEAF], both[4 * OBJ :, LEAF:]):
                pair = [half[j : j + OBJ] + half[j + OBJ : j + 2 * OBJ] for j in (0, 2 * OBJ)]
                reduced += two_terms(jnp.where(own_half, jnp.concatenate(pair, axis=0), 0.0))
        near_parts = []
        for i in range(0, NEAR_STEP, 2):
            slot = near_first + i
            pair = jnp.concatenate([near_v[slot], near_v[slot + 1]], axis=1)
            both = jnp.dot(rows(NEAR_TARGETS, slot, 2), pair, preferred_element_type=jnp.float32)
            near_parts.append(both[:OBJ, :LEAF] + both[OBJ : 2 * OBJ, :LEAF])
            near_parts.append(both[2 * OBJ : 3 * OBJ, LEAF:] + both[3 * OBJ :, LEAF:])
        add(near_parts, NEAR_SOURCES, near_first)
        far_parts = []
        for i in range(0, FAR_STEP, 4):
            slot = far_first + i
            rights = jnp.concatenate(
                [
                    right_v[pl.ds(slot, 2)].reshape(2 * RANK, LEAF),
                    right_v[pl.ds(slot + 2, 2)].reshape(2 * RANK, LEAF),
                ],
                axis=1,
            )
            both = jnp.dot(
                jnp.concatenate(reduced[i : i + 4], axis=0), rights, preferred_element_type=jnp.float32
            )
            for half in (both[: 4 * OBJ, :LEAF], both[4 * OBJ :, LEAF:]):
                far_parts += [half[j : j + OBJ] + half[j + 2 * OBJ : j + 3 * OBJ] for j in (0, OBJ)]
        add(far_parts, FAR_SOURCES, far_first)

    steps = jnp.maximum((live[0] + NEAR_STEP - 1) // NEAR_STEP, (live[1] + FAR_STEP - 1) // FAR_STEP)
    per_chunk = NEAR_CHUNK // NEAR_STEP
    for chunk in range(NEAR_DEV // NEAR_CHUNK):
        for copy in copies[3 * chunk : 3 * chunk + 3]:
            copy.wait()

        def body(index, carry, first=chunk * per_chunk):
            step(first + index)
            return carry

        lax.fori_loop(0, jnp.clip(steps - chunk * per_chunk, 0, per_chunk), body, 0)
    keep[...] = acc[: SOURCES // 2]
    send[...] = acc[SOURCES // 2 : SOURCES]


def product(rows_of, live, field, blocks):
    half = jax.ShapeDtypeStruct((SOURCES // 2, OBJ, LEAF), jnp.float32)
    return pl.pallas_call(
        multiply,
        out_shape=(half, half),
        in_specs=[SMEM] * 2 + [VMEM] + [HBM] * 3,
        out_specs=(VMEM, VMEM),
        scratch_shapes=[
            pltpu.VMEM((TARGETS, 2 * OBJ, LEAF), jnp.bfloat16),
            pltpu.VMEM((SOURCES + 1, OBJ, LEAF), jnp.float32),
            pltpu.VMEM((NEAR_DEV, LEAF, LEAF), jnp.bfloat16),
            pltpu.VMEM((FAR_DEV, RANK, LEAF), jnp.bfloat16),
            pltpu.VMEM((FAR_DEV, RANK, LEAF), jnp.bfloat16),
            pltpu.SemaphoreType.DMA((3 * (NEAR_DEV // NEAR_CHUNK),)),
        ],
        compiler_params=pltpu.CompilerParams(vmem_limit_bytes=24 * 1024 * 1024),
        cost_estimate=pl.CostEstimate(flops=170_000_000, bytes_accessed=12_000_000, transcendentals=0),
    )(rows_of, live, field, *blocks)


def to_all(value, axes):
    size = lax.axis_size(axes)
    return lax.all_to_all(jnp.broadcast_to(value[None], (size,) + value.shape), axes, split_axis=0, concat_axis=0)


def scatter_sum(keep, send):
    chip = keep + lax.ppermute(send, "core", [(0, 1), (1, 0)])
    pieces = (chip * SCALE).astype(jnp.float16).reshape(-1, CL_DEV, OBJ, LEAF)
    moved = lax.all_to_all(pieces, ("gy", "gq"), split_axis=0, concat_axis=0)
    return jnp.sum(moved.astype(jnp.float32), axis=0) * (1.0 / SCALE)


def gather_targets(value, scale):
    moved = to_all((value * scale).astype(jnp.float16), PLANE)
    return moved.astype(jnp.float32).reshape(TARGETS, OBJ, LEAF) * (1.0 / scale)


def dot(first, second):
    return jnp.sum(first * second, axis=(0, 2))


def column(value):
    return value[None, :, None]


def finish(sums_ref, r_ref, u_ref, w_ref, basis_ref, entries_ref, fails_ref):
    sums = jnp.sum(sums_ref[...], axis=0)
    rr, ru, uu, rw, uw, ww = (sums[i : i + 1] for i in range(6))
    beta_sq = rr + EPS
    beta = jnp.sqrt(beta_sq)
    h11 = ru / beta_sq
    left_1 = (uu - 2.0 * h11 * ru + h11 * h11 * rr) / beta_sq
    h21 = jnp.sqrt(left_1 + EPS)
    scale = 1.0 / (beta * h21)
    g11 = rr / beta_sq
    g12 = (ru - h11 * rr) / beta_sq / h21
    g22 = left_1 / (left_1 + EPS)
    h12 = (rw - h11 * ru) / beta_sq / h21
    h22 = (uw - h11 * uu - h11 * (rw - h11 * ru)) * scale * scale
    image_sq = (ww - 2.0 * h11 * uw + h11 * h11 * uu) * scale * scale
    left_2 = image_sq - h12 * h12 * (2.0 - g11) - h22 * h22 * (2.0 - g22) + 2.0 * h12 * h22 * g12
    h32 = jnp.sqrt(left_2 + EPS)
    entries_ref[...] = jnp.concatenate([beta, h11, h21, h12, h22, h32], axis=0)
    in_w = scale / h32
    in_u = -(h11 + h22) * in_w
    in_r = (h11 * h22 * scale - h12 / beta) / h32
    own = lax.broadcasted_iota(jnp.int32, (OBJ, OBJ), 0) == lax.broadcasted_iota(jnp.int32, (OBJ, OBJ), 1)

    def down(row):
        return jnp.sum(jnp.where(own, row, 0.0), axis=1, keepdims=True)

    in_w, in_u, in_r = down(in_w), down(in_u), down(in_r)
    for i in range(CL_DEV):
        lanes = pl.ds(i * LEAF, LEAF)
        basis_ref[:, lanes] = in_w * w_ref[i] + in_u * u_ref[i] + in_r * r_ref[:, lanes]
    rest_1 = left_1 * beta_sq
    rest_2 = left_2 * beta_sq * h21 * h21
    sound = (rest_1 >= RATIO * uu) & (rest_2 >= RATIO * ww) & (rest_1 >= FLOOR) & (rest_2 >= FLOOR)
    fails_ref[0] = jnp.sum(jnp.where(sound, 0.0, 1.0)).astype(jnp.int32)


def plainly(r, indices, blocks):
    nt, ns, nc, ft, fs, fc = indices
    near, left, right = blocks
    near_alive = (jnp.arange(NEAR_DEV, dtype=jnp.int32) < nc[0]).astype(jnp.float32)
    far_alive = (jnp.arange(FAR_DEV, dtype=jnp.int32) < fc[0]).astype(jnp.float32)

    def total(first, second):
        plane = jnp.sum(to_all(dot(first, second)[None], PLANE), axis=0)
        return jnp.sum(to_all(plane, "gy"), axis=0)[0]

    def apply(vector):
        gathered = to_all(vector, PLANE).reshape(TARGETS, OBJ, LEAF).astype(jnp.bfloat16)
        partial = jnp.zeros((SOURCES, OBJ, LEAF), jnp.float32)
        picked = gathered[target_row(nt)]
        parts = jnp.einsum("bol,bls->bos", picked, near, preferred_element_type=jnp.float32)
        partial = partial.at[ns & (SOURCES - 1)].add(parts * near_alive[:, None, None])
        picked = gathered[target_row(ft)]
        reduced = jnp.einsum("bol,brl->bor", picked, left, preferred_element_type=jnp.float32).astype(jnp.bfloat16)
        parts = jnp.einsum("bor,brs->bos", reduced, right, preferred_element_type=jnp.float32)
        partial = partial.at[fs & (SOURCES - 1)].add(parts * far_alive[:, None, None])
        pieces = partial.reshape(-1, CL_DEV, OBJ, LEAF)
        moved = lax.all_to_all(pieces, ("gy", "gq", "core"), split_axis=0, concat_axis=0)
        return 0.5 * vector + jnp.sum(moved, axis=0)

    length = jnp.sqrt(total(r, r) + EPS)
    basis = [r / column(length)]
    entries = [length]
    for _ in range(2):
        image = apply(basis[-1])
        coeffs = [total(member, image) for member in basis]
        remainder = image
        for member, coeff in zip(basis, coeffs):
            remainder = remainder - column(coeff) * member
        length = jnp.sqrt(total(remainder, remainder) + EPS)
        basis.append(remainder / column(length))
        entries += coeffs + [length]
    return jnp.swapaxes(basis[-1], 0, 1).reshape(OBJ, CL_DEV * LEAF), jnp.stack(entries)


def on_device(r0, near_tiles, nt, ns, nc, far_left, far_right, ft, fs, fc):
    indices = (nt, ns, nc, ft, fs, fc)
    blocks = (near_tiles, jnp.swapaxes(far_left, 1, 2), jnp.swapaxes(far_right, 1, 2))
    r = jnp.swapaxes(r0.reshape(OBJ, CL_DEV, LEAF), 0, 1)

    core = lax.axis_index("core")
    near_live = jnp.arange(NEAR_DEV, dtype=jnp.int32) < nc[0]
    far_live = jnp.arange(FAR_DEV, dtype=jnp.int32) < fc[0]
    rows_of = jnp.concatenate(
        [
            target_row(nt),
            jnp.where(near_live, source_row(ns, core), SOURCES),
            target_row(ft),
            jnp.where(far_live, source_row(fs, core), SOURCES),
        ]
    )
    live = jnp.concatenate([nc, fc])

    u = 0.5 * r + scatter_sum(*product(rows_of, live, gather_targets(r, SCALE_R), blocks))
    w = 0.5 * u + scatter_sum(*product(rows_of, live, gather_targets(u, SCALE), blocks))
    local = jnp.stack([dot(r, r), dot(r, u), dot(u, u), dot(r, w), dot(u, w), dot(w, w)])
    sums = to_all(jnp.sum(to_all(local, PLANE), axis=0), "gy")
    basis_3, entries, fails = pl.pallas_call(
        finish,
        out_shape=(
            jax.ShapeDtypeStruct((OBJ, CL_DEV * LEAF), jnp.float32),
            jax.ShapeDtypeStruct((6, OBJ), jnp.float32),
            jax.ShapeDtypeStruct((1,), jnp.int32),
        ),
        in_specs=[VMEM] * 4,
        out_specs=(VMEM, VMEM, SMEM),
    )(sums, r0, u, w)
    basis_3, entries = lax.cond(
        fails[0] == 0, lambda: (basis_3, entries), lambda: plainly(r, indices, blocks)
    )
    return basis_3, entries.T


def solution(mesh):
    fine = Mesh(mesh.devices.reshape(4, 8, 4, 2), ALL)
    spread = P(ALL)
    return jax.shard_map(
        on_device,
        mesh=fine,
        in_specs=(P(None, ALL),) + (spread,) * 9,
        out_specs=(P(None, ALL), P()),
        check_vma=False,
    )
```

time: 159 us -> 115 us (0.72)
  blocking collectives: 77.5 us -> 63.6 us
  between operations: 16.1 us -> 2.85 us
  local copies, waits for them, and re-layouts: 12.4 us -> 2.67 us
  waiting for transfers between devices: 20.8 us -> 15.9 us
  Pallas kernels: 14.9 us -> 11.2 us
  starting transfers between devices: 12.2 us -> 14.5 us
    all_to_all x2, blocking collectives: 46.4 us -> 36.6 us  [scatter_sum(): moved = lax.all_to_all(pieces, ('gy', 'gq'), split_axis=0, concat_axis=0)]
    unnamed x26 -> x24, local copies, waits for them, and re-layouts: 10.2 us -> 1.25 us
    all_to_all x2, waiting for transfers between devices: 17.1 us -> 12.8 us  [to_all(): lax.all_to_all(jnp.broadcast_to(value[None], (size,) + value.shape), axes...]
    all_to_all x2, blocking collectives: 31.1 us -> 27.1 us  [to_all(): lax.all_to_all(jnp.broadcast_to(value[None], (size,) + value.shape), axes...]
    pallas_call x2 -> x3, Pallas kernels: 14.9 us -> 11.2 us  [the longest x2 9.7 us: product(): pl.pallas_call(multiply, out_shape=(half, half), in_specs=[SMEM] * 2 + [V...]
    ppermute x2, starting transfers between devices: 0.25 us -> 2.57 us  [scatter_sum(): chip = keep + lax.ppermute(send, 'core', [(0, 1), (1, 0)])]
    reduce_sum x4 -> x3, other arithmetic: 2.23 us -> 0.14 us  [the longest x2 0.1 us: scatter_sum(): return jnp.sum(moved.astype(jnp.float32), axis=0) * (1.0 / SCALE)]
  transfers between devices with their start and end apart: 4 -> 4, of which waited for: 4 -> 4; matrix products, arithmetic and copies ran while one was open for 0% -> 1% of each run, Pallas kernels for 0% -> 0%
where the time goes in v3:
time: 115 us; the launch traced here: 114 us
  blocking collectives  63.6 us (55%)
  waiting for transfers between devices  15.9 us (14%)
  starting transfers between devices  14.5 us (13%)
  Pallas kernels  11.2 us (10%)
  other arithmetic  3.47 us (3%)
  between operations  2.85 us (2%)
  local copies, waits for them, and re-layouts  2.67 us (2%)
    all_to_all x2, blocking collectives, scatter_sum(): moved = lax.all_to_all(pieces, ('gy', 'gq'), split_axis=0, concat_axis=0)  36.6 us
    all_to_all x2, blocking collectives, to_all(): lax.all_to_all(jnp.broadcast_to(value[None], (size,) + value.shape), axes...  27.1 us
    all_to_all x2, waiting for transfers between devices, to_all(): lax.all_to_all(jnp.broadcast_to(value[None], (size,) + value.shape), axes...  12.8 us
    all_to_all x2, starting transfers between devices, to_all(): lax.all_to_all(jnp.broadcast_to(value[None], (size,) + value.shape), axes...  11.9 us
    pallas_call x2, Pallas kernels, product(): pl.pallas_call(multiply, out_shape=(half, half), in_specs=[SMEM] * 2 + [V...  9.7 us
    ppermute x2, waiting for transfers between devices, scatter_sum(): chip = keep + lax.ppermute(send, 'core', [(0, 1), (1, 0)])  3.07 us
    ppermute x2, starting transfers between devices, scatter_sum(): chip = keep + lax.ppermute(send, 'core', [(0, 1), (1, 0)])  2.57 us
  transfers between devices with their start and end apart: 4, of which 4 were waited for; matrix products, arithmetic and copies ran while one was open for 1% of the time, Pallas kernels for 0%

profile of v3, /device:TPU:1, one launch (start us, length us, event | category | flops | bytes accessed | tf_op | source)
XLA Modules:
  0.0 114.5 jit_solution(17353282598227674604)
XLA Ops:
  0.6 0.7 multiply_convert_fusion.3
  1.4 0.7 broadcast_in_dim.54
  2.1 8.6 %all-to-all-start.16 = ((f16[32,2,16,128]{3,2,1,0:T(8,128)(2,1)}), f16[32,2,16,128]{3,2,1,0:T(8,128)(2,1)S(1)}, u32[]{:S(2)}, u32[]{:S(2)}) async-start(f16[32,2,16,128]{3,2,1,0:T(8,128)(2,1)} %broadcast_in_dim.54), calls=%async_computation.16 | async-start | bytes 524288 | tf_op jit(solution)/shard_map/all_to_all | solution.py:160
  12.0 0.7 compare_select_fusion.4
  12.7 0.7 compare_select_fusion.5
  13.4 0.1 pad_add_fusion.1.live
  13.4 0.1 pad_add_fusion.rows_of
  13.5 6.1 %all-to-all-done.16 = f16[32,2,16,128]{3,2,1,0:T(8,128)(2,1)S(1)} async-done(((f16[32,2,16,128]{3,2,1,0:T(8,128)(2,1)}), f16[32,2,16,128]{3,2,1,0:T(8,128)(2,1)S(1)}, u32[]{:S(2)}, u32[]{:S(2)}) %all-to-all-start.16) | async-done | bytes 262176 | tf_op jit(solution)/shard_map/all_to_all | solution.py:160
  19.6 0.1 convert_multiply_fusion.1
  19.6 0.0 copy-start.4
  19.7 0.0 copy-start.2
  19.7 5.4 %shard_map.113 = (f32[64,16,128]{2,1,0:T(8,128)S(1)}, f32[64,16,128]{2,1,0:T(8,128)S(1)}) custom-call(s32[640]{0:T(1024)S(1)} %pad_add_fusion.rows_of, s32[2]{0:T(128)S(1)} %pad_add_fusion.1.live, f32[64,16,128]{2,1,0:T(8,128)S(1)} %bitcast.91, bf16[128,128,128]{2,1,0:T(8,128)(2,1)} %near.3, bf16[192,64,128]{2,1,0:T(8,128)(2,1)} %bitcast.92, ...), custom_call_target="tpu_custom_call" | custom-call | flops 170000000 | bytes 12000000 | tf_op jit(solution)/shard_map/pallas_call | solution.py:140
  25.1 1.3 %collective-permute-start = (f32[64,16,128]{2,1,0:T(8,128)S(1)}, f32[64,16,128]{2,1,0:T(8,128)S(1)}, u32[]{:S(2)}, u32[]{:S(2)}) collective-permute-start(f32[64,16,128]{2,1,0:T(8,128)S(1)} %get-tuple-element.46), channel_id=1, source_target_pairs={{0,1},{1,0},{2,3},{3,2},{4,5},{5,4},{6,7},{7,6},{8,9},{9,8},{10,11... | collective-permute-start | bytes 1572872 | tf_op jit(solution)/shard_map/ppermute | solution.py:164
  26.4 1.5 %collective-permute-done = f32[64,16,128]{2,1,0:T(8,128)S(1)} collective-permute-done((f32[64,16,128]{2,1,0:T(8,128)S(1)}, f32[64,16,128]{2,1,0:T(8,128)S(1)}, u32[]{:S(2)}, u32[]{:S(2)}) %collective-permute-start) | collective-permute-done | bytes 524320 | tf_op jit(solution)/shard_map/ppermute | solution.py:164
  27.9 0.1 multiply_convert_fusion.1
  28.0 21.3 %all_to_all.96 = f16[32,2,16,128]{3,2,1,0:T(8,128)(2,1)S(1)} all-to-all(f16[32,2,16,128]{3,2,1,0:T(8,128)(2,1)S(1)} %bitcast.104), channel_id=1, replica_groups=mesh['gx'=4,'gy'=8,'gq'=4,'core'=2] {'gy','gq'}, dimensions={0} | all-to-all | bytes 524288 | tf_op jit(solution)/shard_map/all_to_all | solution.py:166
  49.4 14.1 %all_to_all.97 = f16[32,2,16,128]{3,2,1,0:T(8,128)(2,1)S(1)} all-to-all(f16[32,2,16,128]{3,2,1,0:T(8,128)(2,1)S(1)} %broadcast_in_dim.55), channel_id=1, replica_groups=mesh['gx'=4,'gy'=8,'gq'=4,'core'=2] {'gx','gq','core'}, dimensions={0} | all-to-all | bytes 524288 | tf_op jit(solution)/shard_map/all_to_all | solution.py:160
  63.6 0.1 convert_multiply_fusion
  63.7 4.3 %shard_map.114 = (f32[64,16,128]{2,1,0:T(8,128)S(1)}, f32[64,16,128]{2,1,0:T(8,128)S(1)}) custom-call(s32[640]{0:T(1024)S(1)} %pad_add_fusion.rows_of, s32[2]{0:T(128)S(1)} %pad_add_fusion.1.live, f32[64,16,128]{2,1,0:T(8,128)S(1)} %bitcast.90, bf16[128,128,128]{2,1,0:T(8,128)(2,1)S(1)} %copy-done, bf16[192,64,128]{2,1,0:T(8,128)(2,1)S(1)} %bitcast.93, ...), custom_call_target="tpu_custom_call" | custom-call | flops 170000000 | bytes 12000000 | tf_op jit(solution)/shard_map/pallas_call | solution.py:140
  68.0 1.3 %collective-permute-start.1 = (f32[64,16,128]{2,1,0:T(8,128)S(1)}, f32[64,16,128]{2,1,0:T(8,128)S(1)}, u32[]{:S(2)}, u32[]{:S(2)}) collective-permute-start(f32[64,16,128]{2,1,0:T(8,128)S(1)} %get-tuple-element.48), channel_id=1, source_target_pairs={{0,1},{1,0},{2,3},{3,2},{4,5},{5,4},{6,7},{7,6},{8,9},{9,8},{10,11... | collective-permute-start | bytes 1572872 | tf_op jit(solution)/shard_map/ppermute | solution.py:164
  69.3 1.5 %collective-permute-done.1 = f32[64,16,128]{2,1,0:T(8,128)S(1)} collective-permute-done((f32[64,16,128]{2,1,0:T(8,128)S(1)}, f32[64,16,128]{2,1,0:T(8,128)S(1)}, u32[]{:S(2)}, u32[]{:S(2)}) %collective-permute-start.1) | collective-permute-done | bytes 524320 | tf_op jit(solution)/shard_map/ppermute | solution.py:164
  70.9 0.1 multiply_convert_fusion
  70.9 15.3 %all_to_all.98 = f16[32,2,16,128]{3,2,1,0:T(8,128)(2,1)S(1)} all-to-all(f16[32,2,16,128]{3,2,1,0:T(8,128)(2,1)S(1)} %bitcast.105), channel_id=1, replica_groups=mesh['gx'=4,'gy'=8,'gq'=4,'core'=2] {'gy','gq'}, dimensions={0} | all-to-all | bytes 524288 | tf_op jit(solution)/shard_map/all_to_all | solution.py:166
  86.3 0.8 multiply_reduce_fusion.6
  87.1 12.9 %all_to_all.99 = f32[32,6,16]{2,1,0:T(8,128)S(1)} all-to-all(f32[32,6,16]{2,1,0:T(8,128)S(1)} %broadcast_in_dim.56), channel_id=1, replica_groups=mesh['gx'=4,'gy'=8,'gq'=4,'core'=2] {'gx','gq','core'}, dimensions={0} | all-to-all | bytes 24576 | tf_op jit(solution)/shard_map/all_to_all | solution.py:160
  100.1 0.6 broadcast_in_dim.57
  100.7 3.3 %all-to-all-start.21 = ((f32[8,6,16]{2,1,0:T(8,128)}), f32[8,6,16]{2,1,0:T(8,128)S(1)}, u32[]{:S(2)}, u32[]{:S(2)}) async-start(f32[8,6,16]{2,1,0:T(8,128)} %broadcast_in_dim.57), calls=%async_computation.21 | async-start | bytes 65536 | tf_op jit(solution)/shard_map/all_to_all | solution.py:160
  104.1 6.8 %all-to-all-done.21.sums_ref = f32[8,6,16]{2,1,0:T(8,128)S(1)} async-done(((f32[8,6,16]{2,1,0:T(8,128)}), f32[8,6,16]{2,1,0:T(8,128)S(1)}, u32[]{:S(2)}, u32[]{:S(2)}) %all-to-all-start.21) | async-done | bytes 3104 | tf_op jit(solution)/shard_map/all_to_all | solution.py:160
  110.8 0.6 copy-done.6
  111.4 1.5 %shard_map.115 = (f32[16,256]{1,0:T(8,128)S(1)}, f32[6,16]{1,0:T(8,128)S(1)}, s32[1]{0:T(128)}) custom-call(f32[8,6,16]{2,1,0:T(8,128)} %copy-done.6, f32[16,256]{1,0:T(8,128)} %r_ref.1, f32[2,16,128]{2,1,0:T(8,128)} %copy-done.5, f32[2,16,128]{2,1,0:T(8,128)} %get-tuple-element.64.w_ref), custom_call_target="tpu_custom_call" | custom-call | tf_op jit(solution)/shard_map/pallas_call | solution.py:280
  113.6 0.2 conditional.1
  113.9 0.6 copy-done.11
  (28 shorter events, 0.3 us)
Async XLA Ops:
  2.1 17.5 %all-to-all-start.16 = ((f16[32,2,16,128]{3,2,1,0:T(8,128)(2,1)}), f16[32,2,16,128]{3,2,1,0:T(8,128)(2,1)S(1)}, u32[]{:S(2)}, u32[]{:S(2)}) async-start(f16[32,2,16,128]{3,2,1,0:T(8,128)(2,1)} %broadcast_in_dim.54), calls=%async_computation.16 | async-start | bytes 524288 | tf_op jit(solution)/shard_map/all_to_all | solution.py:160
  19.6 29.7 %copy-start.4 = (f32[16,256]{1,0:T(8,128)S(1)}, f32[16,256]{1,0:T(8,128)}, u32[]{:S(2)}) copy-start(f32[16,256]{1,0:T(8,128)} %r_ref.1) | copy-start | bytes 49156
  19.7 44.0 %copy-start = (bf16[128,128,128]{2,1,0:T(8,128)(2,1)S(1)}, bf16[128,128,128]{2,1,0:T(8,128)(2,1)}, u32[]{:S(2)}) copy-start(bf16[128,128,128]{2,1,0:T(8,128)(2,1)} %near.3) | copy-start | bytes 12582916
  19.7 44.0 %copy-start.2 = (bf16[192,128,64]{1,2,0:T(8,128)(2,1)S(1)}, bf16[192,128,64]{1,2,0:T(8,128)(2,1)}, u32[]{:S(2)}) copy-start(bf16[192,128,64]{1,2,0:T(8,128)(2,1)} %param.18) | copy-start | bytes 9437188
  25.1 38.6 %copy-start.1 = (bf16[192,128,64]{1,2,0:T(8,128)(2,1)S(1)}, bf16[192,128,64]{1,2,0:T(8,128)(2,1)}, u32[]{:S(2)}) copy-start(bf16[192,128,64]{1,2,0:T(8,128)(2,1)} %param.17) | copy-start | bytes 9437188
  25.1 2.8 %collective-permute-start = (f32[64,16,128]{2,1,0:T(8,128)S(1)}, f32[64,16,128]{2,1,0:T(8,128)S(1)}, u32[]{:S(2)}, u32[]{:S(2)}) collective-permute-start(f32[64,16,128]{2,1,0:T(8,128)S(1)} %get-tuple-element.46), channel_id=1, source_target_pairs={{0,1},{1,0},{2,3},{3,2},{4,5},{5,4},{6,7},{7,6},{8,9},{9,8},{10,11... | collective-permute-start | bytes 1572872 | tf_op jit(solution)/shard_map/ppermute | solution.py:164
  49.4 36.9 %copy-start.5 = (f32[2,16,128]{2,1,0:T(8,128)}, f32[2,16,128]{2,1,0:T(8,128)S(1)}, u32[]{:S(2)}) copy-start(f32[2,16,128]{2,1,0:T(8,128)S(1)} %get-tuple-element.66.u_ref) | copy-start | bytes 49156
  63.7 49.9 %copy-start.7 = (s32[192]{0:T(256)S(1)}, s32[192]{0:T(256)}, u32[]{:S(2)}) copy-start(s32[192]{0:T(256)} %param.20) | copy-start | bytes 2308
  63.7 49.9 %copy-start.8 = (s32[192]{0:T(256)S(1)}, s32[192]{0:T(256)}, u32[]{:S(2)}) copy-start(s32[192]{0:T(256)} %param.19) | copy-start | bytes 2308
  63.7 49.9 %copy-start.9 = (s32[128]{0:T(128)S(1)}, s32[128]{0:T(128)}, u32[]{:S(2)}) copy-start(s32[128]{0:T(128)} %param.15) | copy-start | bytes 1540
  63.7 49.9 %copy-start.10 = (s32[128]{0:T(128)S(1)}, s32[128]{0:T(128)}, u32[]{:S(2)}) copy-start(s32[128]{0:T(128)} %param.14) | copy-start | bytes 1540
  68.0 2.8 %collective-permute-start.1 = (f32[64,16,128]{2,1,0:T(8,128)S(1)}, f32[64,16,128]{2,1,0:T(8,128)S(1)}, u32[]{:S(2)}, u32[]{:S(2)}) collective-permute-start(f32[64,16,128]{2,1,0:T(8,128)S(1)} %get-tuple-element.48), channel_id=1, source_target_pairs={{0,1},{1,0},{2,3},{3,2},{4,5},{5,4},{6,7},{7,6},{8,9},{9,8},{10,11... | collective-permute-start | bytes 1572872 | tf_op jit(solution)/shard_map/ppermute | solution.py:164
  100.7 10.1 %all-to-all-start.21 = ((f32[8,6,16]{2,1,0:T(8,128)}), f32[8,6,16]{2,1,0:T(8,128)S(1)}, u32[]{:S(2)}, u32[]{:S(2)}) async-start(f32[8,6,16]{2,1,0:T(8,128)} %broadcast_in_dim.57), calls=%async_computation.21 | async-start | bytes 65536 | tf_op jit(solution)/shard_map/all_to_all | solution.py:160
  110.8 0.6 copy-start.6
  113.8 0.6 copy-start.11
  113.9 0.6 copy-start.12

commit v4 on v3

--- a/solution.py
+++ b/solution.py
@@ -28,11 +28,6 @@
 RATIO = 1.0 / 1024.0
 FLOOR = 1e-5
 
-NEAR_TARGETS = 0
-NEAR_SOURCES = NEAR_TARGETS + NEAR_DEV
-FAR_TARGETS = NEAR_SOURCES + NEAR_DEV
-FAR_SOURCES = FAR_TARGETS + FAR_DEV
-
 SMEM = pl.BlockSpec(memory_space=pltpu.SMEM)
 VMEM = pl.BlockSpec(memory_space=pltpu.VMEM)
 HBM = pl.BlockSpec(memory_space=pltpu.HBM)
@@ -40,12 +35,6 @@
 
 def target_row(cluster):
     return (cluster >> 7) * 16 + (cluster & 15)
-
-
-def source_row(cluster, core):
-    local = cluster & (SOURCES - 1)
-    other = ((local >> 1) & 1) ^ core
-    return other * (SOURCES // 2) + ((local >> 2) << 1) + (local & 1)
 
 
 def start_blocks(near, left, right, near_v, left_v, right_v, sems):
@@ -65,22 +54,42 @@
     return high, (value - high.astype(jnp.float32)).astype(jnp.bfloat16)
 
 
-def multiply(rows_of, live, field, near, left, right, keep, send, x, acc, near_v, left_v, right_v, sems):
+def multiply(
+    nt, ns, ft, fs, nc, fc, field, near, left, right, keep, send,
+    x, acc, near_v, left_v, right_v, sems, nt_s, ns_s, ft_s, fs_s, nc_s, fc_s, index_sems,
+):
+    fetches = [
+        pltpu.make_async_copy(source, held, index_sems.at[i])
+        for i, (source, held) in enumerate(
+            ((nt, nt_s), (ns, ns_s), (ft, ft_s), (fs, fs_s), (nc, nc_s), (fc, fc_s))
+        )
+    ]
+    for fetch in fetches:
+        fetch.start()
     copies = start_blocks(near, left, right, near_v, left_v, right_v, sems)
     high, low = two_terms(field[...])
-    x[:, :OBJ] = high
-    x[:, OBJ:] = low
+    x[:TARGETS, :OBJ] = high
+    x[:TARGETS, OBJ:] = low
+    x[TARGETS] = jnp.zeros((2 * OBJ, LEAF), jnp.bfloat16)
     acc[...] = jnp.zeros_like(acc)
     own_half = lax.broadcasted_iota(jnp.int32, (2 * OBJ, LEAF), 0) // OBJ == (
         lax.broadcasted_iota(jnp.int32, (2 * OBJ, LEAF), 1) // RANK
     )
 
-    def rows(base, slot, count):
-        return jnp.concatenate([x[rows_of[base + slot + i]] for i in range(count)], axis=0)
-
-    def add(parts, base, slot):
+    for fetch in fetches:
+        fetch.wait()
+    near_live = nc_s[0]
+    far_live = fc_s[0]
+
+    def rows(targets, live, slot, count):
+        picked = [
+            x[jnp.where(slot + i < live, target_row(targets[slot + i]), TARGETS)] for i in range(count)
+        ]
+        return jnp.concatenate(picked, axis=0)
+
+    def add(parts, sources, slot):
         for i, part in enumerate(parts):
-            acc[rows_of[base + slot + i]] += part
+            acc[sources[slot + i] & (SOURCES - 1)] += part
 
     def step(index):
         near_first = index * NEAR_STEP
@@ -90,7 +99,7 @@
             slot = far_first + i
             lefts = left_v[pl.ds(slot, 4)].reshape(4 * RANK, LEAF)
             both = lax.dot_general(
-                rows(FAR_TARGETS, slot, 4), lefts, (((1,), (1,)), ((), ())), preferred_element_type=jnp.float32
+                rows(ft_s, far_live, slot, 4), lefts, (((1,), (1,)), ((), ())), preferred_element_type=jnp.float32
             )
             for half in (both[: 4 * OBJ, :LEAF], both[4 * OBJ :, LEAF:]):
                 pair = [half[j : j + OBJ] + half[j + OBJ : j + 2 * OBJ] for j in (0, 2 * OBJ)]
@@ -99,10 +108,10 @@
         for i in range(0, NEAR_STEP, 2):
             slot = near_first + i
             pair = jnp.concatenate([near_v[slot], near_v[slot + 1]], axis=1)
-            both = jnp.dot(rows(NEAR_TARGETS, slot, 2), pair, preferred_element_type=jnp.float32)
+            both = jnp.dot(rows(nt_s, near_live, slot, 2), pair, preferred_element_type=jnp.float32)
             near_parts.append(both[:OBJ, :LEAF] + both[OBJ : 2 * OBJ, :LEAF])
             near_parts.append(both[2 * OBJ : 3 * OBJ, LEAF:] + both[3 * OBJ :, LEAF:])
-        add(near_parts, NEAR_SOURCES, near_first)
+        add(near_parts, ns_s, near_first)
         far_parts = []
         for i in range(0, FAR_STEP, 4):
             slot = far_first + i
@@ -118,9 +127,9 @@
             )
             for half in (both[: 4 * OBJ, :LEAF], both[4 * OBJ :, LEAF:]):
                 far_parts += [half[j : j + OBJ] + half[j + 2 * OBJ : j + 3 * OBJ] for j in (0, OBJ)]
-        add(far_parts, FAR_SOURCES, far_first)
-
-    steps = jnp.maximum((live[0] + NEAR_STEP - 1) // NEAR_STEP, (live[1] + FAR_STEP - 1) // FAR_STEP)
+        add(far_parts, fs_s, far_first)
+
+    steps = jnp.maximum((near_live + NEAR_STEP - 1) // NEAR_STEP, (far_live + FAR_STEP - 1) // FAR_STEP)
     per_chunk = NEAR_CHUNK // NEAR_STEP
     for chunk in range(NEAR_DEV // NEAR_CHUNK):
         for copy in copies[3 * chunk : 3 * chunk + 3]:
@@ -131,28 +140,37 @@
             return carry
 
         lax.fori_loop(0, jnp.clip(steps - chunk * per_chunk, 0, per_chunk), body, 0)
-    keep[...] = acc[: SOURCES // 2]
-    send[...] = acc[SOURCES // 2 : SOURCES]
-
-
-def product(rows_of, live, field, blocks):
+    core = lax.axis_index("core")
+    by_core = acc.reshape(SOURCES // 4, 4, OBJ, LEAF)
+    keep[...] = by_core[:, pl.ds(2 * core, 2)].reshape(keep.shape)
+    send[...] = by_core[:, pl.ds(2 - 2 * core, 2)].reshape(send.shape)
+
+
+def product(lists, field, blocks):
     half = jax.ShapeDtypeStruct((SOURCES // 2, OBJ, LEAF), jnp.float32)
     return pl.pallas_call(
         multiply,
         out_shape=(half, half),
-        in_specs=[SMEM] * 2 + [VMEM] + [HBM] * 3,
+        in_specs=[HBM] * 6 + [VMEM] + [HBM] * 3,
         out_specs=(VMEM, VMEM),
         scratch_shapes=[
-            pltpu.VMEM((TARGETS, 2 * OBJ, LEAF), jnp.bfloat16),
-            pltpu.VMEM((SOURCES + 1, OBJ, LEAF), jnp.float32),
+            pltpu.VMEM((TARGETS + 1, 2 * OBJ, LEAF), jnp.bfloat16),
+            pltpu.VMEM((SOURCES, OBJ, LEAF), jnp.float32),
             pltpu.VMEM((NEAR_DEV, LEAF, LEAF), jnp.bfloat16),
             pltpu.VMEM((FAR_DEV, RANK, LEAF), jnp.bfloat16),
             pltpu.VMEM((FAR_DEV, RANK, LEAF), jnp.bfloat16),
             pltpu.SemaphoreType.DMA((3 * (NEAR_DEV // NEAR_CHUNK),)),
+            pltpu.SMEM((NEAR_DEV,), jnp.int32),
+            pltpu.SMEM((NEAR_DEV,), jnp.int32),
+            pltpu.SMEM((FAR_DEV,), jnp.int32),
+            pltpu.SMEM((FAR_DEV,), jnp.int32),
+            pltpu.SMEM((1,), jnp.int32),
+            pltpu.SMEM((1,), jnp.int32),
+            pltpu.SemaphoreType.DMA((6,)),
         ],
         compiler_params=pltpu.CompilerParams(vmem_limit_bytes=24 * 1024 * 1024),
         cost_estimate=pl.CostEstimate(flops=170_000_000, bytes_accessed=12_000_000, transcendentals=0),
-    )(rows_of, live, field, *blocks)
+    )(*lists, field, *blocks)
 
 
 def to_all(value, axes):
@@ -161,8 +179,8 @@
 
 
 def scatter_sum(keep, send):
-    chip = keep + lax.ppermute(send, "core", [(0, 1), (1, 0)])
-    pieces = (chip * SCALE).astype(jnp.float16).reshape(-1, CL_DEV, OBJ, LEAF)
+    other = lax.ppermute((send * SCALE).astype(jnp.float16), "core", [(0, 1), (1, 0)])
+    pieces = (keep * SCALE + other.astype(jnp.float32)).astype(jnp.float16).reshape(-1, CL_DEV, OBJ, LEAF)
     moved = lax.all_to_all(pieces, ("gy", "gq"), split_axis=0, concat_axis=0)
     return jnp.sum(moved.astype(jnp.float32), axis=0) * (1.0 / SCALE)
 
@@ -181,7 +199,7 @@
 
 
 def finish(sums_ref, r_ref, u_ref, w_ref, basis_ref, entries_ref, fails_ref):
-    sums = jnp.sum(sums_ref[...], axis=0)
+    sums = sums_ref[...]
     rr, ru, uu, rw, uw, ww = (sums[i : i + 1] for i in range(6))
     beta_sq = rr + EPS
     beta = jnp.sqrt(beta_sq)
@@ -216,7 +234,8 @@
     fails_ref[0] = jnp.sum(jnp.where(sound, 0.0, 1.0)).astype(jnp.int32)
 
 
-def plainly(r, indices, blocks):
+def plainly(r0, indices, blocks):
+    r = jnp.swapaxes(r0.reshape(OBJ, CL_DEV, LEAF), 0, 1)
     nt, ns, nc, ft, fs, fc = indices
     near, left, right = blocks
     near_alive = (jnp.arange(NEAR_DEV, dtype=jnp.int32) < nc[0]).astype(jnp.float32)
@@ -260,23 +279,13 @@
     blocks = (near_tiles, jnp.swapaxes(far_left, 1, 2), jnp.swapaxes(far_right, 1, 2))
     r = jnp.swapaxes(r0.reshape(OBJ, CL_DEV, LEAF), 0, 1)
 
-    core = lax.axis_index("core")
-    near_live = jnp.arange(NEAR_DEV, dtype=jnp.int32) < nc[0]
-    far_live = jnp.arange(FAR_DEV, dtype=jnp.int32) < fc[0]
-    rows_of = jnp.concatenate(
-        [
-            target_row(nt),
-            jnp.where(near_live, source_row(ns, core), SOURCES),
-            target_row(ft),
-            jnp.where(far_live, source_row(fs, core), SOURCES),
-        ]
-    )
-    live = jnp.concatenate([nc, fc])
-
-    u = 0.5 * r + scatter_sum(*product(rows_of, live, gather_targets(r, SCALE_R), blocks))
-    w = 0.5 * u + scatter_sum(*product(rows_of, live, gather_targets(u, SCALE), blocks))
+    lists = (nt, ns, ft, fs, nc, fc)
+    u = 0.5 * r + scatter_sum(*product(lists, gather_targets(r, SCALE_R), blocks))
+    w = 0.5 * u + scatter_sum(*product(lists, gather_targets(u, SCALE), blocks))
     local = jnp.stack([dot(r, r), dot(r, u), dot(u, u), dot(r, w), dot(u, w), dot(w, w)])
-    sums = to_all(jnp.sum(to_all(local, PLANE), axis=0), "gy")
+    sums = jnp.sum(to_all(local, PLANE), axis=0)
+    for distance in (1, 2, 4):
+        sums += lax.ppermute(sums, "gy", [(i, i ^ distance) for i in range(8)])
     basis_3, entries, fails = pl.pallas_call(
         finish,
         out_shape=(
@@ -286,9 +295,10 @@
         ),
         in_specs=[VMEM] * 4,
         out_specs=(VMEM, VMEM, SMEM),
+        compiler_params=pltpu.CompilerParams(vmem_limit_bytes=2 * 1024 * 1024),
     )(sums, r0, u, w)
     basis_3, entries = lax.cond(
-        fails[0] == 0, lambda: (basis_3, entries), lambda: plainly(r, indices, blocks)
+        fails[0] == 0, lambda: (basis_3, entries), lambda: plainly(r0, indices, blocks)
     )
     return basis_3, entries.T
 

time: 115 us -> 114 us (level); the launches traced: 114 us -> 112 us
  waiting for transfers between devices: 15.9 us -> 21.3 us
  starting transfers between devices: 14.5 us -> 10.6 us
  other arithmetic: 3.47 us -> 1.5 us
  local copies, waits for them, and re-layouts: 2.67 us -> 1.45 us
    ppermute x2 -> x5, waiting for transfers between devices: 3.07 us -> 13.6 us  [the longest x3 10.6 us: on_device(): sums += lax.ppermute(sums, 'gy', [(i, i ^ distance) for i in range(8)])]
    all_to_all x2 -> x1, waiting for transfers between devices: 12.8 us -> 7.61 us  [to_all(): lax.all_to_all(jnp.broadcast_to(value[None], (size,) + value.shape), axes...]
    all_to_all x2 -> x1, starting transfers between devices: 11.9 us -> 8.59 us  [to_all(): lax.all_to_all(jnp.broadcast_to(value[None], (size,) + value.shape), axes...]
    select_n x2 -> x0, other arithmetic: 1.39 us -> none  [the longest x1 0.71 us: on_device(): jnp.where(far_live, source_row(fs, core), SOURCES)]
    ppermute x2 -> x5, starting transfers between devices: 2.57 us -> 2.03 us  [the longest x3 1.85 us: on_device(): sums += lax.ppermute(sums, 'gy', [(i, i ^ distance) for i in range(8)])]
  transfers between devices with their start and end apart: 4 -> 6, of which waited for: 4 -> 6; matrix products, arithmetic and copies ran while one was open for 1% -> 0% of each run, Pallas kernels for 0% -> 0%
where the time goes in v4:
time: 114 us; the launch traced here: 112 us
  blocking collectives  63.6 us (56%)
  waiting for transfers between devices  21.3 us (19%)
  Pallas kernels  10.8 us (9%)
  starting transfers between devices  10.6 us (9%)
  between operations  2.84 us (2%)
  other arithmetic  1.5 us (1%)
  local copies, waits for them, and re-layouts  1.45 us (1%)
    all_to_all x2, blocking collectives, scatter_sum(): moved = lax.all_to_all(pieces, ('gy', 'gq'), split_axis=0, concat_axis=0)  36.1 us
    all_to_all x2, blocking collectives, to_all(): lax.all_to_all(jnp.broadcast_to(value[None], (size,) + value.shape), axes...  27.5 us
    ppermute x3, waiting for transfers between devices, on_device(): sums += lax.ppermute(sums, 'gy', [(i, i ^ distance) for i in range(8)])  10.6 us
    pallas_call x2, Pallas kernels, product(): pl.pallas_call(multiply, out_shape=(half, half), in_specs=[HBM] * 6 + [VM...  10.1 us
    all_to_all x1, starting transfers between devices, to_all(): lax.all_to_all(jnp.broadcast_to(value[None], (size,) + value.shape), axes...  8.59 us
    all_to_all x1, waiting for transfers between devices, to_all(): lax.all_to_all(jnp.broadcast_to(value[None], (size,) + value.shape), axes...  7.61 us
    ppermute x2, waiting for transfers between devices, scatter_sum(): lax.ppermute((send * SCALE).astype(jnp.float16), 'core', [(0, 1), (1, 0)])  3.04 us
  transfers between devices with their start and end apart: 6, of which 6 were waited for; matrix products, arithmetic and copies ran while one was open for 0% of the time, Pallas kernels for 0%

profile of v4, /device:TPU:1, one launch (start us, length us, event | category | flops | bytes accessed | tf_op | source)
XLA Modules:
  0.0 112.1 jit_solution(10019051926088415854)
XLA Ops:
  0.6 0.7 fusion.17
  1.4 0.7 broadcast_in_dim.42
  2.1 8.6 %all-to-all-start.16 = ((f16[32,2,16,128]{3,2,1,0:T(8,128)(2,1)}), f16[32,2,16,128]{3,2,1,0:T(8,128)(2,1)S(1)}, u32[]{:S(2)}, u32[]{:S(2)}) async-start(f16[32,2,16,128]{3,2,1,0:T(8,128)(2,1)} %broadcast_in_dim.42), calls=%async_computation.16 | async-start | bytes 524288 | tf_op jit(solution)/shard_map/all_to_all | solution.py:178
  12.0 7.6 %all-to-all-done.16 = f16[32,2,16,128]{3,2,1,0:T(8,128)(2,1)S(1)} async-done(((f16[32,2,16,128]{3,2,1,0:T(8,128)(2,1)}), f16[32,2,16,128]{3,2,1,0:T(8,128)(2,1)S(1)}, u32[]{:S(2)}, u32[]{:S(2)}) %all-to-all-start.16) | async-done | bytes 262176 | tf_op jit(solution)/shard_map/all_to_all | solution.py:178
  19.6 0.1 convert_multiply_fusion.1
  19.7 0.0 copy-start.2
  19.7 5.5 %shard_map.113 = (f32[64,16,128]{2,1,0:T(8,128)S(1)}, f32[64,16,128]{2,1,0:T(8,128)S(1)}) custom-call(s32[128]{0:T(128)} %nt.3, s32[128]{0:T(128)} %ns.3, s32[192]{0:T(256)} %ft.3, s32[192]{0:T(256)} %fs.3, s32[1]{0:T(128)S(6)} %copy.92.nc, s32[1]{0:T(128)S(6)} %copy.93.fc, f32[64,16,128]{2,1,0:T(8,128)S(1)} %bitcast.169, bf16[128,128,128]{2,1,0:T(8,128)(2,1)} %near.3, ...), custom_call_target="tpu_custom_call" | custom-call | flops 170000000 | bytes 12000000 | tf_op jit(solution)/shard_map/pallas_call | solution.py:151
  25.2 0.0 copy-start
  25.2 0.0 copy-start.6
  25.2 0.1 multiply_convert_fusion.1
  25.3 0.1 collective-permute-start
  25.4 1.5 %collective-permute-done = f16[64,16,128]{2,1,0:T(8,128)(2,1)S(1)} collective-permute-done((f16[64,16,128]{2,1,0:T(8,128)(2,1)S(1)}, f16[64,16,128]{2,1,0:T(8,128)(2,1)S(1)}, u32[]{:S(2)}, u32[]{:S(2)}) %collective-permute-start) | collective-permute-done | bytes 262176 | tf_op jit(solution)/shard_map/ppermute | solution.py:182
  26.9 0.1 add_convert_fusion.1
  27.0 21.1 %all_to_all.91 = f16[32,2,16,128]{3,2,1,0:T(8,128)(2,1)S(1)} all-to-all(f16[32,2,16,128]{3,2,1,0:T(8,128)(2,1)S(1)} %bitcast.182), channel_id=1, replica_groups=mesh['gx'=4,'gy'=8,'gq'=4,'core'=2] {'gy','gq'}, dimensions={0} | all-to-all | bytes 524288 | tf_op jit(solution)/shard_map/all_to_all | solution.py:184
  48.2 14.4 %all_to_all.92 = f16[32,2,16,128]{3,2,1,0:T(8,128)(2,1)S(1)} all-to-all(f16[32,2,16,128]{3,2,1,0:T(8,128)(2,1)S(1)} %broadcast_in_dim.43), channel_id=1, replica_groups=mesh['gx'=4,'gy'=8,'gq'=4,'core'=2] {'gx','gq','core'}, dimensions={0} | all-to-all | bytes 524288 | tf_op jit(solution)/shard_map/all_to_all | solution.py:178
  62.6 0.1 convert_multiply_fusion
  62.7 4.6 %shard_map.114 = (f32[64,16,128]{2,1,0:T(8,128)S(1)}, f32[64,16,128]{2,1,0:T(8,128)S(1)}) custom-call(s32[128]{0:T(128)S(1)} %copy-done.7, s32[128]{0:T(128)S(1)} %copy-done.8, s32[192]{0:T(256)S(1)} %copy-done.5, s32[192]{0:T(256)S(1)} %copy-done.6, s32[1]{0:T(128)S(6)} %copy.92.nc, s32[1]{0:T(128)S(6)} %copy.93.fc, f32[64,16,128]{2,1,0:T(8,128)S(1)} %bitcast.168, ...), custom_call_target="tpu_custom_call" | custom-call | flops 170000000 | bytes 12000000 | tf_op jit(solution)/shard_map/pallas_call | solution.py:151
  67.3 0.1 multiply_convert_fusion
  67.4 0.1 collective-permute-start.1
  67.5 1.5 %collective-permute-done.1 = f16[64,16,128]{2,1,0:T(8,128)(2,1)S(1)} collective-permute-done((f16[64,16,128]{2,1,0:T(8,128)(2,1)S(1)}, f16[64,16,128]{2,1,0:T(8,128)(2,1)S(1)}, u32[]{:S(2)}, u32[]{:S(2)}) %collective-permute-start.1) | collective-permute-done | bytes 262176 | tf_op jit(solution)/shard_map/ppermute | solution.py:182
  69.0 0.1 add_convert_fusion
  69.1 15.1 %all_to_all.93 = f16[32,2,16,128]{3,2,1,0:T(8,128)(2,1)S(1)} all-to-all(f16[32,2,16,128]{3,2,1,0:T(8,128)(2,1)S(1)} %bitcast.183), channel_id=1, replica_groups=mesh['gx'=4,'gy'=8,'gq'=4,'core'=2] {'gy','gq'}, dimensions={0} | all-to-all | bytes 524288 | tf_op jit(solution)/shard_map/all_to_all | solution.py:184
  84.2 0.2 multiply_reduce_fusion.6
  84.5 13.1 %all_to_all.94 = f32[32,6,16]{2,1,0:T(8,128)S(1)} all-to-all(f32[32,6,16]{2,1,0:T(8,128)S(1)} %broadcast_in_dim.44), channel_id=1, replica_groups=mesh['gx'=4,'gy'=8,'gq'=4,'core'=2] {'gx','gq','core'}, dimensions={0} | all-to-all | bytes 24576 | tf_op jit(solution)/shard_map/all_to_all | solution.py:178
  97.6 0.6 collective-permute-start.2
  98.2 2.1 %collective-permute-done.2 = f32[6,16]{1,0:T(8,128)S(1)} collective-permute-done((f32[6,16]{1,0:T(8,128)S(1)}, f32[6,16]{1,0:T(8,128)S(1)}, u32[]{:S(2)}, u32[]{:S(2)}) %collective-permute-start.2) | collective-permute-done | bytes 416 | tf_op jit(solution)/shard_map/ppermute | solution.py:288
  100.3 0.4 collective-permute-start.3
  100.7 3.0 %collective-permute-done.3 = f32[6,16]{1,0:T(8,128)S(1)} collective-permute-done((f32[6,16]{1,0:T(8,128)S(1)}, f32[6,16]{1,0:T(8,128)S(1)}, u32[]{:S(2)}, u32[]{:S(2)}) %collective-permute-start.3) | collective-permute-done | bytes 416 | tf_op jit(solution)/shard_map/ppermute | solution.py:288
  103.7 0.9 collective-permute-start.4
  104.6 5.5 %collective-permute-done.4 = f32[6,16]{1,0:T(8,128)S(1)} collective-permute-done((f32[6,16]{1,0:T(8,128)S(1)}, f32[6,16]{1,0:T(8,128)S(1)}, u32[]{:S(2)}, u32[]{:S(2)}) %collective-permute-start.4) | collective-permute-done | bytes 416 | tf_op jit(solution)/shard_map/ppermute | solution.py:288
  110.1 0.7 shard_map.115
  111.5 0.6 copy-done.9
  (27 shorter events, 0.3 us)
Async XLA Ops:
  2.1 17.5 %all-to-all-start.16 = ((f16[32,2,16,128]{3,2,1,0:T(8,128)(2,1)}), f16[32,2,16,128]{3,2,1,0:T(8,128)(2,1)S(1)}, u32[]{:S(2)}, u32[]{:S(2)}) async-start(f16[32,2,16,128]{3,2,1,0:T(8,128)(2,1)} %broadcast_in_dim.42), calls=%async_computation.16 | async-start | bytes 524288 | tf_op jit(solution)/shard_map/all_to_all | solution.py:178
  19.6 28.5 %copy-start.4 = (f32[16,256]{1,0:T(8,128)S(1)}, f32[16,256]{1,0:T(8,128)}, u32[]{:S(2)}) copy-start(f32[16,256]{1,0:T(8,128)} %r_ref.1) | copy-start | bytes 49156
  19.7 43.0 %copy-start.1 = (bf16[192,128,64]{1,2,0:T(8,128)(2,1)S(1)}, bf16[192,128,64]{1,2,0:T(8,128)(2,1)}, u32[]{:S(2)}) copy-start(bf16[192,128,64]{1,2,0:T(8,128)(2,1)} %param.17) | copy-start | bytes 9437188
  19.7 43.0 %copy-start.2 = (bf16[192,128,64]{1,2,0:T(8,128)(2,1)S(1)}, bf16[192,128,64]{1,2,0:T(8,128)(2,1)}, u32[]{:S(2)}) copy-start(bf16[192,128,64]{1,2,0:T(8,128)(2,1)} %param.18) | copy-start | bytes 9437188
  25.2 37.5 %copy-start = (bf16[128,128,128]{2,1,0:T(8,128)(2,1)S(1)}, bf16[128,128,128]{2,1,0:T(8,128)(2,1)}, u32[]{:S(2)}) copy-start(bf16[128,128,128]{2,1,0:T(8,128)(2,1)} %near.3) | copy-start | bytes 12582916
  25.2 37.5 %copy-start.5 = (s32[192]{0:T(256)S(1)}, s32[192]{0:T(256)}, u32[]{:S(2)}) copy-start(s32[192]{0:T(256)} %ft.3) | copy-start | bytes 2308
  25.2 37.5 %copy-start.6 = (s32[192]{0:T(256)S(1)}, s32[192]{0:T(256)}, u32[]{:S(2)}) copy-start(s32[192]{0:T(256)} %fs.3) | copy-start | bytes 2308
  25.2 37.5 %copy-start.7 = (s32[128]{0:T(128)S(1)}, s32[128]{0:T(128)}, u32[]{:S(2)}) copy-start(s32[128]{0:T(128)} %nt.3) | copy-start | bytes 1540
  25.2 37.5 %copy-start.8 = (s32[128]{0:T(128)S(1)}, s32[128]{0:T(128)}, u32[]{:S(2)}) copy-start(s32[128]{0:T(128)} %ns.3) | copy-start | bytes 1540
  25.3 1.6 %collective-permute-start = (f16[64,16,128]{2,1,0:T(8,128)(2,1)S(1)}, f16[64,16,128]{2,1,0:T(8,128)(2,1)S(1)}, u32[]{:S(2)}, u32[]{:S(2)}) collective-permute-start(f16[64,16,128]{2,1,0:T(8,128)(2,1)S(1)} %multiply_convert_fusion.1), channel_id=1, source_target_pairs={{0,1},{1,0},{2,3},{3,2},{4,5},{5,4},{6,7},{7,6},{8,9},{9,8},{10,11... | collective-permute-start | bytes 786440 | tf_op jit(solution)/shard_map/ppermute | solution.py:182
  67.4 1.6 %collective-permute-start.1 = (f16[64,16,128]{2,1,0:T(8,128)(2,1)S(1)}, f16[64,16,128]{2,1,0:T(8,128)(2,1)S(1)}, u32[]{:S(2)}, u32[]{:S(2)}) collective-permute-start(f16[64,16,128]{2,1,0:T(8,128)(2,1)S(1)} %multiply_convert_fusion), channel_id=1, source_target_pairs={{0,1},{1,0},{2,3},{3,2},{4,5},{5,4},{6,7},{7,6},{8,9},{9,8},{10,11... | collective-permute-start | bytes 786440 | tf_op jit(solution)/shard_map/ppermute | solution.py:182
  97.6 2.7 %collective-permute-start.2 = (f32[6,16]{1,0:T(8,128)S(1)}, f32[6,16]{1,0:T(8,128)S(1)}, u32[]{:S(2)}, u32[]{:S(2)}) collective-permute-start(f32[6,16]{1,0:T(8,128)S(1)} %reduce_sum.279), channel_id=1, source_target_pairs={{0,8},{8,0},{16,24},{24,16},{32,40},{40,32},{48,56},{56,48},{1,9},... | collective-permute-start | bytes 1160 | tf_op jit(solution)/shard_map/ppermute | solution.py:288
  100.3 3.4 %collective-permute-start.3 = (f32[6,16]{1,0:T(8,128)S(1)}, f32[6,16]{1,0:T(8,128)S(1)}, u32[]{:S(2)}, u32[]{:S(2)}) collective-permute-start(f32[6,16]{1,0:T(8,128)S(1)} %add.114), channel_id=1, source_target_pairs={{0,16},{8,24},{16,0},{24,8},{32,48},{40,56},{48,32},{56,40},{1,17}... | collective-permute-start | bytes 1160 | tf_op jit(solution)/shard_map/ppermute | solution.py:288
  103.7 6.4 %collective-permute-start.4 = (f32[6,16]{1,0:T(8,128)S(1)}, f32[6,16]{1,0:T(8,128)S(1)}, u32[]{:S(2)}, u32[]{:S(2)}) collective-permute-start(f32[6,16]{1,0:T(8,128)S(1)} %add.115), channel_id=1, source_target_pairs={{0,32},{8,40},{16,48},{24,56},{32,0},{40,8},{48,16},{56,24},{1,33}... | collective-permute-start | bytes 1160 | tf_op jit(solution)/shard_map/ppermute | solution.py:288
  111.4 0.6 copy-start.9
  111.5 0.6 copy-start.10

commit v5 on v4

--- a/solution.py
+++ b/solution.py
@@ -18,10 +18,8 @@
 PLANE = ("gx", "gq", "core")
 TARGETS = 64
 SOURCES = 128
-NEAR_CHUNK = 32
-FAR_CHUNK = 48
-NEAR_STEP = 32
-FAR_STEP = 48
+NEAR_STEP = NEAR_CHUNK = 32
+FAR_STEP = FAR_CHUNK = 48
 
 SCALE_R = 2.0**15
 SCALE = 2.0**4
@@ -54,9 +52,18 @@
     return high, (value - high.astype(jnp.float32)).astype(jnp.bfloat16)
 
 
+def first_kernel(*refs):
+    *indices, field, near, left, right, keep, send, near_v, left_v, right_v, sems = refs[:16]
+    multiply(*indices, field, near_v, left_v, right_v, keep, send, *refs[16:], blocks_in=(near, left, right, sems))
+
+
+def second_kernel(*refs):
+    multiply(*refs)
+
+
 def multiply(
-    nt, ns, ft, fs, nc, fc, field, near, left, right, keep, send,
-    x, acc, near_v, left_v, right_v, sems, nt_s, ns_s, ft_s, fs_s, nc_s, fc_s, index_sems,
+    nt, ns, ft, fs, nc, fc, field, near_v, left_v, right_v, keep, send,
+    x, acc, nt_s, ns_s, ft_s, fs_s, nc_s, fc_s, index_sems, blocks_in=None,
 ):
     fetches = [
         pltpu.make_async_copy(source, held, index_sems.at[i])
@@ -66,7 +73,9 @@
     ]
     for fetch in fetches:
         fetch.start()
-    copies = start_blocks(near, left, right, near_v, left_v, right_v, sems)
+    if blocks_in:
+        near, left, right, sems = blocks_in
+        copies = start_blocks(near, left, right, near_v, left_v, right_v, sems)
     high, low = two_terms(field[...])
     x[:TARGETS, :OBJ] = high
     x[:TARGETS, OBJ:] = low
@@ -130,36 +139,37 @@
         add(far_parts, fs_s, far_first)
 
     steps = jnp.maximum((near_live + NEAR_STEP - 1) // NEAR_STEP, (far_live + FAR_STEP - 1) // FAR_STEP)
-    per_chunk = NEAR_CHUNK // NEAR_STEP
-    for chunk in range(NEAR_DEV // NEAR_CHUNK):
-        for copy in copies[3 * chunk : 3 * chunk + 3]:
-            copy.wait()
-
-        def body(index, carry, first=chunk * per_chunk):
-            step(first + index)
-            return carry
-
-        lax.fori_loop(0, jnp.clip(steps - chunk * per_chunk, 0, per_chunk), body, 0)
+
+    def body(index, carry):
+        step(index)
+        return carry
+
+    if blocks_in:
+        for chunk in range(NEAR_DEV // NEAR_CHUNK):
+            for copy in copies[3 * chunk : 3 * chunk + 3]:
+                copy.wait()
+            lax.fori_loop(chunk, jnp.clip(steps, chunk, chunk + 1), body, 0)
+    else:
+        lax.fori_loop(0, steps, body, 0)
     core = lax.axis_index("core")
     by_core = acc.reshape(SOURCES // 4, 4, OBJ, LEAF)
     keep[...] = by_core[:, pl.ds(2 * core, 2)].reshape(keep.shape)
     send[...] = by_core[:, pl.ds(2 - 2 * core, 2)].reshape(send.shape)
 
 
-def product(lists, field, blocks):
+def product(lists, field, blocks, first):
     half = jax.ShapeDtypeStruct((SOURCES // 2, OBJ, LEAF), jnp.float32)
+    held = [pltpu.VMEM(block.shape, block.dtype) for block in blocks]
+    held.append(pltpu.SemaphoreType.DMA((3 * (NEAR_DEV // NEAR_CHUNK),)))
     return pl.pallas_call(
-        multiply,
+        first_kernel if first else second_kernel,
         out_shape=(half, half),
-        in_specs=[HBM] * 6 + [VMEM] + [HBM] * 3,
+        in_specs=[HBM] * 6 + [VMEM] + [HBM if first else VMEM] * 3,
         out_specs=(VMEM, VMEM),
-        scratch_shapes=[
+        scratch_shapes=(held if first else [])
+        + [
             pltpu.VMEM((TARGETS + 1, 2 * OBJ, LEAF), jnp.bfloat16),
             pltpu.VMEM((SOURCES, OBJ, LEAF), jnp.float32),
-            pltpu.VMEM((NEAR_DEV, LEAF, LEAF), jnp.bfloat16),
-            pltpu.VMEM((FAR_DEV, RANK, LEAF), jnp.bfloat16),
-            pltpu.VMEM((FAR_DEV, RANK, LEAF), jnp.bfloat16),
-            pltpu.SemaphoreType.DMA((3 * (NEAR_DEV // NEAR_CHUNK),)),
             pltpu.SMEM((NEAR_DEV,), jnp.int32),
             pltpu.SMEM((NEAR_DEV,), jnp.int32),
             pltpu.SMEM((FAR_DEV,), jnp.int32),
@@ -199,7 +209,7 @@
 
 
 def finish(sums_ref, r_ref, u_ref, w_ref, basis_ref, entries_ref, fails_ref):
-    sums = sums_ref[...]
+    sums = jnp.sum(sums_ref[...], axis=0)
     rr, ru, uu, rw, uw, ww = (sums[i : i + 1] for i in range(6))
     beta_sq = rr + EPS
     beta = jnp.sqrt(beta_sq)
@@ -280,12 +290,10 @@
     r = jnp.swapaxes(r0.reshape(OBJ, CL_DEV, LEAF), 0, 1)
 
     lists = (nt, ns, ft, fs, nc, fc)
-    u = 0.5 * r + scatter_sum(*product(lists, gather_targets(r, SCALE_R), blocks))
-    w = 0.5 * u + scatter_sum(*product(lists, gather_targets(u, SCALE), blocks))
+    u = 0.5 * r + scatter_sum(*product(lists, gather_targets(r, SCALE_R), blocks, True))
+    w = 0.5 * u + scatter_sum(*product(lists, gather_targets(u, SCALE), blocks, False))
     local = jnp.stack([dot(r, r), dot(r, u), dot(u, u), dot(r, w), dot(u, w), dot(w, w)])
-    sums = jnp.sum(to_all(local, PLANE), axis=0)
-    for distance in (1, 2, 4):
-        sums += lax.ppermute(sums, "gy", [(i, i ^ distance) for i in range(8)])
+    sums = to_all(jnp.sum(to_all(local, PLANE), axis=0), "gy")
     basis_3, entries, fails = pl.pallas_call(
         finish,
         out_shape=(

time: 114 us -> 110 us (0.965); the launches traced: 112 us -> 110 us
  waiting for transfers between devices: 21.3 us -> 17 us
  starting transfers between devices: 10.6 us -> 12.6 us
    ppermute x3 -> x0, waiting for transfers between devices: 10.6 us -> none  [on_device(): sums += lax.ppermute(sums, 'gy', [(i, i ^ distance) for i in range(8)])]
    all_to_all x1 -> x2, waiting for transfers between devices: 7.61 us -> 14.4 us  [to_all(): lax.all_to_all(jnp.broadcast_to(value[None], (size,) + value.shape), axes...]
    all_to_all x1 -> x2, starting transfers between devices: 8.59 us -> 11.9 us  [to_all(): lax.all_to_all(jnp.broadcast_to(value[None], (size,) + value.shape), axes...]
    ppermute x3 -> x0, starting transfers between devices: 1.85 us -> none  [on_device(): sums += lax.ppermute(sums, 'gy', [(i, i ^ distance) for i in range(8)])]
  transfers between devices with their start and end apart: 6 -> 4, of which waited for: 6 -> 4; matrix products, arithmetic and copies ran while one was open for 0% -> 0% of each run, Pallas kernels for 0% -> 0%
where the time goes in v5:
time: 110 us
  blocking collectives  63.6 us (58%)
  waiting for transfers between devices  17 us (15%)
  starting transfers between devices  12.6 us (11%)
  Pallas kernels  10.2 us (9%)
  between operations  2.83 us (3%)
  local copies, waits for them, and re-layouts  2.06 us (2%)
  other arithmetic  1.49 us (1%)
    all_to_all x2, blocking collectives, scatter_sum(): moved = lax.all_to_all(pieces, ('gy', 'gq'), split_axis=0, concat_axis=0)  36.1 us
    all_to_all x2, blocking collectives, to_all(): lax.all_to_all(jnp.broadcast_to(value[None], (size,) + value.shape), axes...  27.4 us
    all_to_all x2, waiting for transfers between devices, to_all(): lax.all_to_all(jnp.broadcast_to(value[None], (size,) + value.shape), axes...  14.4 us
    all_to_all x2, starting transfers between devices, to_all(): lax.all_to_all(jnp.broadcast_to(value[None], (size,) + value.shape), axes...  11.9 us
    pallas_call x2, Pallas kernels, product(): pl.pallas_call(first_kernel if first else second_kernel, out_shape=(half,...  9.51 us
    ppermute x2, waiting for transfers between devices, scatter_sum(): lax.ppermute((send * SCALE).astype(jnp.float16), 'core', [(0, 1), (1, 0)])  2.59 us
  transfers between devices with their start and end apart: 4, of which 4 were waited for; matrix products, arithmetic and copies ran while one was open for 0% of the time, Pallas kernels for 0%

profile of v5, /device:TPU:1, one launch (start us, length us, event | category | flops | bytes accessed | tf_op | source)
XLA Modules:
  0.0 109.9 jit_solution(376611312573693095)
XLA Ops:
  0.6 0.7 fusion.17
  1.4 0.7 broadcast_in_dim.44
  2.1 8.6 %all-to-all-start.16 = ((f16[32,2,16,128]{3,2,1,0:T(8,128)(2,1)}), f16[32,2,16,128]{3,2,1,0:T(8,128)(2,1)S(1)}, u32[]{:S(2)}, u32[]{:S(2)}) async-start(f16[32,2,16,128]{3,2,1,0:T(8,128)(2,1)} %broadcast_in_dim.44), calls=%async_computation.16 | async-start | bytes 524288 | tf_op jit(solution)/shard_map/all_to_all | solution.py:188
  12.0 7.6 %all-to-all-done.16 = f16[32,2,16,128]{3,2,1,0:T(8,128)(2,1)S(1)} async-done(((f16[32,2,16,128]{3,2,1,0:T(8,128)(2,1)}), f16[32,2,16,128]{3,2,1,0:T(8,128)(2,1)S(1)}, u32[]{:S(2)}, u32[]{:S(2)}) %all-to-all-start.16) | async-done | bytes 262176 | tf_op jit(solution)/shard_map/all_to_all | solution.py:188
  19.6 0.1 convert_multiply_fusion.1
  19.6 0.0 copy-start.4
  19.7 0.0 copy-start.1
  19.7 5.4 %shard_map.113 = (f32[64,16,128]{2,1,0:T(8,128)S(1)}, f32[64,16,128]{2,1,0:T(8,128)S(1)}) custom-call(s32[128]{0:T(128)} %refs_0_.3, s32[128]{0:T(128)} %refs_1_.3, s32[192]{0:T(256)} %refs_2_.3, s32[192]{0:T(256)} %refs_3_.3, s32[1]{0:T(128)S(6)} %copy.92.refs_4_, s32[1]{0:T(128)S(6)} %copy.93.refs_5_, f32[64,16,128]{2,1,0:T(8,128)S(1)} %bitcast.169, ...), custom_call_target="tpu_custom_call" | custom-call | flops 170000000 | bytes 12000000 | tf_op jit(solution)/shard_map/pallas_call | solution.py:164
  25.1 0.0 copy-start.5
  25.1 0.0 copy-start.6
  25.2 0.1 multiply_convert_fusion.1
  25.2 0.3 collective-permute-start
  25.6 1.3 %collective-permute-done = f16[64,16,128]{2,1,0:T(8,128)(2,1)S(1)} collective-permute-done((f16[64,16,128]{2,1,0:T(8,128)(2,1)S(1)}, f16[64,16,128]{2,1,0:T(8,128)(2,1)S(1)}, u32[]{:S(2)}, u32[]{:S(2)}) %collective-permute-start) | collective-permute-done | bytes 262176 | tf_op jit(solution)/shard_map/ppermute | solution.py:192
  26.9 0.1 add_convert_fusion.1
  27.0 21.1 %all_to_all.96 = f16[32,2,16,128]{3,2,1,0:T(8,128)(2,1)S(1)} all-to-all(f16[32,2,16,128]{3,2,1,0:T(8,128)(2,1)S(1)} %bitcast.182), channel_id=1, replica_groups=mesh['gx'=4,'gy'=8,'gq'=4,'core'=2] {'gy','gq'}, dimensions={0} | all-to-all | bytes 524288 | tf_op jit(solution)/shard_map/all_to_all | solution.py:194
  48.2 14.4 %all_to_all.97 = f16[32,2,16,128]{3,2,1,0:T(8,128)(2,1)S(1)} all-to-all(f16[32,2,16,128]{3,2,1,0:T(8,128)(2,1)S(1)} %broadcast_in_dim.45), channel_id=1, replica_groups=mesh['gx'=4,'gy'=8,'gq'=4,'core'=2] {'gx','gq','core'}, dimensions={0} | all-to-all | bytes 524288 | tf_op jit(solution)/shard_map/all_to_all | solution.py:188
  62.5 0.1 convert_multiply_fusion
  62.6 4.1 %shard_map.114 = (f32[64,16,128]{2,1,0:T(8,128)S(1)}, f32[64,16,128]{2,1,0:T(8,128)S(1)}) custom-call(s32[128]{0:T(128)S(1)} %copy-done.7, s32[128]{0:T(128)S(1)} %copy-done.8, s32[192]{0:T(256)S(1)} %copy-done.5, s32[192]{0:T(256)S(1)} %copy-done.6, s32[1]{0:T(128)S(6)} %copy.92.refs_4_, s32[1]{0:T(128)S(6)} %copy.93.refs_5_, f32[64,16,128]{2,1,0:T(8,128)S(1)} %bitcast.168, ...), custom_call_target="tpu_custom_call" | custom-call | flops 170000000 | bytes 12000000 | tf_op jit(solution)/shard_map/pallas_call | solution.py:164
  66.7 0.1 multiply_convert_fusion
  66.8 0.3 collective-permute-start.1
  67.1 1.3 %collective-permute-done.1 = f16[64,16,128]{2,1,0:T(8,128)(2,1)S(1)} collective-permute-done((f16[64,16,128]{2,1,0:T(8,128)(2,1)S(1)}, f16[64,16,128]{2,1,0:T(8,128)(2,1)S(1)}, u32[]{:S(2)}, u32[]{:S(2)}) %collective-permute-start.1) | collective-permute-done | bytes 262176 | tf_op jit(solution)/shard_map/ppermute | solution.py:192
  68.4 0.1 add_convert_fusion
  68.5 15.0 %all_to_all.98 = f16[32,2,16,128]{3,2,1,0:T(8,128)(2,1)S(1)} all-to-all(f16[32,2,16,128]{3,2,1,0:T(8,128)(2,1)S(1)} %bitcast.183), channel_id=1, replica_groups=mesh['gx'=4,'gy'=8,'gq'=4,'core'=2] {'gy','gq'}, dimensions={0} | all-to-all | bytes 524288 | tf_op jit(solution)/shard_map/all_to_all | solution.py:194
  83.6 0.2 multiply_reduce_fusion.6
  83.9 13.1 %all_to_all.99 = f32[32,6,16]{2,1,0:T(8,128)S(1)} all-to-all(f32[32,6,16]{2,1,0:T(8,128)S(1)} %broadcast_in_dim.46), channel_id=1, replica_groups=mesh['gx'=4,'gy'=8,'gq'=4,'core'=2] {'gx','gq','core'}, dimensions={0} | all-to-all | bytes 24576 | tf_op jit(solution)/shard_map/all_to_all | solution.py:188
  97.0 0.6 broadcast_in_dim.47
  97.6 3.3 %all-to-all-start.21 = ((f32[8,6,16]{2,1,0:T(8,128)}), f32[8,6,16]{2,1,0:T(8,128)S(1)}, u32[]{:S(2)}, u32[]{:S(2)}) async-start(f32[8,6,16]{2,1,0:T(8,128)} %broadcast_in_dim.47), calls=%async_computation.21 | async-start | bytes 65536 | tf_op jit(solution)/shard_map/all_to_all | solution.py:188
  101.0 6.8 %all-to-all-done.21.sums_ref = f32[8,6,16]{2,1,0:T(8,128)S(1)} async-done(((f32[8,6,16]{2,1,0:T(8,128)}), f32[8,6,16]{2,1,0:T(8,128)S(1)}, u32[]{:S(2)}, u32[]{:S(2)}) %all-to-all-start.21) | async-done | bytes 3104 | tf_op jit(solution)/shard_map/all_to_all | solution.py:188
  107.7 0.7 shard_map.115
  109.1 0.2 conditional.1
  109.3 0.0 copy-start.10
  109.4 0.6 copy-done.9
  (21 shorter events, 0.3 us)
Async XLA Ops:
  2.1 17.5 %all-to-all-start.16 = ((f16[32,2,16,128]{3,2,1,0:T(8,128)(2,1)}), f16[32,2,16,128]{3,2,1,0:T(8,128)(2,1)S(1)}, u32[]{:S(2)}, u32[]{:S(2)}) async-start(f16[32,2,16,128]{3,2,1,0:T(8,128)(2,1)} %broadcast_in_dim.44), calls=%async_computation.16 | async-start | bytes 524288 | tf_op jit(solution)/shard_map/all_to_all | solution.py:188
  19.6 28.4 %copy-start.4 = (f32[16,256]{1,0:T(8,128)S(1)}, f32[16,256]{1,0:T(8,128)}, u32[]{:S(2)}) copy-start(f32[16,256]{1,0:T(8,128)} %r_ref.1) | copy-start | bytes 49156
  19.7 42.9 %copy-start.1 = (bf16[192,128,64]{1,2,0:T(8,128)(2,1)S(1)}, bf16[192,128,64]{1,2,0:T(8,128)(2,1)}, u32[]{:S(2)}) copy-start(bf16[192,128,64]{1,2,0:T(8,128)(2,1)} %param.17) | copy-start | bytes 9437188
  19.7 42.9 %copy-start.2 = (bf16[192,128,64]{1,2,0:T(8,128)(2,1)S(1)}, bf16[192,128,64]{1,2,0:T(8,128)(2,1)}, u32[]{:S(2)}) copy-start(bf16[192,128,64]{1,2,0:T(8,128)(2,1)} %param.18) | copy-start | bytes 9437188
  25.1 37.5 %copy-start = (bf16[128,128,128]{2,1,0:T(8,128)(2,1)S(1)}, bf16[128,128,128]{2,1,0:T(8,128)(2,1)}, u32[]{:S(2)}) copy-start(bf16[128,128,128]{2,1,0:T(8,128)(2,1)} %refs_7_.3) | copy-start | bytes 12582916
  25.1 37.5 %copy-start.5 = (s32[192]{0:T(256)S(1)}, s32[192]{0:T(256)}, u32[]{:S(2)}) copy-start(s32[192]{0:T(256)} %refs_2_.3) | copy-start | bytes 2308
  25.1 37.5 %copy-start.6 = (s32[192]{0:T(256)S(1)}, s32[192]{0:T(256)}, u32[]{:S(2)}) copy-start(s32[192]{0:T(256)} %refs_3_.3) | copy-start | bytes 2308
  25.1 37.5 %copy-start.7 = (s32[128]{0:T(128)S(1)}, s32[128]{0:T(128)}, u32[]{:S(2)}) copy-start(s32[128]{0:T(128)} %refs_0_.3) | copy-start | bytes 1540
  25.2 37.5 %copy-start.8 = (s32[128]{0:T(128)S(1)}, s32[128]{0:T(128)}, u32[]{:S(2)}) copy-start(s32[128]{0:T(128)} %refs_1_.3) | copy-start | bytes 1540
  25.2 1.6 %collective-permute-start = (f16[64,16,128]{2,1,0:T(8,128)(2,1)S(1)}, f16[64,16,128]{2,1,0:T(8,128)(2,1)S(1)}, u32[]{:S(2)}, u32[]{:S(2)}) collective-permute-start(f16[64,16,128]{2,1,0:T(8,128)(2,1)S(1)} %multiply_convert_fusion.1), channel_id=1, source_target_pairs={{0,1},{1,0},{2,3},{3,2},{4,5},{5,4},{6,7},{7,6},{8,9},{9,8},{10,11... | collective-permute-start | bytes 786440 | tf_op jit(solution)/shard_map/ppermute | solution.py:192
  66.8 1.6 %collective-permute-start.1 = (f16[64,16,128]{2,1,0:T(8,128)(2,1)S(1)}, f16[64,16,128]{2,1,0:T(8,128)(2,1)S(1)}, u32[]{:S(2)}, u32[]{:S(2)}) collective-permute-start(f16[64,16,128]{2,1,0:T(8,128)(2,1)S(1)} %multiply_convert_fusion), channel_id=1, source_target_pairs={{0,1},{1,0},{2,3},{3,2},{4,5},{5,4},{6,7},{7,6},{8,9},{9,8},{10,11... | collective-permute-start | bytes 786440 | tf_op jit(solution)/shard_map/ppermute | solution.py:192
  97.6 10.1 %all-to-all-start.21 = ((f32[8,6,16]{2,1,0:T(8,128)}), f32[8,6,16]{2,1,0:T(8,128)S(1)}, u32[]{:S(2)}, u32[]{:S(2)}) async-start(f32[8,6,16]{2,1,0:T(8,128)} %broadcast_in_dim.47), calls=%async_computation.21 | async-start | bytes 65536 | tf_op jit(solution)/shard_map/all_to_all | solution.py:188
  109.3 0.6 copy-start.9
  109.3 0.6 copy-start.10

commit v6 on v5

--- a/solution.py
+++ b/solution.py
@@ -208,9 +208,9 @@
     return value[None, :, None]
 
 
-def finish(sums_ref, r_ref, u_ref, w_ref, basis_ref, entries_ref, fails_ref):
-    sums = jnp.sum(sums_ref[...], axis=0)
-    rr, ru, uu, rw, uw, ww = (sums[i : i + 1] for i in range(6))
+def finish(sums_ref, r_ref, u_ref, applied_ref, basis_ref, entries_ref, fails_ref):
+    sums = sums_ref[...]
+    rr, ru, uu, rw, uw, ww = (sums[:, i * OBJ : (i + 1) * OBJ] for i in range(6))
     beta_sq = rr + EPS
     beta = jnp.sqrt(beta_sq)
     h11 = ru / beta_sq
@@ -237,7 +237,8 @@
     in_w, in_u, in_r = down(in_w), down(in_u), down(in_r)
     for i in range(CL_DEV):
         lanes = pl.ds(i * LEAF, LEAF)
-        basis_ref[:, lanes] = in_w * w_ref[i] + in_u * u_ref[i] + in_r * r_ref[:, lanes]
+        w = 0.5 * u_ref[i] + applied_ref[i]
+        basis_ref[:, lanes] = in_w * w + in_u * u_ref[i] + in_r * r_ref[:, lanes]
     rest_1 = left_1 * beta_sq
     rest_2 = left_2 * beta_sq * h21 * h21
     sound = (rest_1 >= RATIO * uu) & (rest_2 >= RATIO * ww) & (rest_1 >= FLOOR) & (rest_2 >= FLOOR)
@@ -291,9 +292,12 @@
 
     lists = (nt, ns, ft, fs, nc, fc)
     u = 0.5 * r + scatter_sum(*product(lists, gather_targets(r, SCALE_R), blocks, True))
-    w = 0.5 * u + scatter_sum(*product(lists, gather_targets(u, SCALE), blocks, False))
-    local = jnp.stack([dot(r, r), dot(r, u), dot(u, u), dot(r, w), dot(u, w), dot(w, w)])
-    sums = to_all(jnp.sum(to_all(local, PLANE), axis=0), "gy")
+    applied = scatter_sum(*product(lists, gather_targets(u, SCALE), blocks, False))
+    w = 0.5 * u + applied
+    dots = [dot(r, r), dot(r, u), dot(u, u), dot(r, w), dot(u, w), dot(w, w)]
+    local = jnp.concatenate(dots + [jnp.zeros((LEAF - len(dots) * OBJ,), jnp.float32)])[None]
+    chip = local + lax.ppermute(local, "core", [(0, 1), (1, 0)])
+    sums = jnp.sum(to_all(chip, ("gx", "gy", "gq")), axis=0)
     basis_3, entries, fails = pl.pallas_call(
         finish,
         out_shape=(
@@ -304,9 +308,9 @@
         in_specs=[VMEM] * 4,
         out_specs=(VMEM, VMEM, SMEM),
         compiler_params=pltpu.CompilerParams(vmem_limit_bytes=2 * 1024 * 1024),
-    )(sums, r0, u, w)
-    basis_3, entries = lax.cond(
-        fails[0] == 0, lambda: (basis_3, entries), lambda: plainly(r0, indices, blocks)
+    )(sums, r0, u, applied)
+    basis_3, entries = lax.switch(
+        fails[0], (lambda: (basis_3, entries), lambda: plainly(r0, indices, blocks))
     )
     return basis_3, entries.T
 

time: 110 us -> 107 us (0.973)
  blocking collectives: 63.6 us -> 50.5 us
  starting transfers between devices: 12.6 us -> 17.6 us
  waiting for transfers between devices: 17 us -> 21.6 us
    all_to_all x2 -> x1, blocking collectives: 27.4 us -> 14.4 us  [to_all(): lax.all_to_all(jnp.broadcast_to(value[None], (size,) + value.shape), axes...]
    all_to_all x2, waiting for transfers between devices: 14.4 us -> 18.2 us  [to_all(): lax.all_to_all(jnp.broadcast_to(value[None], (size,) + value.shape), axes...]
    all_to_all x2, starting transfers between devices: 11.9 us -> 14.8 us  [to_all(): lax.all_to_all(jnp.broadcast_to(value[None], (size,) + value.shape), axes...]
    ppermute x0 -> x1, starting transfers between devices: none -> 2.18 us  [on_device(): chip = local + lax.ppermute(local, 'core', [(0, 1), (1, 0)])]
  transfers between devices with their start and end apart: 4 -> 5, of which waited for: 4 -> 5; matrix products, arithmetic and copies ran while one was open for 0% -> 0% of each run, Pallas kernels for 0% -> 0%
where the time goes in v6:
time: 107 us
  blocking collectives  50.5 us (47%)
  waiting for transfers between devices  21.6 us (20%)
  starting transfers between devices  17.6 us (16%)
  Pallas kernels  10.8 us (10%)
  between operations  2.83 us (3%)
  local copies, waits for them, and re-layouts  2.15 us (2%)
  other arithmetic  1.49 us (1%)
    all_to_all x2, blocking collectives, scatter_sum(): moved = lax.all_to_all(pieces, ('gy', 'gq'), split_axis=0, concat_axis=0)  36.1 us
    all_to_all x2, waiting for transfers between devices, to_all(): lax.all_to_all(jnp.broadcast_to(value[None], (size,) + value.shape), axes...  18.2 us
    all_to_all x2, starting transfers between devices, to_all(): lax.all_to_all(jnp.broadcast_to(value[None], (size,) + value.shape), axes...  14.8 us
    all_to_all x1, blocking collectives, to_all(): lax.all_to_all(jnp.broadcast_to(value[None], (size,) + value.shape), axes...  14.4 us
    pallas_call x2, Pallas kernels, product(): pl.pallas_call(first_kernel if first else second_kernel, out_shape=(half,...  9.53 us
    ppermute x2, waiting for transfers between devices, scatter_sum(): lax.ppermute((send * SCALE).astype(jnp.float16), 'core', [(0, 1), (1, 0)])  2.6 us
    ppermute x1, starting transfers between devices, on_device(): chip = local + lax.ppermute(local, 'core', [(0, 1), (1, 0)])  2.18 us
  transfers between devices with their start and end apart: 5, of which 5 were waited for; matrix products, arithmetic and copies ran while one was open for 0% of the time, Pallas kernels for 0%

profile of v6, /device:TPU:1, one launch (start us, length us, event | category | flops | bytes accessed | tf_op | source)
XLA Modules:
  0.0 107.1 jit_solution(6437975487893537542)
XLA Ops:
  0.6 0.7 fusion.17
  1.4 0.7 broadcast_in_dim.48
  2.1 8.6 %all-to-all-start.16 = ((f16[32,2,16,128]{3,2,1,0:T(8,128)(2,1)}), f16[32,2,16,128]{3,2,1,0:T(8,128)(2,1)S(1)}, u32[]{:S(2)}, u32[]{:S(2)}) async-start(f16[32,2,16,128]{3,2,1,0:T(8,128)(2,1)} %broadcast_in_dim.48), calls=%async_computation.16 | async-start | bytes 524288 | tf_op jit(solution)/shard_map/all_to_all | solution.py:188
  12.0 7.6 %all-to-all-done.16 = f16[32,2,16,128]{3,2,1,0:T(8,128)(2,1)S(1)} async-done(((f16[32,2,16,128]{3,2,1,0:T(8,128)(2,1)}), f16[32,2,16,128]{3,2,1,0:T(8,128)(2,1)S(1)}, u32[]{:S(2)}, u32[]{:S(2)}) %all-to-all-start.16) | async-done | bytes 262176 | tf_op jit(solution)/shard_map/all_to_all | solution.py:188
  19.6 0.1 convert_multiply_fusion.1
  19.6 0.0 copy-start.4
  19.7 5.4 %shard_map.113 = (f32[64,16,128]{2,1,0:T(8,128)S(1)}, f32[64,16,128]{2,1,0:T(8,128)S(1)}) custom-call(s32[128]{0:T(128)} %refs_0_.3, s32[128]{0:T(128)} %refs_1_.3, s32[192]{0:T(256)} %refs_2_.3, s32[192]{0:T(256)} %refs_3_.3, s32[1]{0:T(128)S(6)} %copy.91.refs_4_, s32[1]{0:T(128)S(6)} %copy.92.refs_5_, f32[64,16,128]{2,1,0:T(8,128)S(1)} %bitcast.169, ...), custom_call_target="tpu_custom_call" | custom-call | flops 170000000 | bytes 12000000 | tf_op jit(solution)/shard_map/pallas_call | solution.py:164
  25.1 0.0 copy-start
  25.1 0.0 copy-start.5
  25.2 0.1 multiply_convert_fusion.1
  25.3 0.3 collective-permute-start
  25.6 1.3 %collective-permute-done = f16[64,16,128]{2,1,0:T(8,128)(2,1)S(1)} collective-permute-done((f16[64,16,128]{2,1,0:T(8,128)(2,1)S(1)}, f16[64,16,128]{2,1,0:T(8,128)(2,1)S(1)}, u32[]{:S(2)}, u32[]{:S(2)}) %collective-permute-start) | collective-permute-done | bytes 262176 | tf_op jit(solution)/shard_map/ppermute | solution.py:192
  26.9 0.1 add_convert_fusion.1
  27.0 21.1 %all_to_all.91 = f16[32,2,16,128]{3,2,1,0:T(8,128)(2,1)S(1)} all-to-all(f16[32,2,16,128]{3,2,1,0:T(8,128)(2,1)S(1)} %bitcast.183), channel_id=1, replica_groups=mesh['gx'=4,'gy'=8,'gq'=4,'core'=2] {'gy','gq'}, dimensions={0} | all-to-all | bytes 524288 | tf_op jit(solution)/shard_map/all_to_all | solution.py:194
  48.2 14.4 %all_to_all.92 = f16[32,2,16,128]{3,2,1,0:T(8,128)(2,1)S(1)} all-to-all(f16[32,2,16,128]{3,2,1,0:T(8,128)(2,1)S(1)} %broadcast_in_dim.49), channel_id=1, replica_groups=mesh['gx'=4,'gy'=8,'gq'=4,'core'=2] {'gx','gq','core'}, dimensions={0} | all-to-all | bytes 524288 | tf_op jit(solution)/shard_map/all_to_all | solution.py:188
  62.5 0.1 convert_multiply_fusion
  62.7 4.1 %shard_map.114 = (f32[64,16,128]{2,1,0:T(8,128)S(1)}, f32[64,16,128]{2,1,0:T(8,128)S(1)}) custom-call(s32[128]{0:T(128)S(1)} %copy-done.7, s32[128]{0:T(128)S(1)} %copy-done.8, s32[192]{0:T(256)S(1)} %copy-done.5, s32[192]{0:T(256)S(1)} %copy-done.6, s32[1]{0:T(128)S(6)} %copy.91.refs_4_, s32[1]{0:T(128)S(6)} %copy.92.refs_5_, f32[64,16,128]{2,1,0:T(8,128)S(1)} %bitcast.168, ...), custom_call_target="tpu_custom_call" | custom-call | flops 170000000 | bytes 12000000 | tf_op jit(solution)/shard_map/pallas_call | solution.py:164
  66.8 0.1 multiply_convert_fusion
  66.8 0.3 collective-permute-start.1
  67.2 1.3 %collective-permute-done.1 = f16[64,16,128]{2,1,0:T(8,128)(2,1)S(1)} collective-permute-done((f16[64,16,128]{2,1,0:T(8,128)(2,1)S(1)}, f16[64,16,128]{2,1,0:T(8,128)(2,1)S(1)}, u32[]{:S(2)}, u32[]{:S(2)}) %collective-permute-start.1) | collective-permute-done | bytes 262176 | tf_op jit(solution)/shard_map/ppermute | solution.py:192
  68.5 0.1 add_convert_fusion
  68.6 15.0 %all_to_all.93 = f16[32,2,16,128]{3,2,1,0:T(8,128)(2,1)S(1)} all-to-all(f16[32,2,16,128]{3,2,1,0:T(8,128)(2,1)S(1)} %bitcast.184), channel_id=1, replica_groups=mesh['gx'=4,'gy'=8,'gq'=4,'core'=2] {'gy','gq'}, dimensions={0} | all-to-all | bytes 524288 | tf_op jit(solution)/shard_map/all_to_all | solution.py:194
  83.6 0.2 multiply_reduce_fusion.6
  83.8 0.1 concatenate.3
  83.9 2.2 %collective-permute-start.2 = (f32[1,128]{1,0:T(1,128)S(1)}, f32[1,128]{1,0:T(1,128)S(1)}, u32[]{:S(2)}, u32[]{:S(2)}) collective-permute-start(f32[1,128]{1,0:T(1,128)S(1)} %bitcast.195), channel_id=1, source_target_pairs={{0,1},{1,0},{2,3},{3,2},{4,5},{5,4},{6,7},{7,6},{8,9},{9,8},{10,11... | collective-permute-start | bytes 1544 | tf_op jit(solution)/shard_map/ppermute | solution.py:299
  86.1 0.8 collective-permute-done.2
  86.9 0.7 broadcast_in_dim.53
  87.6 6.2 %all-to-all-start.20 = ((f32[128,1,128]{2,1,0:T(1,128)}), f32[128,1,128]{2,1,0:T(1,128)S(1)}, u32[]{:S(2)}, u32[]{:S(2)}) async-start(f32[128,1,128]{2,1,0:T(1,128)} %broadcast_in_dim.53), calls=%async_computation.20 | async-start | bytes 131072 | tf_op jit(solution)/shard_map/all_to_all | solution.py:188
  93.8 10.6 %all-to-all-done.20 = f32[128,1,128]{2,1,0:T(1,128)S(1)} async-done(((f32[128,1,128]{2,1,0:T(1,128)}), f32[128,1,128]{2,1,0:T(1,128)S(1)}, u32[]{:S(2)}, u32[]{:S(2)}) %all-to-all-start.20) | async-done | bytes 65568 | tf_op jit(solution)/shard_map/all_to_all | solution.py:188
  104.4 1.2 %shard_map.115 = (f32[16,256]{1,0:T(8,128)S(1)}, f32[6,16]{1,0:T(8,128)S(1)}, s32[1]{0:T(128)}) custom-call(f32[1,128]{1,0:T(1,128)S(1)} %bitcast.170, f32[16,256]{1,0:T(8,128)S(1)} %copy-done.4, f32[2,16,128]{2,1,0:T(8,128)S(1)} %get-tuple-element.63.u_ref, f32[2,16,128]{2,1,0:T(8,128)S(1)} %get-tuple-element.72.applied_ref), custom_call_target="tpu_custom_call" | custom-call | tf_op jit(solution)/shard_map/pallas_call | solution.py:301
  106.3 0.2 conditional.1
  106.5 0.6 copy-done.9
  (23 shorter events, 0.2 us)
Async XLA Ops:
  2.1 17.5 %all-to-all-start.16 = ((f16[32,2,16,128]{3,2,1,0:T(8,128)(2,1)}), f16[32,2,16,128]{3,2,1,0:T(8,128)(2,1)S(1)}, u32[]{:S(2)}, u32[]{:S(2)}) async-start(f16[32,2,16,128]{3,2,1,0:T(8,128)(2,1)} %broadcast_in_dim.48), calls=%async_computation.16 | async-start | bytes 524288 | tf_op jit(solution)/shard_map/all_to_all | solution.py:188
  19.6 28.4 %copy-start.4 = (f32[16,256]{1,0:T(8,128)S(1)}, f32[16,256]{1,0:T(8,128)}, u32[]{:S(2)}) copy-start(f32[16,256]{1,0:T(8,128)} %r_ref.1) | copy-start | bytes 49156
  19.7 42.9 %copy-start.1 = (bf16[192,128,64]{1,2,0:T(8,128)(2,1)S(1)}, bf16[192,128,64]{1,2,0:T(8,128)(2,1)}, u32[]{:S(2)}) copy-start(bf16[192,128,64]{1,2,0:T(8,128)(2,1)} %param.17) | copy-start | bytes 9437188
  19.7 42.9 %copy-start.2 = (bf16[192,128,64]{1,2,0:T(8,128)(2,1)S(1)}, bf16[192,128,64]{1,2,0:T(8,128)(2,1)}, u32[]{:S(2)}) copy-start(bf16[192,128,64]{1,2,0:T(8,128)(2,1)} %param.18) | copy-start | bytes 9437188
  25.1 37.5 %copy-start = (bf16[128,128,128]{2,1,0:T(8,128)(2,1)S(1)}, bf16[128,128,128]{2,1,0:T(8,128)(2,1)}, u32[]{:S(2)}) copy-start(bf16[128,128,128]{2,1,0:T(8,128)(2,1)} %refs_7_.3) | copy-start | bytes 12582916
  25.1 37.5 %copy-start.5 = (s32[192]{0:T(256)S(1)}, s32[192]{0:T(256)}, u32[]{:S(2)}) copy-start(s32[192]{0:T(256)} %refs_2_.3) | copy-start | bytes 2308
  25.1 37.5 %copy-start.6 = (s32[192]{0:T(256)S(1)}, s32[192]{0:T(256)}, u32[]{:S(2)}) copy-start(s32[192]{0:T(256)} %refs_3_.3) | copy-start | bytes 2308
  25.2 37.5 %copy-start.7 = (s32[128]{0:T(128)S(1)}, s32[128]{0:T(128)}, u32[]{:S(2)}) copy-start(s32[128]{0:T(128)} %refs_0_.3) | copy-start | bytes 1540
  25.2 37.5 %copy-start.8 = (s32[128]{0:T(128)S(1)}, s32[128]{0:T(128)}, u32[]{:S(2)}) copy-start(s32[128]{0:T(128)} %refs_1_.3) | copy-start | bytes 1540
  25.3 1.6 %collective-permute-start = (f16[64,16,128]{2,1,0:T(8,128)(2,1)S(1)}, f16[64,16,128]{2,1,0:T(8,128)(2,1)S(1)}, u32[]{:S(2)}, u32[]{:S(2)}) collective-permute-start(f16[64,16,128]{2,1,0:T(8,128)(2,1)S(1)} %multiply_convert_fusion.1), channel_id=1, source_target_pairs={{0,1},{1,0},{2,3},{3,2},{4,5},{5,4},{6,7},{7,6},{8,9},{9,8},{10,11... | collective-permute-start | bytes 786440 | tf_op jit(solution)/shard_map/ppermute | solution.py:192
  66.8 1.6 %collective-permute-start.1 = (f16[64,16,128]{2,1,0:T(8,128)(2,1)S(1)}, f16[64,16,128]{2,1,0:T(8,128)(2,1)S(1)}, u32[]{:S(2)}, u32[]{:S(2)}) collective-permute-start(f16[64,16,128]{2,1,0:T(8,128)(2,1)S(1)} %multiply_convert_fusion), channel_id=1, source_target_pairs={{0,1},{1,0},{2,3},{3,2},{4,5},{5,4},{6,7},{7,6},{8,9},{9,8},{10,11... | collective-permute-start | bytes 786440 | tf_op jit(solution)/shard_map/ppermute | solution.py:192
  83.9 3.0 %collective-permute-start.2 = (f32[1,128]{1,0:T(1,128)S(1)}, f32[1,128]{1,0:T(1,128)S(1)}, u32[]{:S(2)}, u32[]{:S(2)}) collective-permute-start(f32[1,128]{1,0:T(1,128)S(1)} %bitcast.195), channel_id=1, source_target_pairs={{0,1},{1,0},{2,3},{3,2},{4,5},{5,4},{6,7},{7,6},{8,9},{9,8},{10,11... | collective-permute-start | bytes 1544 | tf_op jit(solution)/shard_map/ppermute | solution.py:299
  87.6 16.7 %all-to-all-start.20 = ((f32[128,1,128]{2,1,0:T(1,128)}), f32[128,1,128]{2,1,0:T(1,128)S(1)}, u32[]{:S(2)}, u32[]{:S(2)}) async-start(f32[128,1,128]{2,1,0:T(1,128)} %broadcast_in_dim.53), calls=%async_computation.20 | async-start | bytes 131072 | tf_op jit(solution)/shard_map/all_to_all | solution.py:188
  106.5 0.6 copy-start.9
  106.5 0.6 copy-start.10

commit v7 on v6

--- a/solution.py
+++ b/solution.py
@@ -210,7 +210,7 @@
 
 def finish(sums_ref, r_ref, u_ref, applied_ref, basis_ref, entries_ref, fails_ref):
     sums = sums_ref[...]
-    rr, ru, uu, rw, uw, ww = (sums[:, i * OBJ : (i + 1) * OBJ] for i in range(6))
+    rr, ru, uu, rw, uw, ww = (sums[i : i + 1] for i in range(6))
     beta_sq = rr + EPS
     beta = jnp.sqrt(beta_sq)
     h11 = ru / beta_sq
@@ -248,7 +248,7 @@
 def plainly(r0, indices, blocks):
     r = jnp.swapaxes(r0.reshape(OBJ, CL_DEV, LEAF), 0, 1)
     nt, ns, nc, ft, fs, fc = indices
-    near, left, right = blocks
+    near, left, right = blocks[0], jnp.swapaxes(blocks[1], 1, 2), jnp.swapaxes(blocks[2], 1, 2)
     near_alive = (jnp.arange(NEAR_DEV, dtype=jnp.int32) < nc[0]).astype(jnp.float32)
     far_alive = (jnp.arange(FAR_DEV, dtype=jnp.int32) < fc[0]).astype(jnp.float32)
 
@@ -297,7 +297,8 @@
     dots = [dot(r, r), dot(r, u), dot(u, u), dot(r, w), dot(u, w), dot(w, w)]
     local = jnp.concatenate(dots + [jnp.zeros((LEAF - len(dots) * OBJ,), jnp.float32)])[None]
     chip = local + lax.ppermute(local, "core", [(0, 1), (1, 0)])
-    sums = jnp.sum(to_all(chip, ("gx", "gy", "gq")), axis=0)
+    sums = jnp.sum(to_all(chip, ("gx", "gy", "gq")), axis=0)[0]
+    sums = jnp.stack([sums[i * OBJ : (i + 1) * OBJ] for i in range(len(dots))])
     basis_3, entries, fails = pl.pallas_call(
         finish,
         out_shape=(
@@ -310,7 +311,7 @@
         compiler_params=pltpu.CompilerParams(vmem_limit_bytes=2 * 1024 * 1024),
     )(sums, r0, u, applied)
     basis_3, entries = lax.switch(
-        fails[0], (lambda: (basis_3, entries), lambda: plainly(r0, indices, blocks))
+        fails[0], (lambda: (basis_3, entries), lambda: plainly(r0, indices, (near_tiles, far_left, far_right)))
     )
     return basis_3, entries.T
 

time: 107 us -> 107 us (level)
  no operation moved by 1% of the time
where the time goes in v7:
time: 107 us
  blocking collectives  50.4 us (47%)
  waiting for transfers between devices  22 us (21%)
  starting transfers between devices  17.1 us (16%)
  Pallas kernels  10.2 us (10%)
  between operations  2.85 us (3%)
  local copies, waits for them, and re-layouts  2.26 us (2%)
  other arithmetic  1.49 us (1%)
    all_to_all x2, blocking collectives, scatter_sum(): moved = lax.all_to_all(pieces, ('gy', 'gq'), split_axis=0, concat_axis=0)  36.1 us
    all_to_all x2, waiting for transfers between devices, to_all(): lax.all_to_all(jnp.broadcast_to(value[None], (size,) + value.shape), axes...  18.2 us
    all_to_all x2, starting transfers between devices, to_all(): lax.all_to_all(jnp.broadcast_to(value[None], (size,) + value.shape), axes...  14.8 us
    all_to_all x1, blocking collectives, to_all(): lax.all_to_all(jnp.broadcast_to(value[None], (size,) + value.shape), axes...  14.3 us
    pallas_call x2, Pallas kernels, product(): pl.pallas_call(first_kernel if first else second_kernel, out_shape=(half,...  9.52 us
    ppermute x2, waiting for transfers between devices, scatter_sum(): lax.ppermute((send * SCALE).astype(jnp.float16), 'core', [(0, 1), (1, 0)])  3.04 us
    ppermute x1, starting transfers between devices, on_device(): chip = local + lax.ppermute(local, 'core', [(0, 1), (1, 0)])  2.18 us
  transfers between devices with their start and end apart: 5, of which 5 were waited for; matrix products, arithmetic and copies ran while one was open for 0% of the time, Pallas kernels for 0%

profile of v7, /device:TPU:1, one launch (start us, length us, event | category | flops | bytes accessed | tf_op | source)
XLA Modules:
  0.0 106.6 jit_solution(6057315476660422561)
XLA Ops:
  0.6 0.7 fusion.17
  1.4 0.7 broadcast_in_dim.48
  2.1 8.6 %all-to-all-start.16 = ((f16[32,2,16,128]{3,2,1,0:T(8,128)(2,1)}), f16[32,2,16,128]{3,2,1,0:T(8,128)(2,1)S(1)}, u32[]{:S(2)}, u32[]{:S(2)}) async-start(f16[32,2,16,128]{3,2,1,0:T(8,128)(2,1)} %broadcast_in_dim.48), calls=%async_computation.16 | async-start | bytes 524288 | tf_op jit(solution)/shard_map/all_to_all | solution.py:188
  12.0 7.6 %all-to-all-done.16 = f16[32,2,16,128]{3,2,1,0:T(8,128)(2,1)S(1)} async-done(((f16[32,2,16,128]{3,2,1,0:T(8,128)(2,1)}), f16[32,2,16,128]{3,2,1,0:T(8,128)(2,1)S(1)}, u32[]{:S(2)}, u32[]{:S(2)}) %all-to-all-start.16) | async-done | bytes 262176 | tf_op jit(solution)/shard_map/all_to_all | solution.py:188
  19.6 0.1 convert_multiply_fusion.1
  19.7 0.0 copy-start.1
  19.7 0.0 copy-start.2
  19.7 5.4 %shard_map.113 = (f32[64,16,128]{2,1,0:T(8,128)S(1)}, f32[64,16,128]{2,1,0:T(8,128)S(1)}) custom-call(s32[128]{0:T(128)} %refs_0_.3, s32[128]{0:T(128)} %refs_1_.3, s32[192]{0:T(256)} %refs_2_.3, s32[192]{0:T(256)} %refs_3_.3, s32[1]{0:T(128)S(6)} %copy.93.refs_4_, s32[1]{0:T(128)S(6)} %copy.94.refs_5_, f32[64,16,128]{2,1,0:T(8,128)S(1)} %bitcast.169, ...), custom_call_target="tpu_custom_call" | custom-call | flops 170000000 | bytes 12000000 | tf_op jit(solution)/shard_map/pallas_call | solution.py:164
  25.2 0.1 multiply_convert_fusion.1
  25.3 0.1 collective-permute-start
  25.4 1.5 %collective-permute-done = f16[64,16,128]{2,1,0:T(8,128)(2,1)S(1)} collective-permute-done((f16[64,16,128]{2,1,0:T(8,128)(2,1)S(1)}, f16[64,16,128]{2,1,0:T(8,128)(2,1)S(1)}, u32[]{:S(2)}, u32[]{:S(2)}) %collective-permute-start) | collective-permute-done | bytes 262176 | tf_op jit(solution)/shard_map/ppermute | solution.py:192
  26.9 0.1 add_convert_fusion.1
  27.0 21.1 %all_to_all.91 = f16[32,2,16,128]{3,2,1,0:T(8,128)(2,1)S(1)} all-to-all(f16[32,2,16,128]{3,2,1,0:T(8,128)(2,1)S(1)} %bitcast.180), channel_id=1, replica_groups=mesh['gx'=4,'gy'=8,'gq'=4,'core'=2] {'gy','gq'}, dimensions={0} | all-to-all | bytes 524288 | tf_op jit(solution)/shard_map/all_to_all | solution.py:194
  48.2 14.3 %all_to_all.92 = f16[32,2,16,128]{3,2,1,0:T(8,128)(2,1)S(1)} all-to-all(f16[32,2,16,128]{3,2,1,0:T(8,128)(2,1)S(1)} %broadcast_in_dim.49), channel_id=1, replica_groups=mesh['gx'=4,'gy'=8,'gq'=4,'core'=2] {'gx','gq','core'}, dimensions={0} | all-to-all | bytes 524288 | tf_op jit(solution)/shard_map/all_to_all | solution.py:188
  62.5 0.1 convert_multiply_fusion
  62.6 4.1 %shard_map.114 = (f32[64,16,128]{2,1,0:T(8,128)S(1)}, f32[64,16,128]{2,1,0:T(8,128)S(1)}) custom-call(s32[128]{0:T(128)S(1)} %copy-done.7, s32[128]{0:T(128)S(1)} %copy-done.8, s32[192]{0:T(256)S(1)} %copy-done.5, s32[192]{0:T(256)S(1)} %copy-done.6, s32[1]{0:T(128)S(6)} %copy.93.refs_4_, s32[1]{0:T(128)S(6)} %copy.94.refs_5_, f32[64,16,128]{2,1,0:T(8,128)S(1)} %bitcast.168, ...), custom_call_target="tpu_custom_call" | custom-call | flops 170000000 | bytes 12000000 | tf_op jit(solution)/shard_map/pallas_call | solution.py:164
  66.7 0.1 multiply_convert_fusion
  66.8 0.1 collective-permute-start.1
  66.9 1.5 %collective-permute-done.1 = f16[64,16,128]{2,1,0:T(8,128)(2,1)S(1)} collective-permute-done((f16[64,16,128]{2,1,0:T(8,128)(2,1)S(1)}, f16[64,16,128]{2,1,0:T(8,128)(2,1)S(1)}, u32[]{:S(2)}, u32[]{:S(2)}) %collective-permute-start.1) | collective-permute-done | bytes 262176 | tf_op jit(solution)/shard_map/ppermute | solution.py:192
  68.4 0.1 add_convert_fusion
  68.5 15.0 %all_to_all.93 = f16[32,2,16,128]{3,2,1,0:T(8,128)(2,1)S(1)} all-to-all(f16[32,2,16,128]{3,2,1,0:T(8,128)(2,1)S(1)} %bitcast.181), channel_id=1, replica_groups=mesh['gx'=4,'gy'=8,'gq'=4,'core'=2] {'gy','gq'}, dimensions={0} | all-to-all | bytes 524288 | tf_op jit(solution)/shard_map/all_to_all | solution.py:194
  83.6 0.2 multiply_reduce_fusion.6
  83.8 0.1 concatenate.3
  83.9 2.2 %collective-permute-start.2 = (f32[1,128]{1,0:T(1,128)S(1)}, f32[1,128]{1,0:T(1,128)S(1)}, u32[]{:S(2)}, u32[]{:S(2)}) collective-permute-start(f32[1,128]{1,0:T(1,128)S(1)} %bitcast.193), channel_id=1, source_target_pairs={{0,1},{1,0},{2,3},{3,2},{4,5},{5,4},{6,7},{7,6},{8,9},{9,8},{10,11... | collective-permute-start | bytes 1544 | tf_op jit(solution)/shard_map/ppermute | solution.py:299
  86.0 0.8 collective-permute-done.2
  86.9 0.7 broadcast_in_dim.53
  87.5 6.2 %all-to-all-start.20 = ((f32[128,1,128]{2,1,0:T(1,128)}), f32[128,1,128]{2,1,0:T(1,128)S(1)}, u32[]{:S(2)}, u32[]{:S(2)}) async-start(f32[128,1,128]{2,1,0:T(1,128)} %broadcast_in_dim.53), calls=%async_computation.20 | async-start | bytes 131072 | tf_op jit(solution)/shard_map/all_to_all | solution.py:188
  93.7 10.6 %all-to-all-done.20 = f32[128,1,128]{2,1,0:T(1,128)S(1)} async-done(((f32[128,1,128]{2,1,0:T(1,128)}), f32[128,1,128]{2,1,0:T(1,128)S(1)}, u32[]{:S(2)}, u32[]{:S(2)}) %all-to-all-start.20) | async-done | bytes 65568 | tf_op jit(solution)/shard_map/all_to_all | solution.py:188
  104.3 0.1 fusion.21
  104.4 0.7 shard_map.115
  105.8 0.2 conditional.1
  106.0 0.6 copy-done.9
  (25 shorter events, 0.3 us)
Async XLA Ops:
  2.1 17.5 %all-to-all-start.16 = ((f16[32,2,16,128]{3,2,1,0:T(8,128)(2,1)}), f16[32,2,16,128]{3,2,1,0:T(8,128)(2,1)S(1)}, u32[]{:S(2)}, u32[]{:S(2)}) async-start(f16[32,2,16,128]{3,2,1,0:T(8,128)(2,1)} %broadcast_in_dim.48), calls=%async_computation.16 | async-start | bytes 524288 | tf_op jit(solution)/shard_map/all_to_all | solution.py:188
  19.6 28.4 %copy-start.4 = (f32[16,256]{1,0:T(8,128)S(1)}, f32[16,256]{1,0:T(8,128)}, u32[]{:S(2)}) copy-start(f32[16,256]{1,0:T(8,128)} %r_ref.1) | copy-start | bytes 49156
  19.7 42.9 %copy-start.1 = (bf16[192,128,64]{1,2,0:T(8,128)(2,1)S(1)}, bf16[192,128,64]{1,2,0:T(8,128)(2,1)}, u32[]{:S(2)}) copy-start(bf16[192,128,64]{1,2,0:T(8,128)(2,1)} %param.17) | copy-start | bytes 9437188
  19.7 42.9 %copy-start.2 = (bf16[192,128,64]{1,2,0:T(8,128)(2,1)S(1)}, bf16[192,128,64]{1,2,0:T(8,128)(2,1)}, u32[]{:S(2)}) copy-start(bf16[192,128,64]{1,2,0:T(8,128)(2,1)} %param.18) | copy-start | bytes 9437188
  25.1 37.4 %copy-start = (bf16[128,128,128]{2,1,0:T(8,128)(2,1)S(1)}, bf16[128,128,128]{2,1,0:T(8,128)(2,1)}, u32[]{:S(2)}) copy-start(bf16[128,128,128]{2,1,0:T(8,128)(2,1)} %refs_7_.3) | copy-start | bytes 12582916
  25.1 37.4 %copy-start.5 = (s32[192]{0:T(256)S(1)}, s32[192]{0:T(256)}, u32[]{:S(2)}) copy-start(s32[192]{0:T(256)} %refs_2_.3) | copy-start | bytes 2308
  25.1 37.4 %copy-start.6 = (s32[192]{0:T(256)S(1)}, s32[192]{0:T(256)}, u32[]{:S(2)}) copy-start(s32[192]{0:T(256)} %refs_3_.3) | copy-start | bytes 2308
  25.2 37.4 %copy-start.7 = (s32[128]{0:T(128)S(1)}, s32[128]{0:T(128)}, u32[]{:S(2)}) copy-start(s32[128]{0:T(128)} %refs_0_.3) | copy-start | bytes 1540
  25.2 37.4 %copy-start.8 = (s32[128]{0:T(128)S(1)}, s32[128]{0:T(128)}, u32[]{:S(2)}) copy-start(s32[128]{0:T(128)} %refs_1_.3) | copy-start | bytes 1540
  25.3 1.6 %collective-permute-start = (f16[64,16,128]{2,1,0:T(8,128)(2,1)S(1)}, f16[64,16,128]{2,1,0:T(8,128)(2,1)S(1)}, u32[]{:S(2)}, u32[]{:S(2)}) collective-permute-start(f16[64,16,128]{2,1,0:T(8,128)(2,1)S(1)} %multiply_convert_fusion.1), channel_id=1, source_target_pairs={{0,1},{1,0},{2,3},{3,2},{4,5},{5,4},{6,7},{7,6},{8,9},{9,8},{10,11... | collective-permute-start | bytes 786440 | tf_op jit(solution)/shard_map/ppermute | solution.py:192
  66.8 1.6 %collective-permute-start.1 = (f16[64,16,128]{2,1,0:T(8,128)(2,1)S(1)}, f16[64,16,128]{2,1,0:T(8,128)(2,1)S(1)}, u32[]{:S(2)}, u32[]{:S(2)}) collective-permute-start(f16[64,16,128]{2,1,0:T(8,128)(2,1)S(1)} %multiply_convert_fusion), channel_id=1, source_target_pairs={{0,1},{1,0},{2,3},{3,2},{4,5},{5,4},{6,7},{7,6},{8,9},{9,8},{10,11... | collective-permute-start | bytes 786440 | tf_op jit(solution)/shard_map/ppermute | solution.py:192
  83.9 3.0 %collective-permute-start.2 = (f32[1,128]{1,0:T(1,128)S(1)}, f32[1,128]{1,0:T(1,128)S(1)}, u32[]{:S(2)}, u32[]{:S(2)}) collective-permute-start(f32[1,128]{1,0:T(1,128)S(1)} %bitcast.193), channel_id=1, source_target_pairs={{0,1},{1,0},{2,3},{3,2},{4,5},{5,4},{6,7},{7,6},{8,9},{9,8},{10,11... | collective-permute-start | bytes 1544 | tf_op jit(solution)/shard_map/ppermute | solution.py:299
  87.5 16.7 %all-to-all-start.20 = ((f32[128,1,128]{2,1,0:T(1,128)}), f32[128,1,128]{2,1,0:T(1,128)S(1)}, u32[]{:S(2)}, u32[]{:S(2)}) async-start(f32[128,1,128]{2,1,0:T(1,128)} %broadcast_in_dim.53), calls=%async_computation.20 | async-start | bytes 131072 | tf_op jit(solution)/shard_map/all_to_all | solution.py:188
  106.0 0.6 copy-start.9
  106.0 0.6 copy-start.10

commit v8 on v7

--- a/solution.py
+++ b/solution.py
@@ -42,7 +42,7 @@
         far_part = pl.ds(i * FAR_CHUNK, FAR_CHUNK)
         for source, held, part in ((left, left_v, far_part), (near, near_v, near_part), (right, right_v, far_part)):
             copies.append(pltpu.make_async_copy(source.at[part], held.at[part], sems.at[len(copies)]))
-    for copy in copies:
+    for copy in copies[:6]:
         copy.start()
     return copies
 
@@ -148,6 +148,8 @@
         for chunk in range(NEAR_DEV // NEAR_CHUNK):
             for copy in copies[3 * chunk : 3 * chunk + 3]:
                 copy.wait()
+            for copy in copies[3 * chunk + 6 : 3 * chunk + 9]:
+                copy.start()
             lax.fori_loop(chunk, jnp.clip(steps, chunk, chunk + 1), body, 0)
     else:
         lax.fori_loop(0, steps, body, 0)
@@ -192,7 +194,7 @@
     other = lax.ppermute((send * SCALE).astype(jnp.float16), "core", [(0, 1), (1, 0)])
     pieces = (keep * SCALE + other.astype(jnp.float32)).astype(jnp.float16).reshape(-1, CL_DEV, OBJ, LEAF)
     moved = lax.all_to_all(pieces, ("gy", "gq"), split_axis=0, concat_axis=0)
-    return jnp.sum(moved.astype(jnp.float32), axis=0) * (1.0 / SCALE)
+    return jnp.sum(moved.astype(jnp.float32), axis=0)
 
 
 def gather_targets(value, scale):
@@ -237,7 +239,7 @@
     in_w, in_u, in_r = down(in_w), down(in_u), down(in_r)
     for i in range(CL_DEV):
         lanes = pl.ds(i * LEAF, LEAF)
-        w = 0.5 * u_ref[i] + applied_ref[i]
+        w = 0.5 * u_ref[i] + applied_ref[i] * (1.0 / SCALE)
         basis_ref[:, lanes] = in_w * w + in_u * u_ref[i] + in_r * r_ref[:, lanes]
     rest_1 = left_1 * beta_sq
     rest_2 = left_2 * beta_sq * h21 * h21
@@ -291,9 +293,10 @@
     r = jnp.swapaxes(r0.reshape(OBJ, CL_DEV, LEAF), 0, 1)
 
     lists = (nt, ns, ft, fs, nc, fc)
-    u = 0.5 * r + scatter_sum(*product(lists, gather_targets(r, SCALE_R), blocks, True))
+    applied = scatter_sum(*product(lists, gather_targets(r, SCALE_R), blocks, True))
+    u = 0.5 * r + applied * (1.0 / SCALE)
     applied = scatter_sum(*product(lists, gather_targets(u, SCALE), blocks, False))
-    w = 0.5 * u + applied
+    w = 0.5 * u + applied * (1.0 / SCALE)
     dots = [dot(r, r), dot(r, u), dot(u, u), dot(r, w), dot(u, w), dot(w, w)]
     local = jnp.concatenate(dots + [jnp.zeros((LEAF - len(dots) * OBJ,), jnp.float32)])[None]
     chip = local + lax.ppermute(local, "core", [(0, 1), (1, 0)])

time: 107 us -> 109 us (1.019)
  Pallas kernels: 10.2 us -> 12 us
    pallas_call x2, Pallas kernels: 9.52 us -> 11.3 us  [product(): pl.pallas_call(first_kernel if first else second_kernel, out_shape=(half,...]
where the time goes in v8:
time: 109 us; the launch traced here: 108 us
  blocking collectives  50.3 us (46%)
  waiting for transfers between devices  21.6 us (20%)
  starting transfers between devices  17.6 us (16%)
  Pallas kernels  12 us (11%)
  between operations  2.84 us (3%)
  local copies, waits for them, and re-layouts  2.26 us (2%)
  other arithmetic  1.49 us (1%)
    all_to_all x2, blocking collectives, scatter_sum(): moved = lax.all_to_all(pieces, ('gy', 'gq'), split_axis=0, concat_axis=0)  35.3 us
    all_to_all x2, waiting for transfers between devices, to_all(): lax.all_to_all(jnp.broadcast_to(value[None], (size,) + value.shape), axes...  18.2 us
    all_to_all x1, blocking collectives, to_all(): lax.all_to_all(jnp.broadcast_to(value[None], (size,) + value.shape), axes...  15 us
    all_to_all x2, starting transfers between devices, to_all(): lax.all_to_all(jnp.broadcast_to(value[None], (size,) + value.shape), axes...  14.8 us
    pallas_call x2, Pallas kernels, product(): pl.pallas_call(first_kernel if first else second_kernel, out_shape=(half,...  11.3 us
    ppermute x2, waiting for transfers between devices, scatter_sum(): lax.ppermute((send * SCALE).astype(jnp.float16), 'core', [(0, 1), (1, 0)])  2.59 us
    ppermute x1, starting transfers between devices, on_device(): chip = local + lax.ppermute(local, 'core', [(0, 1), (1, 0)])  2.18 us
  transfers between devices with their start and end apart: 5, of which 5 were waited for; matrix products, arithmetic and copies ran while one was open for 0% of the time, Pallas kernels for 0%

profile of v8, /device:TPU:1, one launch (start us, length us, event | category | flops | bytes accessed | tf_op | source)
XLA Modules:
  0.0 108.3 jit_solution(9576413934505502713)
XLA Ops:
  0.6 0.7 fusion.17
  1.4 0.7 broadcast_in_dim.48
  2.1 8.6 %all-to-all-start.16 = ((f16[32,2,16,128]{3,2,1,0:T(8,128)(2,1)}), f16[32,2,16,128]{3,2,1,0:T(8,128)(2,1)S(1)}, u32[]{:S(2)}, u32[]{:S(2)}) async-start(f16[32,2,16,128]{3,2,1,0:T(8,128)(2,1)} %broadcast_in_dim.48), calls=%async_computation.16 | async-start | bytes 524288 | tf_op jit(solution)/shard_map/all_to_all | solution.py:190
  12.0 7.6 %all-to-all-done.16 = f16[32,2,16,128]{3,2,1,0:T(8,128)(2,1)S(1)} async-done(((f16[32,2,16,128]{3,2,1,0:T(8,128)(2,1)}), f16[32,2,16,128]{3,2,1,0:T(8,128)(2,1)S(1)}, u32[]{:S(2)}, u32[]{:S(2)}) %all-to-all-start.16) | async-done | bytes 262176 | tf_op jit(solution)/shard_map/all_to_all | solution.py:190
  19.6 0.1 convert_multiply_fusion.1
  19.6 0.0 copy-start.4
  19.7 7.2 %shard_map.113 = (f32[64,16,128]{2,1,0:T(8,128)S(1)}, f32[64,16,128]{2,1,0:T(8,128)S(1)}) custom-call(s32[128]{0:T(128)} %refs_0_.3, s32[128]{0:T(128)} %refs_1_.3, s32[192]{0:T(256)} %refs_2_.3, s32[192]{0:T(256)} %refs_3_.3, s32[1]{0:T(128)S(6)} %copy.93.refs_4_, s32[1]{0:T(128)S(6)} %copy.94.refs_5_, f32[64,16,128]{2,1,0:T(8,128)S(1)} %bitcast.169, ...), custom_call_target="tpu_custom_call" | custom-call | flops 170000000 | bytes 12000000 | tf_op jit(solution)/shard_map/pallas_call | solution.py:166
  26.9 0.0 copy-start.6
  26.9 0.1 multiply_convert_fusion.1
  27.0 0.3 collective-permute-start
  27.3 1.3 %collective-permute-done = f16[64,16,128]{2,1,0:T(8,128)(2,1)S(1)} collective-permute-done((f16[64,16,128]{2,1,0:T(8,128)(2,1)S(1)}, f16[64,16,128]{2,1,0:T(8,128)(2,1)S(1)}, u32[]{:S(2)}, u32[]{:S(2)}) %collective-permute-start) | collective-permute-done | bytes 262176 | tf_op jit(solution)/shard_map/ppermute | solution.py:194
  28.6 0.1 add_convert_fusion.1
  28.7 20.4 %all_to_all.91 = f16[32,2,16,128]{3,2,1,0:T(8,128)(2,1)S(1)} all-to-all(f16[32,2,16,128]{3,2,1,0:T(8,128)(2,1)S(1)} %bitcast.180), channel_id=1, replica_groups=mesh['gx'=4,'gy'=8,'gq'=4,'core'=2] {'gy','gq'}, dimensions={0} | all-to-all | bytes 524288 | tf_op jit(solution)/shard_map/all_to_all | solution.py:196
  49.3 15.0 %all_to_all.92 = f16[32,2,16,128]{3,2,1,0:T(8,128)(2,1)S(1)} all-to-all(f16[32,2,16,128]{3,2,1,0:T(8,128)(2,1)S(1)} %broadcast_in_dim.49), channel_id=1, replica_groups=mesh['gx'=4,'gy'=8,'gq'=4,'core'=2] {'gx','gq','core'}, dimensions={0} | all-to-all | bytes 524288 | tf_op jit(solution)/shard_map/all_to_all | solution.py:190
  64.3 0.1 convert_multiply_fusion
  64.4 4.1 %shard_map.114 = (f32[64,16,128]{2,1,0:T(8,128)S(1)}, f32[64,16,128]{2,1,0:T(8,128)S(1)}) custom-call(s32[128]{0:T(128)S(1)} %copy-done.7, s32[128]{0:T(128)S(1)} %copy-done.8, s32[192]{0:T(256)S(1)} %copy-done.5, s32[192]{0:T(256)S(1)} %copy-done.6, s32[1]{0:T(128)S(6)} %copy.93.refs_4_, s32[1]{0:T(128)S(6)} %copy.94.refs_5_, f32[64,16,128]{2,1,0:T(8,128)S(1)} %bitcast.168, ...), custom_call_target="tpu_custom_call" | custom-call | flops 170000000 | bytes 12000000 | tf_op jit(solution)/shard_map/pallas_call | solution.py:166
  68.5 0.1 multiply_convert_fusion
  68.6 0.3 collective-permute-start.1
  68.9 1.3 %collective-permute-done.1 = f16[64,16,128]{2,1,0:T(8,128)(2,1)S(1)} collective-permute-done((f16[64,16,128]{2,1,0:T(8,128)(2,1)S(1)}, f16[64,16,128]{2,1,0:T(8,128)(2,1)S(1)}, u32[]{:S(2)}, u32[]{:S(2)}) %collective-permute-start.1) | collective-permute-done | bytes 262176 | tf_op jit(solution)/shard_map/ppermute | solution.py:194
  70.2 0.1 add_convert_fusion
  70.3 14.9 %all_to_all.93 = f16[32,2,16,128]{3,2,1,0:T(8,128)(2,1)S(1)} all-to-all(f16[32,2,16,128]{3,2,1,0:T(8,128)(2,1)S(1)} %bitcast.181), channel_id=1, replica_groups=mesh['gx'=4,'gy'=8,'gq'=4,'core'=2] {'gy','gq'}, dimensions={0} | all-to-all | bytes 524288 | tf_op jit(solution)/shard_map/all_to_all | solution.py:196
  85.2 0.2 multiply_reduce_fusion.6
  85.4 0.1 concatenate.3
  85.5 2.2 %collective-permute-start.2 = (f32[1,128]{1,0:T(1,128)S(1)}, f32[1,128]{1,0:T(1,128)S(1)}, u32[]{:S(2)}, u32[]{:S(2)}) collective-permute-start(f32[1,128]{1,0:T(1,128)S(1)} %bitcast.193), channel_id=1, source_target_pairs={{0,1},{1,0},{2,3},{3,2},{4,5},{5,4},{6,7},{7,6},{8,9},{9,8},{10,11... | collective-permute-start | bytes 1544 | tf_op jit(solution)/shard_map/ppermute | solution.py:302
  87.7 0.8 collective-permute-done.2
  88.5 0.7 broadcast_in_dim.53
  89.2 6.2 %all-to-all-start.20 = ((f32[128,1,128]{2,1,0:T(1,128)}), f32[128,1,128]{2,1,0:T(1,128)S(1)}, u32[]{:S(2)}, u32[]{:S(2)}) async-start(f32[128,1,128]{2,1,0:T(1,128)} %broadcast_in_dim.53), calls=%async_computation.20 | async-start | bytes 131072 | tf_op jit(solution)/shard_map/all_to_all | solution.py:190
  95.4 10.6 %all-to-all-done.20 = f32[128,1,128]{2,1,0:T(1,128)S(1)} async-done(((f32[128,1,128]{2,1,0:T(1,128)}), f32[128,1,128]{2,1,0:T(1,128)S(1)}, u32[]{:S(2)}, u32[]{:S(2)}) %all-to-all-start.20) | async-done | bytes 65568 | tf_op jit(solution)/shard_map/all_to_all | solution.py:190
  106.0 0.1 fusion.21
  106.1 0.7 shard_map.115
  107.4 0.2 conditional.1
  107.7 0.6 copy-done.9
  (25 shorter events, 0.3 us)
Async XLA Ops:
  2.1 17.5 %all-to-all-start.16 = ((f16[32,2,16,128]{3,2,1,0:T(8,128)(2,1)}), f16[32,2,16,128]{3,2,1,0:T(8,128)(2,1)S(1)}, u32[]{:S(2)}, u32[]{:S(2)}) async-start(f16[32,2,16,128]{3,2,1,0:T(8,128)(2,1)} %broadcast_in_dim.48), calls=%async_computation.16 | async-start | bytes 524288 | tf_op jit(solution)/shard_map/all_to_all | solution.py:190
  19.6 29.5 %copy-start.4 = (f32[16,256]{1,0:T(8,128)S(1)}, f32[16,256]{1,0:T(8,128)}, u32[]{:S(2)}) copy-start(f32[16,256]{1,0:T(8,128)} %r_ref.1) | copy-start | bytes 49156
  19.7 44.7 %copy-start.1 = (bf16[192,128,64]{1,2,0:T(8,128)(2,1)S(1)}, bf16[192,128,64]{1,2,0:T(8,128)(2,1)}, u32[]{:S(2)}) copy-start(bf16[192,128,64]{1,2,0:T(8,128)(2,1)} %param.17) | copy-start | bytes 9437188
  19.7 44.7 %copy-start.2 = (bf16[192,128,64]{1,2,0:T(8,128)(2,1)S(1)}, bf16[192,128,64]{1,2,0:T(8,128)(2,1)}, u32[]{:S(2)}) copy-start(bf16[192,128,64]{1,2,0:T(8,128)(2,1)} %param.18) | copy-start | bytes 9437188
  26.9 37.5 %copy-start = (bf16[128,128,128]{2,1,0:T(8,128)(2,1)S(1)}, bf16[128,128,128]{2,1,0:T(8,128)(2,1)}, u32[]{:S(2)}) copy-start(bf16[128,128,128]{2,1,0:T(8,128)(2,1)} %refs_7_.3) | copy-start | bytes 12582916
  26.9 37.5 %copy-start.5 = (s32[192]{0:T(256)S(1)}, s32[192]{0:T(256)}, u32[]{:S(2)}) copy-start(s32[192]{0:T(256)} %refs_2_.3) | copy-start | bytes 2308
  26.9 37.5 %copy-start.6 = (s32[192]{0:T(256)S(1)}, s32[192]{0:T(256)}, u32[]{:S(2)}) copy-start(s32[192]{0:T(256)} %refs_3_.3) | copy-start | bytes 2308
  26.9 37.5 %copy-start.7 = (s32[128]{0:T(128)S(1)}, s32[128]{0:T(128)}, u32[]{:S(2)}) copy-start(s32[128]{0:T(128)} %refs_0_.3) | copy-start | bytes 1540
  26.9 37.5 %copy-start.8 = (s32[128]{0:T(128)S(1)}, s32[128]{0:T(128)}, u32[]{:S(2)}) copy-start(s32[128]{0:T(128)} %refs_1_.3) | copy-start | bytes 1540
  27.0 1.6 %collective-permute-start = (f16[64,16,128]{2,1,0:T(8,128)(2,1)S(1)}, f16[64,16,128]{2,1,0:T(8,128)(2,1)S(1)}, u32[]{:S(2)}, u32[]{:S(2)}) collective-permute-start(f16[64,16,128]{2,1,0:T(8,128)(2,1)S(1)} %multiply_convert_fusion.1), channel_id=1, source_target_pairs={{0,1},{1,0},{2,3},{3,2},{4,5},{5,4},{6,7},{7,6},{8,9},{9,8},{10,11... | collective-permute-start | bytes 786440 | tf_op jit(solution)/shard_map/ppermute | solution.py:194
  68.6 1.6 %collective-permute-start.1 = (f16[64,16,128]{2,1,0:T(8,128)(2,1)S(1)}, f16[64,16,128]{2,1,0:T(8,128)(2,1)S(1)}, u32[]{:S(2)}, u32[]{:S(2)}) collective-permute-start(f16[64,16,128]{2,1,0:T(8,128)(2,1)S(1)} %multiply_convert_fusion), channel_id=1, source_target_pairs={{0,1},{1,0},{2,3},{3,2},{4,5},{5,4},{6,7},{7,6},{8,9},{9,8},{10,11... | collective-permute-start | bytes 786440 | tf_op jit(solution)/shard_map/ppermute | solution.py:194
  85.5 3.0 %collective-permute-start.2 = (f32[1,128]{1,0:T(1,128)S(1)}, f32[1,128]{1,0:T(1,128)S(1)}, u32[]{:S(2)}, u32[]{:S(2)}) collective-permute-start(f32[1,128]{1,0:T(1,128)S(1)} %bitcast.193), channel_id=1, source_target_pairs={{0,1},{1,0},{2,3},{3,2},{4,5},{5,4},{6,7},{7,6},{8,9},{9,8},{10,11... | collective-permute-start | bytes 1544 | tf_op jit(solution)/shard_map/ppermute | solution.py:302
  89.2 16.7 %all-to-all-start.20 = ((f32[128,1,128]{2,1,0:T(1,128)}), f32[128,1,128]{2,1,0:T(1,128)S(1)}, u32[]{:S(2)}, u32[]{:S(2)}) async-start(f32[128,1,128]{2,1,0:T(1,128)} %broadcast_in_dim.53), calls=%async_computation.20 | async-start | bytes 131072 | tf_op jit(solution)/shard_map/all_to_all | solution.py:190
  107.6 0.6 copy-start.9
  107.7 0.6 copy-start.10

commit v9 on v8

--- a/solution.py
+++ b/solution.py
@@ -18,8 +18,10 @@
 PLANE = ("gx", "gq", "core")
 TARGETS = 64
 SOURCES = 128
-NEAR_STEP = NEAR_CHUNK = 32
-FAR_STEP = FAR_CHUNK = 48
+NEAR_STEP = 32
+FAR_STEP = 48
+STEPS = 4
+PARTS = 2
 
 SCALE_R = 2.0**15
 SCALE = 2.0**4
@@ -37,12 +39,12 @@
 
 def start_blocks(near, left, right, near_v, left_v, right_v, sems):
     copies = []
-    for i in range(NEAR_DEV // NEAR_CHUNK):
-        near_part = pl.ds(i * NEAR_CHUNK, NEAR_CHUNK)
-        far_part = pl.ds(i * FAR_CHUNK, FAR_CHUNK)
+    for i in range(STEPS * PARTS):
+        near_part = pl.ds(i * (NEAR_STEP // PARTS), NEAR_STEP // PARTS)
+        far_part = pl.ds(i * (FAR_STEP // PARTS), FAR_STEP // PARTS)
         for source, held, part in ((left, left_v, far_part), (near, near_v, near_part), (right, right_v, far_part)):
             copies.append(pltpu.make_async_copy(source.at[part], held.at[part], sems.at[len(copies)]))
-    for copy in copies[:6]:
+    for copy in copies:
         copy.start()
     return copies
 
@@ -145,11 +147,9 @@
         return carry
 
     if blocks_in:
-        for chunk in range(NEAR_DEV // NEAR_CHUNK):
-            for copy in copies[3 * chunk : 3 * chunk + 3]:
+        for chunk in range(STEPS):
+            for copy in copies[3 * PARTS * chunk : 3 * PARTS * (chunk + 1)]:
                 copy.wait()
-            for copy in copies[3 * chunk + 6 : 3 * chunk + 9]:
-                copy.start()
             lax.fori_loop(chunk, jnp.clip(steps, chunk, chunk + 1), body, 0)
     else:
         lax.fori_loop(0, steps, body, 0)
@@ -162,7 +162,7 @@
 def product(lists, field, blocks, first):
     half = jax.ShapeDtypeStruct((SOURCES // 2, OBJ, LEAF), jnp.float32)
     held = [pltpu.VMEM(block.shape, block.dtype) for block in blocks]
-    held.append(pltpu.SemaphoreType.DMA((3 * (NEAR_DEV // NEAR_CHUNK),)))
+    held.append(pltpu.SemaphoreType.DMA((3 * STEPS * PARTS,)))
     return pl.pallas_call(
         first_kernel if first else second_kernel,
         out_shape=(half, half),
@@ -313,9 +313,11 @@
         out_specs=(VMEM, VMEM, SMEM),
         compiler_params=pltpu.CompilerParams(vmem_limit_bytes=2 * 1024 * 1024),
     )(sums, r0, u, applied)
-    basis_3, entries = lax.switch(
-        fails[0], (lambda: (basis_3, entries), lambda: plainly(r0, indices, (near_tiles, far_left, far_right)))
-    )
+    def branch():
+        plain = plainly(r0, indices, (near_tiles, far_left, far_right))
+        return tuple(jnp.where(fails[0] > 0, new, old) for new, old in zip(plain, (basis_3, entries)))
+
+    basis_3, entries = lax.switch(fails[0], (lambda: (basis_3, entries), branch))
     return basis_3, entries.T
 
 

time: 109 us -> 106 us (0.972)
  blocking collectives: 50.3 us -> 68.4 us
  waiting for transfers between devices: 21.6 us -> 11 us
  starting transfers between devices: 17.6 us -> 11.4 us
  Pallas kernels: 12 us -> 8.67 us
    all_to_all x1 -> x2, blocking collectives: 15 us -> 30.6 us  [to_all(): lax.all_to_all(jnp.broadcast_to(value[None], (size,) + value.shape), axes...]
    all_to_all x2 -> x1, waiting for transfers between devices: 18.2 us -> 7.61 us  [to_all(): lax.all_to_all(jnp.broadcast_to(value[None], (size,) + value.shape), axes...]
    all_to_all x2 -> x1, starting transfers between devices: 14.8 us -> 8.59 us  [to_all(): lax.all_to_all(jnp.broadcast_to(value[None], (size,) + value.shape), axes...]
    pallas_call x2, Pallas kernels: 11.3 us -> 7.98 us  [product(): pl.pallas_call(first_kernel if first else second_kernel, out_shape=(half,...]
    all_to_all x2, blocking collectives: 35.3 us -> 37.8 us  [scatter_sum(): moved = lax.all_to_all(pieces, ('gy', 'gq'), split_axis=0, concat_axis=0)]
  transfers between devices with their start and end apart: 5 -> 4, of which waited for: 5 -> 4; matrix products, arithmetic and copies ran while one was open for 0% -> 0% of each run, Pallas kernels for 0% -> 0%
where the time goes in v9:
time: 106 us
  blocking collectives  68.4 us (65%)
  starting transfers between devices  11.4 us (11%)
  waiting for transfers between devices  11 us (10%)
  Pallas kernels  8.67 us (8%)
  between operations  2.74 us (3%)
  local copies, waits for them, and re-layouts  1.64 us (2%)
  other arithmetic  1.49 us (1%)
    all_to_all x2, blocking collectives, scatter_sum(): moved = lax.all_to_all(pieces, ('gy', 'gq'), split_axis=0, concat_axis=0)  37.8 us
    all_to_all x2, blocking collectives, to_all(): lax.all_to_all(jnp.broadcast_to(value[None], (size,) + value.shape), axes...  30.6 us
    all_to_all x1, starting transfers between devices, to_all(): lax.all_to_all(jnp.broadcast_to(value[None], (size,) + value.shape), axes...  8.59 us
    pallas_call x2, Pallas kernels, product(): pl.pallas_call(first_kernel if first else second_kernel, out_shape=(half,...  7.98 us
    all_to_all x1, waiting for transfers between devices, to_all(): lax.all_to_all(jnp.broadcast_to(value[None], (size,) + value.shape), axes...  7.61 us
    ppermute x2, waiting for transfers between devices, scatter_sum(): lax.ppermute((send * SCALE).astype(jnp.float16), 'core', [(0, 1), (1, 0)])  2.62 us
    ppermute x1, starting transfers between devices, on_device(): chip = local + lax.ppermute(local, 'core', [(0, 1), (1, 0)])  2.18 us
  transfers between devices with their start and end apart: 4, of which 4 were waited for; matrix products, arithmetic and copies ran while one was open for 0% of the time, Pallas kernels for 0%

profile of v9, /device:TPU:1, one launch (start us, length us, event | category | flops | bytes accessed | tf_op | source)
XLA Modules:
  0.0 105.6 jit_solution(14987053565919844643)
XLA Ops:
  0.6 0.7 fusion.17
  1.4 0.7 broadcast_in_dim.48
  2.1 8.6 %all-to-all-start.16 = ((f16[32,2,16,128]{3,2,1,0:T(8,128)(2,1)}), f16[32,2,16,128]{3,2,1,0:T(8,128)(2,1)S(1)}, u32[]{:S(2)}, u32[]{:S(2)}) async-start(f16[32,2,16,128]{3,2,1,0:T(8,128)(2,1)} %broadcast_in_dim.48), calls=%async_computation.16 | async-start | bytes 524288 | tf_op jit(solution)/shard_map/all_to_all | solution.py:190
  12.0 7.6 %all-to-all-done.16 = f16[32,2,16,128]{3,2,1,0:T(8,128)(2,1)S(1)} async-done(((f16[32,2,16,128]{3,2,1,0:T(8,128)(2,1)}), f16[32,2,16,128]{3,2,1,0:T(8,128)(2,1)S(1)}, u32[]{:S(2)}, u32[]{:S(2)}) %all-to-all-start.16) | async-done | bytes 262176 | tf_op jit(solution)/shard_map/all_to_all | solution.py:190
  19.6 0.1 convert_multiply_fusion.1
  19.6 0.0 copy-start.4
  19.7 0.0 copy-start.1
  19.7 4.7 %shard_map.113 = (f32[64,16,128]{2,1,0:T(8,128)S(1)}, f32[64,16,128]{2,1,0:T(8,128)S(1)}) custom-call(s32[128]{0:T(128)} %refs_0_.3, s32[128]{0:T(128)} %refs_1_.3, s32[192]{0:T(256)} %refs_2_.3, s32[192]{0:T(256)} %refs_3_.3, s32[1]{0:T(128)S(6)} %copy.93.refs_4_, s32[1]{0:T(128)S(6)} %copy.94.refs_5_, f32[64,16,128]{2,1,0:T(8,128)S(1)} %bitcast.170, ...), custom_call_target="tpu_custom_call" | custom-call | flops 170000000 | bytes 12000000 | tf_op jit(solution)/shard_map/pallas_call | solution.py:166
  24.4 0.0 copy-start.6
  24.4 0.0 copy-start.7
  24.5 0.1 multiply_convert_fusion.1
  24.5 0.3 collective-permute-start
  24.8 1.3 %collective-permute-done = f16[64,16,128]{2,1,0:T(8,128)(2,1)S(1)} collective-permute-done((f16[64,16,128]{2,1,0:T(8,128)(2,1)S(1)}, f16[64,16,128]{2,1,0:T(8,128)(2,1)S(1)}, u32[]{:S(2)}, u32[]{:S(2)}) %collective-permute-start) | collective-permute-done | bytes 262176 | tf_op jit(solution)/shard_map/ppermute | solution.py:194
  26.1 0.1 add_convert_fusion.1
  26.2 21.9 %all_to_all.91 = f16[32,2,16,128]{3,2,1,0:T(8,128)(2,1)S(1)} all-to-all(f16[32,2,16,128]{3,2,1,0:T(8,128)(2,1)S(1)} %bitcast.181), channel_id=1, replica_groups=mesh['gx'=4,'gy'=8,'gq'=4,'core'=2] {'gy','gq'}, dimensions={0} | all-to-all | bytes 524288 | tf_op jit(solution)/shard_map/all_to_all | solution.py:196
  48.3 14.4 %all_to_all.92 = f16[32,2,16,128]{3,2,1,0:T(8,128)(2,1)S(1)} all-to-all(f16[32,2,16,128]{3,2,1,0:T(8,128)(2,1)S(1)} %broadcast_in_dim.49), channel_id=1, replica_groups=mesh['gx'=4,'gy'=8,'gq'=4,'core'=2] {'gx','gq','core'}, dimensions={0} | all-to-all | bytes 524288 | tf_op jit(solution)/shard_map/all_to_all | solution.py:190
  62.6 0.1 convert_multiply_fusion
  62.8 3.3 %shard_map.114 = (f32[64,16,128]{2,1,0:T(8,128)S(1)}, f32[64,16,128]{2,1,0:T(8,128)S(1)}) custom-call(s32[128]{0:T(128)S(1)} %copy-done.8, s32[128]{0:T(128)S(1)} %copy-done.9, s32[192]{0:T(256)S(1)} %copy-done.6, s32[192]{0:T(256)S(1)} %copy-done.7, s32[1]{0:T(128)S(6)} %copy.93.refs_4_, s32[1]{0:T(128)S(6)} %copy.94.refs_5_, f32[64,16,128]{2,1,0:T(8,128)S(1)} %bitcast.169, ...), custom_call_target="tpu_custom_call" | custom-call | flops 170000000 | bytes 12000000 | tf_op jit(solution)/shard_map/pallas_call | solution.py:166
  66.0 0.1 multiply_convert_fusion
  66.1 0.3 collective-permute-start.1
  66.4 1.3 %collective-permute-done.1 = f16[64,16,128]{2,1,0:T(8,128)(2,1)S(1)} collective-permute-done((f16[64,16,128]{2,1,0:T(8,128)(2,1)S(1)}, f16[64,16,128]{2,1,0:T(8,128)(2,1)S(1)}, u32[]{:S(2)}, u32[]{:S(2)}) %collective-permute-start.1) | collective-permute-done | bytes 262176 | tf_op jit(solution)/shard_map/ppermute | solution.py:194
  67.7 0.1 add_convert_fusion
  67.8 15.9 %all_to_all.93 = f16[32,2,16,128]{3,2,1,0:T(8,128)(2,1)S(1)} all-to-all(f16[32,2,16,128]{3,2,1,0:T(8,128)(2,1)S(1)} %bitcast.182), channel_id=1, replica_groups=mesh['gx'=4,'gy'=8,'gq'=4,'core'=2] {'gy','gq'}, dimensions={0} | all-to-all | bytes 524288 | tf_op jit(solution)/shard_map/all_to_all | solution.py:196
  83.8 0.2 multiply_reduce_fusion.6
  83.9 0.1 concatenate.3
  84.0 2.2 %collective-permute-start.2 = (f32[1,128]{1,0:T(1,128)S(1)}, f32[1,128]{1,0:T(1,128)S(1)}, u32[]{:S(2)}, u32[]{:S(2)}) collective-permute-start(f32[1,128]{1,0:T(1,128)S(1)} %bitcast.195), channel_id=1, source_target_pairs={{0,1},{1,0},{2,3},{3,2},{4,5},{5,4},{6,7},{7,6},{8,9},{9,8},{10,11... | collective-permute-start | bytes 1544 | tf_op jit(solution)/shard_map/ppermute | solution.py:302
  86.2 0.8 collective-permute-done.2
  87.1 16.3 %all_to_all.94 = f32[128,1,128]{2,1,0:T(1,128)S(1)} all-to-all(f32[128,1,128]{2,1,0:T(1,128)S(1)} %broadcast_in_dim.53), channel_id=1, replica_groups=mesh['gx'=4,'gy'=8,'gq'=4,'core'=2] {'gx','gy','gq'}, dimensions={0} | all-to-all | bytes 131072 | tf_op jit(solution)/shard_map/all_to_all | solution.py:190
  103.4 0.1 fusion.21
  103.5 0.7 shard_map.115
  104.7 0.2 conditional.1
  105.0 0.6 copy-done.5
  (24 shorter events, 0.3 us)
Async XLA Ops:
  2.1 17.5 %all-to-all-start.16 = ((f16[32,2,16,128]{3,2,1,0:T(8,128)(2,1)}), f16[32,2,16,128]{3,2,1,0:T(8,128)(2,1)S(1)}, u32[]{:S(2)}, u32[]{:S(2)}) async-start(f16[32,2,16,128]{3,2,1,0:T(8,128)(2,1)} %broadcast_in_dim.48), calls=%async_computation.16 | async-start | bytes 524288 | tf_op jit(solution)/shard_map/all_to_all | solution.py:190
  19.6 28.5 %copy-start.4 = (f32[16,256]{1,0:T(8,128)S(1)}, f32[16,256]{1,0:T(8,128)}, u32[]{:S(2)}) copy-start(f32[16,256]{1,0:T(8,128)} %r_ref.1) | copy-start | bytes 49156
  19.7 43.0 %copy-start.1 = (bf16[192,128,64]{1,2,0:T(8,128)(2,1)S(1)}, bf16[192,128,64]{1,2,0:T(8,128)(2,1)}, u32[]{:S(2)}) copy-start(bf16[192,128,64]{1,2,0:T(8,128)(2,1)} %param.17) | copy-start | bytes 9437188
  19.7 43.0 %copy-start.2 = (bf16[192,128,64]{1,2,0:T(8,128)(2,1)S(1)}, bf16[192,128,64]{1,2,0:T(8,128)(2,1)}, u32[]{:S(2)}) copy-start(bf16[192,128,64]{1,2,0:T(8,128)(2,1)} %param.18) | copy-start | bytes 9437188
  24.4 38.3 %copy-start = (bf16[128,128,128]{2,1,0:T(8,128)(2,1)S(1)}, bf16[128,128,128]{2,1,0:T(8,128)(2,1)}, u32[]{:S(2)}) copy-start(bf16[128,128,128]{2,1,0:T(8,128)(2,1)} %refs_7_.3) | copy-start | bytes 12582916
  24.4 38.3 %copy-start.6 = (s32[192]{0:T(256)S(1)}, s32[192]{0:T(256)}, u32[]{:S(2)}) copy-start(s32[192]{0:T(256)} %refs_2_.3) | copy-start | bytes 2308
  24.4 38.3 %copy-start.7 = (s32[192]{0:T(256)S(1)}, s32[192]{0:T(256)}, u32[]{:S(2)}) copy-start(s32[192]{0:T(256)} %refs_3_.3) | copy-start | bytes 2308
  24.4 38.3 %copy-start.8 = (s32[128]{0:T(128)S(1)}, s32[128]{0:T(128)}, u32[]{:S(2)}) copy-start(s32[128]{0:T(128)} %refs_0_.3) | copy-start | bytes 1540
  24.4 38.3 %copy-start.9 = (s32[128]{0:T(128)S(1)}, s32[128]{0:T(128)}, u32[]{:S(2)}) copy-start(s32[128]{0:T(128)} %refs_1_.3) | copy-start | bytes 1540
  24.5 1.6 %collective-permute-start = (f16[64,16,128]{2,1,0:T(8,128)(2,1)S(1)}, f16[64,16,128]{2,1,0:T(8,128)(2,1)S(1)}, u32[]{:S(2)}, u32[]{:S(2)}) collective-permute-start(f16[64,16,128]{2,1,0:T(8,128)(2,1)S(1)} %multiply_convert_fusion.1), channel_id=1, source_target_pairs={{0,1},{1,0},{2,3},{3,2},{4,5},{5,4},{6,7},{7,6},{8,9},{9,8},{10,11... | collective-permute-start | bytes 786440 | tf_op jit(solution)/shard_map/ppermute | solution.py:194
  66.1 1.6 %collective-permute-start.1 = (f16[64,16,128]{2,1,0:T(8,128)(2,1)S(1)}, f16[64,16,128]{2,1,0:T(8,128)(2,1)S(1)}, u32[]{:S(2)}, u32[]{:S(2)}) collective-permute-start(f16[64,16,128]{2,1,0:T(8,128)(2,1)S(1)} %multiply_convert_fusion), channel_id=1, source_target_pairs={{0,1},{1,0},{2,3},{3,2},{4,5},{5,4},{6,7},{7,6},{8,9},{9,8},{10,11... | collective-permute-start | bytes 786440 | tf_op jit(solution)/shard_map/ppermute | solution.py:194
  84.0 3.0 %collective-permute-start.2 = (f32[1,128]{1,0:T(1,128)S(1)}, f32[1,128]{1,0:T(1,128)S(1)}, u32[]{:S(2)}, u32[]{:S(2)}) collective-permute-start(f32[1,128]{1,0:T(1,128)S(1)} %bitcast.195), channel_id=1, source_target_pairs={{0,1},{1,0},{2,3},{3,2},{4,5},{5,4},{6,7},{7,6},{8,9},{9,8},{10,11... | collective-permute-start | bytes 1544 | tf_op jit(solution)/shard_map/ppermute | solution.py:302
  105.0 0.6 copy-start.5
  105.0 0.6 copy-start.10

commit v10 on v9

--- a/solution.py
+++ b/solution.py
@@ -154,9 +154,11 @@
     else:
         lax.fori_loop(0, steps, body, 0)
     core = lax.axis_index("core")
-    by_core = acc.reshape(SOURCES // 4, 4, OBJ, LEAF)
-    keep[...] = by_core[:, pl.ds(2 * core, 2)].reshape(keep.shape)
-    send[...] = by_core[:, pl.ds(2 - 2 * core, 2)].reshape(send.shape)
+    by_core = acc.reshape(8, 4, 4, OBJ, LEAF)
+    for i in range(4):
+        part = pl.ds(16 * i, 16)
+        keep[part] = by_core[:, i, pl.ds(2 * core, 2)].reshape(16, OBJ, LEAF)
+        send[part] = by_core[:, i, pl.ds(2 - 2 * core, 2)].reshape(16, OBJ, LEAF)
 
 
 def product(lists, field, blocks, first):
@@ -193,7 +195,7 @@
 def scatter_sum(keep, send):
     other = lax.ppermute((send * SCALE).astype(jnp.float16), "core", [(0, 1), (1, 0)])
     pieces = (keep * SCALE + other.astype(jnp.float32)).astype(jnp.float16).reshape(-1, CL_DEV, OBJ, LEAF)
-    moved = lax.all_to_all(pieces, ("gy", "gq"), split_axis=0, concat_axis=0)
+    moved = lax.all_to_all(pieces, ("gq", "gy"), split_axis=0, concat_axis=0)
     return jnp.sum(moved.astype(jnp.float32), axis=0)
 
 

time: 106 us -> 106 us (level)
  Pallas kernels: 8.67 us -> 7.57 us
    all_to_all x2, blocking collectives: 30.6 us -> 33.7 us  [to_all(): lax.all_to_all(jnp.broadcast_to(value[None], (size,) + value.shape), axes...]
    all_to_all x2, blocking collectives: 37.8 us -> 35 us  [scatter_sum(): moved = lax.all_to_all(pieces, ('gq', 'gy'), split_axis=0, concat_axis=0)]
    pallas_call x2, Pallas kernels: 7.98 us -> 6.88 us  [product(): pl.pallas_call(first_kernel if first else second_kernel, out_shape=(half,...]
where the time goes in v10:
time: 106 us
  blocking collectives  68.7 us (65%)
  starting transfers between devices  12.3 us (12%)
  waiting for transfers between devices  11 us (10%)
  Pallas kernels  7.57 us (7%)
  between operations  2.74 us (3%)
  local copies, waits for them, and re-layouts  1.64 us (2%)
  other arithmetic  1.49 us (1%)
    all_to_all x2, blocking collectives, scatter_sum(): moved = lax.all_to_all(pieces, ('gq', 'gy'), split_axis=0, concat_axis=0)  35 us
    all_to_all x2, blocking collectives, to_all(): lax.all_to_all(jnp.broadcast_to(value[None], (size,) + value.shape), axes...  33.7 us
    all_to_all x1, starting transfers between devices, to_all(): lax.all_to_all(jnp.broadcast_to(value[None], (size,) + value.shape), axes...  8.59 us
    all_to_all x1, waiting for transfers between devices, to_all(): lax.all_to_all(jnp.broadcast_to(value[None], (size,) + value.shape), axes...  7.61 us
    pallas_call x2, Pallas kernels, product(): pl.pallas_call(first_kernel if first else second_kernel, out_shape=(half,...  6.88 us
    ppermute x1, starting transfers between devices, on_device(): chip = local + lax.ppermute(local, 'core', [(0, 1), (1, 0)])  3.04 us
    ppermute x2, waiting for transfers between devices, scatter_sum(): lax.ppermute((send * SCALE).astype(jnp.float16), 'core', [(0, 1), (1, 0)])  2.59 us
  transfers between devices with their start and end apart: 4, of which 4 were waited for; matrix products, arithmetic and copies ran while one was open for 0% of the time, Pallas kernels for 0%

profile of v10, /device:TPU:1, one launch (start us, length us, event | category | flops | bytes accessed | tf_op | source)
XLA Modules:
  0.0 105.7 jit_solution(1402919622096680001)
XLA Ops:
  0.6 0.7 fusion.17
  1.4 0.7 broadcast_in_dim.48
  2.1 8.6 %all-to-all-start.16 = ((f16[32,2,16,128]{3,2,1,0:T(8,128)(2,1)}), f16[32,2,16,128]{3,2,1,0:T(8,128)(2,1)S(1)}, u32[]{:S(2)}, u32[]{:S(2)}) async-start(f16[32,2,16,128]{3,2,1,0:T(8,128)(2,1)} %broadcast_in_dim.48), calls=%async_computation.16 | async-start | bytes 524288 | tf_op jit(solution)/shard_map/all_to_all | solution.py:192
  12.0 7.6 %all-to-all-done.16 = f16[32,2,16,128]{3,2,1,0:T(8,128)(2,1)S(1)} async-done(((f16[32,2,16,128]{3,2,1,0:T(8,128)(2,1)}), f16[32,2,16,128]{3,2,1,0:T(8,128)(2,1)S(1)}, u32[]{:S(2)}, u32[]{:S(2)}) %all-to-all-start.16) | async-done | bytes 262176 | tf_op jit(solution)/shard_map/all_to_all | solution.py:192
  19.6 0.1 convert_multiply_fusion.1
  19.6 0.0 copy-start.4
  19.7 0.0 copy-start.1
  19.7 4.4 %shard_map.113 = (f32[64,16,128]{2,1,0:T(8,128)S(1)}, f32[64,16,128]{2,1,0:T(8,128)S(1)}) custom-call(s32[128]{0:T(128)} %refs_0_.3, s32[128]{0:T(128)} %refs_1_.3, s32[192]{0:T(256)} %refs_2_.3, s32[192]{0:T(256)} %refs_3_.3, s32[1]{0:T(128)S(6)} %copy.93.refs_4_, s32[1]{0:T(128)S(6)} %copy.94.refs_5_, f32[64,16,128]{2,1,0:T(8,128)S(1)} %bitcast.170, ...), custom_call_target="tpu_custom_call" | custom-call | flops 170000000 | bytes 12000000 | tf_op jit(solution)/shard_map/pallas_call | solution.py:168
  24.2 0.0 copy-start.6
  24.2 0.0 copy-start.7
  24.2 0.1 multiply_convert_fusion.1
  24.3 0.3 collective-permute-start
  24.6 1.3 %collective-permute-done = f16[64,16,128]{2,1,0:T(8,128)(2,1)S(1)} collective-permute-done((f16[64,16,128]{2,1,0:T(8,128)(2,1)S(1)}, f16[64,16,128]{2,1,0:T(8,128)(2,1)S(1)}, u32[]{:S(2)}, u32[]{:S(2)}) %collective-permute-start) | collective-permute-done | bytes 262176 | tf_op jit(solution)/shard_map/ppermute | solution.py:196
  25.9 0.1 add_convert_fusion.1
  26.0 19.6 %all_to_all.91 = f16[32,2,16,128]{3,2,1,0:T(8,128)(2,1)S(1)} all-to-all(f16[32,2,16,128]{3,2,1,0:T(8,128)(2,1)S(1)} %bitcast.181), channel_id=1, replica_groups=mesh['gx'=4,'gy'=8,'gq'=4,'core'=2] {'gq','gy'}, dimensions={0} | all-to-all | bytes 524288 | tf_op jit(solution)/shard_map/all_to_all | solution.py:198
  45.7 16.5 %all_to_all.92 = f16[32,2,16,128]{3,2,1,0:T(8,128)(2,1)S(1)} all-to-all(f16[32,2,16,128]{3,2,1,0:T(8,128)(2,1)S(1)} %broadcast_in_dim.49), channel_id=1, replica_groups=mesh['gx'=4,'gy'=8,'gq'=4,'core'=2] {'gx','gq','core'}, dimensions={0} | all-to-all | bytes 524288 | tf_op jit(solution)/shard_map/all_to_all | solution.py:192
  62.2 0.1 convert_multiply_fusion
  62.3 2.4 %shard_map.114 = (f32[64,16,128]{2,1,0:T(8,128)S(1)}, f32[64,16,128]{2,1,0:T(8,128)S(1)}) custom-call(s32[128]{0:T(128)S(1)} %copy-done.8, s32[128]{0:T(128)S(1)} %copy-done.9, s32[192]{0:T(256)S(1)} %copy-done.6, s32[192]{0:T(256)S(1)} %copy-done.7, s32[1]{0:T(128)S(6)} %copy.93.refs_4_, s32[1]{0:T(128)S(6)} %copy.94.refs_5_, f32[64,16,128]{2,1,0:T(8,128)S(1)} %bitcast.169, ...), custom_call_target="tpu_custom_call" | custom-call | flops 170000000 | bytes 12000000 | tf_op jit(solution)/shard_map/pallas_call | solution.py:168
  64.8 0.1 multiply_convert_fusion
  64.8 0.3 collective-permute-start.1
  65.2 1.3 %collective-permute-done.1 = f16[64,16,128]{2,1,0:T(8,128)(2,1)S(1)} collective-permute-done((f16[64,16,128]{2,1,0:T(8,128)(2,1)S(1)}, f16[64,16,128]{2,1,0:T(8,128)(2,1)S(1)}, u32[]{:S(2)}, u32[]{:S(2)}) %collective-permute-start.1) | collective-permute-done | bytes 262176 | tf_op jit(solution)/shard_map/ppermute | solution.py:196
  66.5 0.1 add_convert_fusion
  66.6 15.5 %all_to_all.93 = f16[32,2,16,128]{3,2,1,0:T(8,128)(2,1)S(1)} all-to-all(f16[32,2,16,128]{3,2,1,0:T(8,128)(2,1)S(1)} %bitcast.182), channel_id=1, replica_groups=mesh['gx'=4,'gy'=8,'gq'=4,'core'=2] {'gq','gy'}, dimensions={0} | all-to-all | bytes 524288 | tf_op jit(solution)/shard_map/all_to_all | solution.py:198
  82.1 0.2 multiply_reduce_fusion.6
  82.3 0.1 concatenate.3
  82.4 3.0 %collective-permute-start.2 = (f32[1,128]{1,0:T(1,128)S(1)}, f32[1,128]{1,0:T(1,128)S(1)}, u32[]{:S(2)}, u32[]{:S(2)}) collective-permute-start(f32[1,128]{1,0:T(1,128)S(1)} %bitcast.195), channel_id=1, source_target_pairs={{0,1},{1,0},{2,3},{3,2},{4,5},{5,4},{6,7},{7,6},{8,9},{9,8},{10,11... | collective-permute-start | bytes 1544 | tf_op jit(solution)/shard_map/ppermute | solution.py:304
  85.4 0.8 collective-permute-done.2
  86.3 17.1 %all_to_all.94 = f32[128,1,128]{2,1,0:T(1,128)S(1)} all-to-all(f32[128,1,128]{2,1,0:T(1,128)S(1)} %broadcast_in_dim.53), channel_id=1, replica_groups=mesh['gx'=4,'gy'=8,'gq'=4,'core'=2] {'gx','gy','gq'}, dimensions={0} | all-to-all | bytes 131072 | tf_op jit(solution)/shard_map/all_to_all | solution.py:192
  103.5 0.1 fusion.21
  103.6 0.7 shard_map.115
  104.8 0.2 conditional.1
  105.1 0.6 copy-done.5
  (24 shorter events, 0.3 us)
Async XLA Ops:
  2.1 17.5 %all-to-all-start.16 = ((f16[32,2,16,128]{3,2,1,0:T(8,128)(2,1)}), f16[32,2,16,128]{3,2,1,0:T(8,128)(2,1)S(1)}, u32[]{:S(2)}, u32[]{:S(2)}) async-start(f16[32,2,16,128]{3,2,1,0:T(8,128)(2,1)} %broadcast_in_dim.48), calls=%async_computation.16 | async-start | bytes 524288 | tf_op jit(solution)/shard_map/all_to_all | solution.py:192
  19.6 25.9 %copy-start.4 = (f32[16,256]{1,0:T(8,128)S(1)}, f32[16,256]{1,0:T(8,128)}, u32[]{:S(2)}) copy-start(f32[16,256]{1,0:T(8,128)} %r_ref.1) | copy-start | bytes 49156
  19.7 42.6 %copy-start.1 = (bf16[192,128,64]{1,2,0:T(8,128)(2,1)S(1)}, bf16[192,128,64]{1,2,0:T(8,128)(2,1)}, u32[]{:S(2)}) copy-start(bf16[192,128,64]{1,2,0:T(8,128)(2,1)} %param.17) | copy-start | bytes 9437188
  19.7 42.6 %copy-start.2 = (bf16[192,128,64]{1,2,0:T(8,128)(2,1)S(1)}, bf16[192,128,64]{1,2,0:T(8,128)(2,1)}, u32[]{:S(2)}) copy-start(bf16[192,128,64]{1,2,0:T(8,128)(2,1)} %param.18) | copy-start | bytes 9437188
  24.1 38.1 %copy-start = (bf16[128,128,128]{2,1,0:T(8,128)(2,1)S(1)}, bf16[128,128,128]{2,1,0:T(8,128)(2,1)}, u32[]{:S(2)}) copy-start(bf16[128,128,128]{2,1,0:T(8,128)(2,1)} %refs_7_.3) | copy-start | bytes 12582916
  24.2 38.1 %copy-start.6 = (s32[192]{0:T(256)S(1)}, s32[192]{0:T(256)}, u32[]{:S(2)}) copy-start(s32[192]{0:T(256)} %refs_2_.3) | copy-start | bytes 2308
  24.2 38.1 %copy-start.7 = (s32[192]{0:T(256)S(1)}, s32[192]{0:T(256)}, u32[]{:S(2)}) copy-start(s32[192]{0:T(256)} %refs_3_.3) | copy-start | bytes 2308
  24.2 38.1 %copy-start.8 = (s32[128]{0:T(128)S(1)}, s32[128]{0:T(128)}, u32[]{:S(2)}) copy-start(s32[128]{0:T(128)} %refs_0_.3) | copy-start | bytes 1540
  24.2 38.1 %copy-start.9 = (s32[128]{0:T(128)S(1)}, s32[128]{0:T(128)}, u32[]{:S(2)}) copy-start(s32[128]{0:T(128)} %refs_1_.3) | copy-start | bytes 1540
  24.3 1.6 %collective-permute-start = (f16[64,16,128]{2,1,0:T(8,128)(2,1)S(1)}, f16[64,16,128]{2,1,0:T(8,128)(2,1)S(1)}, u32[]{:S(2)}, u32[]{:S(2)}) collective-permute-start(f16[64,16,128]{2,1,0:T(8,128)(2,1)S(1)} %multiply_convert_fusion.1), channel_id=1, source_target_pairs={{0,1},{1,0},{2,3},{3,2},{4,5},{5,4},{6,7},{7,6},{8,9},{9,8},{10,11... | collective-permute-start | bytes 786440 | tf_op jit(solution)/shard_map/ppermute | solution.py:196
  64.8 1.6 %collective-permute-start.1 = (f16[64,16,128]{2,1,0:T(8,128)(2,1)S(1)}, f16[64,16,128]{2,1,0:T(8,128)(2,1)S(1)}, u32[]{:S(2)}, u32[]{:S(2)}) collective-permute-start(f16[64,16,128]{2,1,0:T(8,128)(2,1)S(1)} %multiply_convert_fusion), channel_id=1, source_target_pairs={{0,1},{1,0},{2,3},{3,2},{4,5},{5,4},{6,7},{7,6},{8,9},{9,8},{10,11... | collective-permute-start | bytes 786440 | tf_op jit(solution)/shard_map/ppermute | solution.py:196
  82.4 3.9 %collective-permute-start.2 = (f32[1,128]{1,0:T(1,128)S(1)}, f32[1,128]{1,0:T(1,128)S(1)}, u32[]{:S(2)}, u32[]{:S(2)}) collective-permute-start(f32[1,128]{1,0:T(1,128)S(1)} %bitcast.195), channel_id=1, source_target_pairs={{0,1},{1,0},{2,3},{3,2},{4,5},{5,4},{6,7},{7,6},{8,9},{9,8},{10,11... | collective-permute-start | bytes 1544 | tf_op jit(solution)/shard_map/ppermute | solution.py:304
  105.1 0.6 copy-start.5
  105.1 0.6 copy-start.10
